TPU v7x, 32 devices: a whole 2x2x4 slice. The times are simulated.
32 devices in a mesh: section: 4 (over z), latent: 8 (over y, x, core).
Axes of the slice: x: 2, y: 2, z: 4, core: 2. Of those that a mesh axis runs over, the one named last changes fastest.
Arguments:
- residual: bfloat16 [4, 320, 4608], P(None, None, 'latent'), may hold values from -6 to 6
- encoder: bfloat16 [4, 4608, 1024], P('section', None, 'latent'), may hold values from -0.09375 to 0.09375
- enc_bias: float32 [4, 1024], P('section', 'latent'), may hold values from -4 to 4
- gate_code: int32 [4, 1024], P('section', 'latent'), may hold values from 0 to 2
- decoder: bfloat16 [4, 3, 1024, 4608], P('section', None, 'latent'), may hold values from -0.15625 to 0.15625
Outputs:
- reconstruction: bfloat16 [4, 320, 4608], P('section', None, 'latent')
- latent_acts: bfloat16 [4, 320, 1024], P('section', None, 'latent')
Inputs may be any that keep to these rules, and one draw needn't show every extreme that they name: `gate_code`: 0: the latent is always active; 1: its threshold is zero; 2: it is never active.
All inputs are finite; a program needn't handle non-finite values.
Results may differ from a plain program's by a relative error of at most 0.019.
Values may be sent and summed in bfloat16 or wider, within the bound.
No kernel may reach another device: no remote copies, remote signals or barrier semaphores. Data moves between devices by JAX's collectives and lax.ppermute only.
A program may use at most 64 MiB of HBM per device.

v0:
```python
import functools
import math

import jax
import jax.numpy as jnp
from jax import lax
from jax.experimental import pallas as pl
from jax.experimental.pallas import tpu as pltpu
from jax.sharding import PartitionSpec as P

LAYERS = 4
VMEM_LIMIT = 16 * 1024 * 1024


def swapped(shard, axis, stride):
    return lax.ppermute(shard, axis, [(i, i ^ 1 << stride) for i in range(lax.axis_size(axis))])


def after(value, *others):
    return lax.optimization_barrier((value, *others))[0]


def layer_offsets(reach):
    return sorted({layer ^ (layer - hop) for hop in range(1, reach) for layer in range(hop, LAYERS)})


def other_layers(value, reach, group_size):
    received = []
    for offset in layer_offsets(reach):
        wanted = {layer for layer in range(LAYERS) if 0 < layer - (layer ^ offset) < reach}
        pairs = [(index, index ^ offset * group_size) for index in range(lax.axis_size("section"))]
        pairs = [pair for pair in pairs if wanted & {end // group_size for end in pair}]
        received.append(lax.ppermute(value, "section", pairs))
    return received


def by_hop(acts, reach):
    layer = lax.axis_index("section") // (lax.axis_size("section") // LAYERS)
    own, *received = acts
    yield own[...]
    for hop in range(1, reach):
        source = jnp.zeros(own.shape, own.dtype)
        for offset, arrived in zip(layer_offsets(reach), received):
            for target in range(hop, LAYERS):
                if target ^ offset == target - hop:
                    source = jnp.where(layer == target, arrived[...], source)
        yield source


def group_reduce(partial_rows, group_size):
    current = partial_rows
    section_index = lax.axis_index("section")
    level_count = group_size.bit_length() - 1
    for level in reversed(range(level_count)):
        half = current.shape[0] // 2
        lower = current[:half]
        upper = current[half:]
        high_side = section_index // 2**level % 2 == 1
        kept = jnp.where(high_side, upper, lower)
        sent = jnp.where(high_side, lower, upper)
        received = swapped(sent.astype(jnp.bfloat16), "section", level).astype(sent.dtype)
        current = kept + received
    return current


def to_peer(value, offset):
    return lax.ppermute(value, "latent", [(i, i ^ offset) for i in range(lax.axis_size("latent"))])


def call(kernel, out_shape, cost=None):
    return pl.pallas_call(
        kernel,
        out_shape=out_shape,
        cost_estimate=cost,
        compiler_params=pltpu.CompilerParams(vmem_limit_bytes=VMEM_LIMIT),
    )


def encode_near_kernel(offsets, far_offsets, *refs):
    *x_refs, own_ref, sib_ref, gates_ref, gates_sib_ref, out_ref, thr_ref, far_ref = refs
    depth = x_refs[0].shape[1]
    place = lax.axis_index("latent")

    def weights(offset):
        rows = pl.ds(pl.multiple_of((place ^ offset) * depth, 16), depth)
        return jnp.concatenate([own_ref[rows, :], sib_ref[rows, :]], axis=1)

    bias, thr = (jnp.concatenate([gates_ref[i:i + 1, :], gates_sib_ref[i:i + 1, :]], axis=1) for i in (0, 1))
    total = jnp.broadcast_to(bias, out_ref.shape)
    for offset, x_ref in zip(offsets, x_refs):
        total += jnp.dot(x_ref[...], weights(offset), preferred_element_type=jnp.float32)
    out_ref[...] = total
    thr_ref[...] = thr
    for index, offset in enumerate(far_offsets):
        far_ref[index] = weights(offset)


def encode_near(pieces, far_offsets, own, sib, gates, gates_sib):
    rows, depth = next(iter(pieces.values())).shape
    lat = 2 * own.shape[1]
    shapes = (
        jax.ShapeDtypeStruct((rows, lat), jnp.float32),
        jax.ShapeDtypeStruct((1, lat), jnp.float32),
        jax.ShapeDtypeStruct((len(far_offsets), depth, lat), own.dtype),
    )
    cost = pl.CostEstimate(2 * len(pieces) * rows * depth * lat, 4 * own.size, 0)
    kernel = functools.partial(encode_near_kernel, tuple(pieces), far_offsets)
    return call(kernel, shapes, cost=cost)(*pieces.values(), own, sib, gates, gates_sib)


def encode_kernel(near_ref, thr_ref, weights_ref, *refs):
    *x_refs, acts_ref = refs
    preact = near_ref[...]
    for index, x_ref in enumerate(x_refs):
        preact += jnp.dot(x_ref[...], weights_ref[index], preferred_element_type=jnp.float32)
    acts_ref[...] = jnp.where(preact > thr_ref[...], preact, 0.0).astype(jnp.bfloat16)


def encode(near, thr, weights, pieces):
    return call(encode_kernel, jax.ShapeDtypeStruct(near.shape, jnp.bfloat16))(near, thr, weights, *pieces)


def decoded(acts, own_ref, sib_ref, columns):
    total = None
    for hop, values in enumerate(by_hop(acts, own_ref.shape[0])):
        weights = jnp.concatenate([own_ref[hop, :, columns], sib_ref[hop, :, columns]], axis=0)
        part = jnp.dot(values, weights, preferred_element_type=jnp.float32)
        total = part if total is None else total + part
    return total


def decode_chip_kernel(chip_offset, *refs):
    *acts, own_ref, sib_ref, same_ref, cross_ref = refs
    width = same_ref.shape[1]
    place = lax.axis_index("latent")
    columns = pl.ds(pl.multiple_of(((place // 2) ^ chip_offset) * (2 * width), 128), 2 * width)
    total = decoded(acts, own_ref, sib_ref, columns).astype(jnp.bfloat16)
    low, high = total[:, :width], total[:, width:]
    first_core = place % 2 == 0
    same_ref[...] = jnp.where(first_core, low, high)
    cross_ref[...] = jnp.where(first_core, high, low)


def decode_chip(chip_offset, acts, own, sib, width):
    shape = jax.ShapeDtypeStruct((acts[0].shape[0], width), jnp.bfloat16)
    return call(functools.partial(decode_chip_kernel, chip_offset), (shape, shape))(*acts, own, sib)


def decode_all_kernel(*refs):
    *acts, own_ref, sib_ref, out_ref = refs
    count, _, width = out_ref.shape
    block = math.lcm(width, 128)
    per_block = block // width
    for step in range(count // per_block):
        total = decoded(acts, own_ref, sib_ref, slice(step * block, (step + 1) * block))
        for piece in range(per_block):
            out_ref[step * per_block + piece] = total[:, piece * width:(piece + 1) * width].astype(jnp.bfloat16)


def sum_two_kernel(a_ref, b_ref, out_ref):
    out_ref[...] = (a_ref[...].astype(jnp.float32) + b_ref[...].astype(jnp.float32)).astype(jnp.bfloat16)


def sum_two(a, b):
    return call(sum_two_kernel, jax.ShapeDtypeStruct(a.shape, jnp.bfloat16))(a, b)


def finish_kernel(*refs):
    *parts, out_ref = refs
    half = len(parts) // 2
    rows = parts[0].shape[0]
    core = lax.axis_index("latent") % 2
    for place, group in ((core, parts[:half]), (1 - core, parts[half:])):
        total = group[0][...].astype(jnp.float32)
        for part in group[1:]:
            total += part[...].astype(jnp.float32)
        out_ref[pl.ds(pl.multiple_of(place * rows, 16), rows), :] = total.astype(out_ref.dtype)


def finish(mine, other, dtype):
    rows, width = mine[0].shape
    return call(finish_kernel, jax.ShapeDtypeStruct((2 * rows, width), dtype))(*mine, *other)


def gather_and_encode(mine, other, gates, encoder, decoder):
    count = lax.axis_size("latent")
    if count != 8:
        core = lax.axis_index("latent") % 2
        pair = jnp.where(core == 0, jnp.stack([mine, other]), jnp.stack([other, mine]))
        outgoing = jnp.broadcast_to(pair, (count // 2, *pair.shape)).reshape(count, *mine.shape)
        everyone = lax.all_to_all(outgoing, "latent", 0, 0, tiled=True)
        place = lax.axis_index("latent")
        pieces = {i: lax.dynamic_index_in_dim(everyone, place ^ i, 0, keepdims=False) for i in range(count)}
        near, far = {i: pieces[i] for i in range(count // 2)}, {i: pieces[i] for i in range(count // 2, count)}
        enc_sib, gates_sib, dec_sib = (to_peer(value, 1) for value in (encoder, gates, decoder))
        near_sum, *rest = encode_near(near, tuple(far), encoder, enc_sib, gates, gates_sib)
    else:
        near = {0: mine, 2: to_peer(mine, 2), 3: to_peer(other, 3), 4: to_peer(mine, 4), 5: to_peer(other, 5)}
        enc_sib = to_peer(encoder, 1)
        far = {6: to_peer(near[2], 4), 7: to_peer(near[5], 2)}
        near[1] = to_peer(after(other, enc_sib), 1)
        gates_sib = to_peer(after(gates, enc_sib), 1)
        near_sum, *rest = encode_near(near, tuple(far), encoder, enc_sib, gates, gates_sib)
        dec_sib = to_peer(after(decoder, far[6], far[7], near_sum), 1)
    return encode(near_sum, *rest, far.values()), dec_sib


def decode_and_scatter(acts, own, sib, width, dtype):
    count = lax.axis_size("latent")
    rows = acts[0].shape[0]
    if count != 8:
        shares = call(decode_all_kernel, jax.ShapeDtypeStruct((count, rows, width), jnp.bfloat16))(*acts, own, sib)
        received = lax.all_to_all(shares, "latent", 0, 0, tiled=True)
        return jnp.sum(received.reshape(count // 2, 2 * rows, width).astype(jnp.float32), axis=0).astype(dtype)
    diag_same, diag_cross = decode_chip(3, acts, own, sib, width)
    for_y, for_x = to_peer(diag_same, 2), to_peer(diag_cross, 4)
    x_same, x_cross = decode_chip(1, acts, own, sib, width)
    y_same, y_cross = decode_chip(2, acts, own, sib, width)
    from_x_same, from_y_cross = to_peer(x_same, 2), to_peer(y_cross, 5)
    own_same, own_cross = decode_chip(0, acts, own, sib, width)
    y_sum, x_sum = sum_two(y_same, for_y), sum_two(x_cross, for_x)
    from_y_same, from_x_cross = to_peer(y_sum, 4), to_peer(x_sum, 3)
    from_sib = to_peer(own_cross, 1)
    return finish((own_same, from_x_same, from_y_same), (from_sib, from_x_cross, from_y_cross), dtype)


def shards(residual, encoder, enc_bias, gate_code, decoder):
    group_size = lax.axis_size("section") // LAYERS
    core = lax.axis_index("latent") % 2
    _, tok, width = residual.shape
    lat = encoder.shape[2]
    reach = decoder.shape[1]

    halves = residual.reshape(residual.shape[0] * 2, tok // 2, width)
    place = 2 * (lax.axis_index("section") // group_size)
    mine, other = (lax.dynamic_index_in_dim(halves, place + half, 0, keepdims=False) for half in (core, 1 - core))
    threshold = 10000.0 * (gate_code[0].astype(jnp.float32) - 1.0)
    gates_own = jnp.stack([enc_bias[0], threshold])
    acts, dec_sib = gather_and_encode(mine, other, gates_own, encoder[0], decoder[0])
    kept, passed = acts[:, :lat], to_peer(acts[:, lat:], 1)
    latent_acts = jnp.where(core == 0, jnp.stack([kept, passed]), jnp.stack([passed, kept])).reshape(tok, lat)

    received = other_layers(acts, reach, group_size)
    received[1] = after(received[1], passed)
    out_type = jnp.bfloat16 if group_size == 1 else jnp.float32
    summed = decode_and_scatter([acts, *received], decoder[0], dec_sib, width, out_type)
    rebuilt = group_reduce(summed, group_size).astype(jnp.bfloat16)
    return (rebuilt[None], latent_acts[None])


def solution(mesh):
    return jax.shard_map(
        shards,
        mesh=mesh,
        in_specs=(
            P(None, None, "latent"),
            P("section", None, "latent"),
            P("section", "latent"),
            P("section", "latent"),
            P("section", None, "latent", None),
        ),
        out_specs=(P("section", None, "latent"), P("section", None, "latent")),
        check_vma=False,
    )
```

profile of v0, /device:TPU:0, one launch (start us, length us, event | category | flops | bytes accessed | tf_op | source)
XLA Modules:
  0.0 47.9 jit_solution(7417190182275019352)
XLA Ops:
  0.6 0.5 %collective-permute-start.4 = (bf16[4608,128]{1,0:T(8,128)(2,1)}, bf16[4608,128]{1,0:T(8,128)(2,1)S(1)}, u32[]{:S(2)}, u32[]{:S(2)}) collective-permute-start(bf16[4608,128]{1,0:T(8,128)(2,1)} %bitcast.17), channel_id=1, source_target_pairs={{0,1},{1,0},{2,3},{3,2},{4,5},{5,4},{6,7},{7,6},{8,9},{9,8},{10,11... | collective-permute-start | bytes 3538952 | tf_op jit(solution)/shard_map/ppermute | solution.py:67
  1.1 1.1 %dynamic-slice_bitcast_fusion = (bf16[160,576]{1,0:T(8,128)(2,1)S(1)}, bf16[160,576]{1,0:T(8,128)(2,1)S(1)}) fusion(bf16[8,160,576]{2,1,0:T(8,128)(2,1)} %bitcast.20, s32[]{:T(128)S(6)} %select_n.36, s32[]{:T(128)S(6)} %select_n.35), kind=kLoop, calls=%fused_computation | loop fusion | bytes 737288 | tf_op jit(solution)/shard_map/jit(dynamic_index_in_dim)/squeeze | solution.py:236
  2.2 2.6 %collective-permute-start = (bf16[160,576]{1,0:T(8,128)(2,1)S(1)}, bf16[160,576]{1,0:T(8,128)(2,1)S(1)}, u32[]{:S(2)}, u32[]{:S(2)}) collective-permute-start(bf16[160,576]{1,0:T(8,128)(2,1)S(1)} %get-tuple-element.33.refs_0_), channel_id=1, source_target_pairs={{0,2},{1,3},{2,0},{3,1},{4,6},{5,7},{6,4},{7,5},{8,10},{9,11},{10,... | collective-permute-start | bytes 552968 | tf_op jit(solution)/shard_map/ppermute | solution.py:67
  4.8 1.3 %collective-permute-start.3 = (bf16[160,576]{1,0:T(8,128)(2,1)S(1)}, bf16[160,576]{1,0:T(8,128)(2,1)S(1)}, u32[]{:S(2)}, u32[]{:S(2)}) collective-permute-start(bf16[160,576]{1,0:T(8,128)(2,1)S(1)} %get-tuple-element.17), channel_id=1, source_target_pairs={{0,5},{1,4},{2,7},{3,6},{4,1},{5,0},{6,3},{7,2},{8,13},{9,12},{10,... | collective-permute-start | bytes 552968 | tf_op jit(solution)/shard_map/ppermute | solution.py:67
  6.7 4.1 %collective-permute-done.refs_1_ = bf16[160,576]{1,0:T(8,128)(2,1)S(1)} collective-permute-done((bf16[160,576]{1,0:T(8,128)(2,1)S(1)}, bf16[160,576]{1,0:T(8,128)(2,1)S(1)}, u32[]{:S(2)}, u32[]{:S(2)}) %collective-permute-start) | collective-permute-done | bytes 184352 | tf_op jit(solution)/shard_map/ppermute | solution.py:67
  10.7 2.0 %collective-permute-start.7 = (bf16[160,576]{1,0:T(8,128)(2,1)S(1)}, bf16[160,576]{1,0:T(8,128)(2,1)S(1)}, u32[]{:S(2)}, u32[]{:S(2)}) collective-permute-start(bf16[160,576]{1,0:T(8,128)(2,1)S(1)} %collective-permute-done.refs_1_), channel_id=1, source_target_pairs={{0,4},{1,5},{2,6},{3,7},{4,0},{5,1},{6,2},{7,3},{8,12},{9,13},{10,... | collective-permute-start | bytes 552968 | tf_op jit(solution)/shard_map/ppermute | solution.py:67
  12.7 1.5 %collective-permute-start.8 = (bf16[160,576]{1,0:T(8,128)(2,1)S(1)}, bf16[160,576]{1,0:T(8,128)(2,1)S(1)}, u32[]{:S(2)}, u32[]{:S(2)}) collective-permute-start(bf16[160,576]{1,0:T(8,128)(2,1)S(1)} %collective-permute-done.3.refs_4_), channel_id=1, source_target_pairs={{0,2},{1,3},{2,0},{3,1},{4,6},{5,7},{6,4},{7,5},{8,10},{9,11},{10,... | collective-permute-start | bytes 552968 | tf_op jit(solution)/shard_map/ppermute | solution.py:67
  14.2 0.7 %add_multiply_fusion = f32[1,128]{1,0:T(1,128)S(1)} fusion(s32[1,128]{1,0:T(1,128)} %param.8), kind=kLoop, calls=%fused_computation.5 | loop fusion | flops 384 | bytes 1024 | tf_op jit(solution)/shard_map/mul | solution.py:237
  14.9 0.7 %pad_maximum_fusion.refs_8_ = f32[2,128]{1,0:T(2,128)S(1)} fusion(f32[1,128]{1,0:T(1,128)S(1)} %add_multiply_fusion, f32[1,128]{1,0:T(1,128)} %param.7), kind=kLoop, calls=%fused_computation.4 | loop fusion | flops 256 | bytes 2048 | tf_op jit(solution)/shard_map/stack | solution.py:238
  15.5 0.6 %collective-permute-start.6 = (f32[2,128]{1,0:T(2,128)S(1)}, f32[2,128]{1,0:T(2,128)S(1)}, u32[]{:S(2)}, u32[]{:S(2)}) collective-permute-start(f32[2,128]{1,0:T(2,128)S(1)} %pad_maximum_fusion.refs_8_), channel_id=1, source_target_pairs={{0,1},{1,0},{2,3},{3,2},{4,5},{5,4},{6,7},{7,6},{8,9},{9,8},{10,11... | collective-permute-start | bytes 3080 | tf_op jit(solution)/shard_map/ppermute | solution.py:67
  16.1 0.7 %collective-permute-done.2.refs_3_ = bf16[160,576]{1,0:T(8,128)(2,1)S(1)} collective-permute-done((bf16[160,576]{1,0:T(8,128)(2,1)S(1)}, bf16[160,576]{1,0:T(8,128)(2,1)S(1)}, u32[]{:S(2)}, u32[]{:S(2)}) %collective-permute-start.2) | collective-permute-done | bytes 184352 | tf_op jit(solution)/shard_map/ppermute | solution.py:67
  16.9 1.3 %copy-done.1 = bf16[1,4608,128]{2,1,0:T(8,128)(2,1)S(1)} copy-done((bf16[1,4608,128]{2,1,0:T(8,128)(2,1)S(1)}, bf16[1,4608,128]{2,1,0:T(8,128)(2,1)}, u32[]{:S(2)}) %copy-start.1) | copy-done | bytes 1179672
  18.2 0.6 %shard_map.68 = (f32[160,256]{1,0:T(8,128)S(1)}, f32[1,256]{1,0:T(1,128)S(1)}, bf16[2,576,256]{2,1,0:T(8,128)(2,1)S(1)}) custom-call(bf16[160,576]{1,0:T(8,128)(2,1)S(1)} %get-tuple-element.33.refs_0_, bf16[160,576]{1,0:T(8,128)(2,1)S(1)} %collective-permute-done.refs_1_, bf16[160,576]{1,0:T(8,128)(2,1)S(1)} %collective-permute-done.1.refs_2_, ...), custom_call_target="tpu_custom_call" | custom-call | flops 283115520 | tf_op jit(solution)/shard_map/pallas_call | solution.py:108
  18.8 2.1 %collective-permute-done.7.refs_0_ = bf16[160,576]{1,0:T(8,128)(2,1)S(1)} collective-permute-done((bf16[160,576]{1,0:T(8,128)(2,1)S(1)}, bf16[160,576]{1,0:T(8,128)(2,1)S(1)}, u32[]{:S(2)}, u32[]{:S(2)}) %collective-permute-start.7) | collective-permute-done | bytes 184352 | tf_op jit(solution)/shard_map/ppermute | solution.py:67
  21.3 2.7 %collective-permute-start.10 = (bf16[160,256]{1,0:T(8,128)(2,1)S(1)}, bf16[160,256]{1,0:T(8,128)(2,1)S(1)}, u32[]{:S(2)}, u32[]{:S(2)}) collective-permute-start(bf16[160,256]{1,0:T(8,128)(2,1)S(1)} %shard_map.69.refs_0_), channel_id=1, source_target_pairs={{0,16},{8,24},{16,0},{24,8},{1,17},{9,25},{17,1},{25,9},{2,18},{10... | collective-permute-start | bytes 245768 | tf_op jit(solution)/shard_map/ppermute | solution.py:33
  23.9 0.7 %collective-permute-start.12 = (bf16[160,256]{1,0:T(8,128)(2,1)S(1)}, bf16[160,256]{1,0:T(8,128)(2,1)S(1)}, u32[]{:S(2)}, u32[]{:S(2)}) collective-permute-start(bf16[160,256]{1,0:T(8,128)(2,1)S(1)} %shard_map.69.refs_0_), channel_id=1, source_target_pairs={{8,16},{16,8},{9,17},{17,9},{10,18},{18,10},{11,19},{19,11},{12,20... | collective-permute-start | bytes 245768 | tf_op jit(solution)/shard_map/ppermute | solution.py:33
  24.6 2.9 %collective-permute-start.9 = (bf16[160,256]{1,0:T(8,128)(2,1)S(1)}, bf16[160,256]{1,0:T(8,128)(2,1)S(1)}, u32[]{:S(2)}, u32[]{:S(2)}) collective-permute-start(bf16[160,256]{1,0:T(8,128)(2,1)S(1)} %shard_map.69.refs_0_), channel_id=1, source_target_pairs={{0,8},{8,0},{16,24},{24,16},{1,9},{9,1},{17,25},{25,17},{2,10},{10... | collective-permute-start | bytes 245768 | tf_op jit(solution)/shard_map/ppermute | solution.py:33
  27.5 1.2 %collective-permute-done.11 = bf16[160,128]{1,0:T(8,128)(2,1)S(1)} collective-permute-done((bf16[160,128]{1,0:T(8,128)(2,1)S(1)}, bf16[160,128]{1,0:T(8,128)(2,1)S(1)}, u32[]{:S(2)}, u32[]{:S(2)}) %collective-permute-start.11) | collective-permute-done | bytes 40992 | tf_op jit(solution)/shard_map/ppermute | solution.py:67
  28.9 1.7 %collective-permute-done.9.refs_1_ = bf16[160,256]{1,0:T(8,128)(2,1)S(1)} collective-permute-done((bf16[160,256]{1,0:T(8,128)(2,1)S(1)}, bf16[160,256]{1,0:T(8,128)(2,1)S(1)}, u32[]{:S(2)}, u32[]{:S(2)}) %collective-permute-start.9) | collective-permute-done | bytes 81952 | tf_op jit(solution)/shard_map/ppermute | solution.py:33
  30.6 0.6 %shard_map.73 = (bf16[160,576]{1,0:T(8,128)(2,1)S(1)}, bf16[160,576]{1,0:T(8,128)(2,1)S(1)}) custom-call(bf16[160,256]{1,0:T(8,128)(2,1)S(1)} %shard_map.69.refs_0_, bf16[160,256]{1,0:T(8,128)(2,1)S(1)} %collective-permute-done.9.refs_1_, bf16[160,256]{1,0:T(8,128)(2,1)S(1)} %collective-permute-done.10.refs_2_, ...), custom_call_target="tpu_custom_call" | custom-call | tf_op jit(solution)/shard_map/pallas_call | solution.py:146
  31.2 1.6 %collective-permute-start.18 = (bf16[160,576]{1,0:T(8,128)(2,1)S(1)}, bf16[160,576]{1,0:T(8,128)(2,1)S(1)}, u32[]{:S(2)}, u32[]{:S(2)}) collective-permute-start(bf16[160,576]{1,0:T(8,128)(2,1)S(1)} %get-tuple-element.30), channel_id=1, source_target_pairs={{0,4},{1,5},{2,6},{3,7},{4,0},{5,1},{6,2},{7,3},{8,12},{9,13},{10,... | collective-permute-start | bytes 552968 | tf_op jit(solution)/shard_map/ppermute | solution.py:67
  32.8 0.5 %collective-permute-start.15 = (bf16[160,576]{1,0:T(8,128)(2,1)S(1)}, bf16[160,576]{1,0:T(8,128)(2,1)S(1)}, u32[]{:S(2)}, u32[]{:S(2)}) collective-permute-start(bf16[160,576]{1,0:T(8,128)(2,1)S(1)} %get-tuple-element.27), channel_id=1, source_target_pairs={{0,2},{1,3},{2,0},{3,1},{4,6},{5,7},{6,4},{7,5},{8,10},{9,11},{10,... | collective-permute-start | bytes 552968 | tf_op jit(solution)/shard_map/ppermute | solution.py:67
  33.3 0.6 %shard_map.72 = (bf16[160,576]{1,0:T(8,128)(2,1)S(1)}, bf16[160,576]{1,0:T(8,128)(2,1)S(1)}) custom-call(bf16[160,256]{1,0:T(8,128)(2,1)S(1)} %shard_map.69.refs_0_, bf16[160,256]{1,0:T(8,128)(2,1)S(1)} %collective-permute-done.9.refs_1_, bf16[160,256]{1,0:T(8,128)(2,1)S(1)} %collective-permute-done.10.refs_2_, ...), custom_call_target="tpu_custom_call" | custom-call | tf_op jit(solution)/shard_map/pallas_call | solution.py:146
  34.1 0.6 %shard_map.71 = (bf16[160,576]{1,0:T(8,128)(2,1)S(1)}, bf16[160,576]{1,0:T(8,128)(2,1)S(1)}) custom-call(bf16[160,256]{1,0:T(8,128)(2,1)S(1)} %shard_map.69.refs_0_, bf16[160,256]{1,0:T(8,128)(2,1)S(1)} %collective-permute-done.9.refs_1_, bf16[160,256]{1,0:T(8,128)(2,1)S(1)} %collective-permute-done.10.refs_2_, ...), custom_call_target="tpu_custom_call" | custom-call | tf_op jit(solution)/shard_map/pallas_call | solution.py:146
  34.7 1.6 %collective-permute-start.14 = (bf16[160,576]{1,0:T(8,128)(2,1)S(1)}, bf16[160,576]{1,0:T(8,128)(2,1)S(1)}, u32[]{:S(2)}, u32[]{:S(2)}) collective-permute-start(bf16[160,576]{1,0:T(8,128)(2,1)S(1)} %get-tuple-element.25), channel_id=1, source_target_pairs={{0,2},{1,3},{2,0},{3,1},{4,6},{5,7},{6,4},{7,5},{8,10},{9,11},{10,... | collective-permute-start | bytes 552968 | tf_op jit(solution)/shard_map/ppermute | solution.py:67
  36.3 0.6 %shard_map.70 = (bf16[160,576]{1,0:T(8,128)(2,1)S(1)}, bf16[160,576]{1,0:T(8,128)(2,1)S(1)}) custom-call(bf16[160,256]{1,0:T(8,128)(2,1)S(1)} %shard_map.69.refs_0_, bf16[160,256]{1,0:T(8,128)(2,1)S(1)} %collective-permute-done.9.refs_1_, bf16[160,256]{1,0:T(8,128)(2,1)S(1)} %collective-permute-done.10.refs_2_, ...), custom_call_target="tpu_custom_call" | custom-call | tf_op jit(solution)/shard_map/pallas_call | solution.py:146
  37.3 2.0 %collective-permute-done.18.b_ref = bf16[160,576]{1,0:T(8,128)(2,1)S(1)} collective-permute-done((bf16[160,576]{1,0:T(8,128)(2,1)S(1)}, bf16[160,576]{1,0:T(8,128)(2,1)S(1)}, u32[]{:S(2)}, u32[]{:S(2)}) %collective-permute-start.18) | collective-permute-done | bytes 184352 | tf_op jit(solution)/shard_map/ppermute | solution.py:67
  39.4 1.4 %collective-permute-done.15.b_ref = bf16[160,576]{1,0:T(8,128)(2,1)S(1)} collective-permute-done((bf16[160,576]{1,0:T(8,128)(2,1)S(1)}, bf16[160,576]{1,0:T(8,128)(2,1)S(1)}, u32[]{:S(2)}, u32[]{:S(2)}) %collective-permute-start.15) | collective-permute-done | bytes 184352 | tf_op jit(solution)/shard_map/ppermute | solution.py:67
  41.0 0.6 %maximum_select_fusion = bf16[2,160,128]{2,1,0:T(8,128)(2,1)} fusion(bf16[1,160,128]{2,1,0:T(8,128)(2,1)S(1)} %bitcast.22, bf16[1,160,128]{2,1,0:T(8,128)(2,1)S(1)} %get-tuple-element.34, pred[]{:T(512)S(6)} %eq.5), kind=kLoop, calls=%fused_computation.2 | loop fusion | flops 122880 | bytes 163841 | tf_op jit(solution)/shard_map/jit(_where)/select_n | solution.py:241
  41.7 3.5 %collective-permute-done.14.refs_1_ = bf16[160,576]{1,0:T(8,128)(2,1)S(1)} collective-permute-done((bf16[160,576]{1,0:T(8,128)(2,1)S(1)}, bf16[160,576]{1,0:T(8,128)(2,1)S(1)}, u32[]{:S(2)}, u32[]{:S(2)}) %collective-permute-start.14) | collective-permute-done | bytes 184352 | tf_op jit(solution)/shard_map/ppermute | solution.py:67
  45.2 1.6 %collective-permute-done.19.refs_4_ = bf16[160,576]{1,0:T(8,128)(2,1)S(1)} collective-permute-done((bf16[160,576]{1,0:T(8,128)(2,1)S(1)}, bf16[160,576]{1,0:T(8,128)(2,1)S(1)}, u32[]{:S(2)}, u32[]{:S(2)}) %collective-permute-start.19) | collective-permute-done | bytes 184352 | tf_op jit(solution)/shard_map/ppermute | solution.py:67
  47.0 0.9 %shard_map.76 = bf16[320,576]{1,0:T(8,128)(2,1)} custom-call(bf16[160,576]{1,0:T(8,128)(2,1)S(1)} %get-tuple-element.24.refs_0_, bf16[160,576]{1,0:T(8,128)(2,1)S(1)} %collective-permute-done.14.refs_1_, bf16[160,576]{1,0:T(8,128)(2,1)S(1)} %collective-permute-done.16.refs_2_, bf16[160,576]{1,0:T(8,128)(2,1)S(1)} %collective-permute-done.17.refs_3_, ...), custom_call_target="tpu_custom_call" | custom-call | tf_op jit(solution)/shard_map/pallas_call | solution.py:182
  (28 shorter events, 2.0 us)
Async XLA Ops:
  0.6 13.6 %collective-permute-start.4 = (bf16[4608,128]{1,0:T(8,128)(2,1)}, bf16[4608,128]{1,0:T(8,128)(2,1)S(1)}, u32[]{:S(2)}, u32[]{:S(2)}) collective-permute-start(bf16[4608,128]{1,0:T(8,128)(2,1)} %bitcast.17), channel_id=1, source_target_pairs={{0,1},{1,0},{2,3},{3,2},{4,5},{5,4},{6,7},{7,6},{8,9},{9,8},{10,11... | collective-permute-start | bytes 3538952 | tf_op jit(solution)/shard_map/ppermute | solution.py:67
  2.2 8.5 %collective-permute-start = (bf16[160,576]{1,0:T(8,128)(2,1)S(1)}, bf16[160,576]{1,0:T(8,128)(2,1)S(1)}, u32[]{:S(2)}, u32[]{:S(2)}) collective-permute-start(bf16[160,576]{1,0:T(8,128)(2,1)S(1)} %get-tuple-element.33.refs_0_), channel_id=1, source_target_pairs={{0,2},{1,3},{2,0},{3,1},{4,6},{5,7},{6,4},{7,5},{8,10},{9,11},{10,... | collective-permute-start | bytes 552968 | tf_op jit(solution)/shard_map/ppermute | solution.py:67
  4.8 7.9 %collective-permute-start.3 = (bf16[160,576]{1,0:T(8,128)(2,1)S(1)}, bf16[160,576]{1,0:T(8,128)(2,1)S(1)}, u32[]{:S(2)}, u32[]{:S(2)}) collective-permute-start(bf16[160,576]{1,0:T(8,128)(2,1)S(1)} %get-tuple-element.17), channel_id=1, source_target_pairs={{0,5},{1,4},{2,7},{3,6},{4,1},{5,0},{6,3},{7,2},{8,13},{9,12},{10,... | collective-permute-start | bytes 552968 | tf_op jit(solution)/shard_map/ppermute | solution.py:67
  6.1 9.4 %collective-permute-start.1 = (bf16[160,576]{1,0:T(8,128)(2,1)S(1)}, bf16[160,576]{1,0:T(8,128)(2,1)S(1)}, u32[]{:S(2)}, u32[]{:S(2)}) collective-permute-start(bf16[160,576]{1,0:T(8,128)(2,1)S(1)} %get-tuple-element.17), channel_id=1, source_target_pairs={{0,3},{1,2},{2,1},{3,0},{4,7},{5,6},{6,5},{7,4},{8,11},{9,10},{10,... | collective-permute-start | bytes 552968 | tf_op jit(solution)/shard_map/ppermute | solution.py:67
  6.6 10.3 %collective-permute-start.2 = (bf16[160,576]{1,0:T(8,128)(2,1)S(1)}, bf16[160,576]{1,0:T(8,128)(2,1)S(1)}, u32[]{:S(2)}, u32[]{:S(2)}) collective-permute-start(bf16[160,576]{1,0:T(8,128)(2,1)S(1)} %get-tuple-element.33.refs_0_), channel_id=1, source_target_pairs={{0,4},{1,5},{2,6},{3,7},{4,0},{5,1},{6,2},{7,3},{8,12},{9,13},{10,... | collective-permute-start | bytes 552968 | tf_op jit(solution)/shard_map/ppermute | solution.py:67
  10.7 10.2 %collective-permute-start.7 = (bf16[160,576]{1,0:T(8,128)(2,1)S(1)}, bf16[160,576]{1,0:T(8,128)(2,1)S(1)}, u32[]{:S(2)}, u32[]{:S(2)}) collective-permute-start(bf16[160,576]{1,0:T(8,128)(2,1)S(1)} %collective-permute-done.refs_1_), channel_id=1, source_target_pairs={{0,4},{1,5},{2,6},{3,7},{4,0},{5,1},{6,2},{7,3},{8,12},{9,13},{10,... | collective-permute-start | bytes 552968 | tf_op jit(solution)/shard_map/ppermute | solution.py:67
  12.7 8.2 %collective-permute-start.8 = (bf16[160,576]{1,0:T(8,128)(2,1)S(1)}, bf16[160,576]{1,0:T(8,128)(2,1)S(1)}, u32[]{:S(2)}, u32[]{:S(2)}) collective-permute-start(bf16[160,576]{1,0:T(8,128)(2,1)S(1)} %collective-permute-done.3.refs_4_), channel_id=1, source_target_pairs={{0,2},{1,3},{2,0},{3,1},{4,6},{5,7},{6,4},{7,5},{8,10},{9,11},{10,... | collective-permute-start | bytes 552968 | tf_op jit(solution)/shard_map/ppermute | solution.py:67
  14.2 2.7 %collective-permute-start.5 = (bf16[160,576]{1,0:T(8,128)(2,1)S(1)}, bf16[160,576]{1,0:T(8,128)(2,1)S(1)}, u32[]{:S(2)}, u32[]{:S(2)}) collective-permute-start(bf16[160,576]{1,0:T(8,128)(2,1)S(1)} %get-tuple-element.17), channel_id=1, source_target_pairs={{0,1},{1,0},{2,3},{3,2},{4,5},{5,4},{6,7},{7,6},{8,9},{9,8},{10,11... | collective-permute-start | bytes 552968 | tf_op jit(solution)/shard_map/ppermute | solution.py:67
  15.5 5.4 %copy-start = (bf16[1,3,128,4608]{3,2,1,0:T(8,128)(2,1)S(1)}, bf16[1,3,128,4608]{3,2,1,0:T(8,128)(2,1)}, u32[]{:S(2)}) copy-start(bf16[1,3,128,4608]{3,2,1,0:T(8,128)(2,1)} %param.9) | copy-start | bytes 10616836
  15.5 1.4 %collective-permute-start.6 = (f32[2,128]{1,0:T(2,128)S(1)}, f32[2,128]{1,0:T(2,128)S(1)}, u32[]{:S(2)}, u32[]{:S(2)}) collective-permute-start(f32[2,128]{1,0:T(2,128)S(1)} %pad_maximum_fusion.refs_8_), channel_id=1, source_target_pairs={{0,1},{1,0},{2,3},{3,2},{4,5},{5,4},{6,7},{7,6},{8,9},{9,8},{10,11... | collective-permute-start | bytes 3080 | tf_op jit(solution)/shard_map/ppermute | solution.py:67
  16.9 1.3 %copy-start.1 = (bf16[1,4608,128]{2,1,0:T(8,128)(2,1)S(1)}, bf16[1,4608,128]{2,1,0:T(8,128)(2,1)}, u32[]{:S(2)}) copy-start(bf16[1,4608,128]{2,1,0:T(8,128)(2,1)} %param.6) | copy-start | bytes 3538948
  21.0 9.6 %collective-permute-start.13 = (bf16[3,128,4608]{2,1,0:T(8,128)(2,1)S(1)}, bf16[3,128,4608]{2,1,0:T(8,128)(2,1)S(1)}, u32[]{:S(2)}, u32[]{:S(2)}) collective-permute-start(bf16[3,128,4608]{2,1,0:T(8,128)(2,1)S(1)} %bitcast.12), channel_id=1, source_target_pairs={{0,1},{1,0},{2,3},{3,2},{4,5},{5,4},{6,7},{7,6},{8,9},{9,8},{10,11... | collective-permute-start | bytes 10616840 | tf_op jit(solution)/shard_map/ppermute | solution.py:67
  21.3 7.6 %collective-permute-start.10 = (bf16[160,256]{1,0:T(8,128)(2,1)S(1)}, bf16[160,256]{1,0:T(8,128)(2,1)S(1)}, u32[]{:S(2)}, u32[]{:S(2)}) collective-permute-start(bf16[160,256]{1,0:T(8,128)(2,1)S(1)} %shard_map.69.refs_0_), channel_id=1, source_target_pairs={{0,16},{8,24},{16,0},{24,8},{1,17},{9,25},{17,1},{25,9},{2,18},{10... | collective-permute-start | bytes 245768 | tf_op jit(solution)/shard_map/ppermute | solution.py:33
  23.9 4.9 %collective-permute-start.12 = (bf16[160,256]{1,0:T(8,128)(2,1)S(1)}, bf16[160,256]{1,0:T(8,128)(2,1)S(1)}, u32[]{:S(2)}, u32[]{:S(2)}) collective-permute-start(bf16[160,256]{1,0:T(8,128)(2,1)S(1)} %shard_map.69.refs_0_), channel_id=1, source_target_pairs={{8,16},{16,8},{9,17},{17,9},{10,18},{18,10},{11,19},{19,11},{12,20... | collective-permute-start | bytes 245768 | tf_op jit(solution)/shard_map/ppermute | solution.py:33
  24.6 6.0 %collective-permute-start.9 = (bf16[160,256]{1,0:T(8,128)(2,1)S(1)}, bf16[160,256]{1,0:T(8,128)(2,1)S(1)}, u32[]{:S(2)}, u32[]{:S(2)}) collective-permute-start(bf16[160,256]{1,0:T(8,128)(2,1)S(1)} %shard_map.69.refs_0_), channel_id=1, source_target_pairs={{0,8},{8,0},{16,24},{24,16},{1,9},{9,1},{17,25},{25,17},{2,10},{10... | collective-permute-start | bytes 245768 | tf_op jit(solution)/shard_map/ppermute | solution.py:33
  27.5 1.2 %collective-permute-start.11 = (bf16[160,128]{1,0:T(8,128)(2,1)S(1)}, bf16[160,128]{1,0:T(8,128)(2,1)S(1)}, u32[]{:S(2)}, u32[]{:S(2)}) collective-permute-start(bf16[160,128]{1,0:T(8,128)(2,1)S(1)} %get-tuple-element.35), channel_id=1, source_target_pairs={{0,1},{1,0},{2,3},{3,2},{4,5},{5,4},{6,7},{7,6},{8,9},{9,8},{10,11... | collective-permute-start | bytes 122888 | tf_op jit(solution)/shard_map/ppermute | solution.py:67
  31.2 8.0 %collective-permute-start.18 = (bf16[160,576]{1,0:T(8,128)(2,1)S(1)}, bf16[160,576]{1,0:T(8,128)(2,1)S(1)}, u32[]{:S(2)}, u32[]{:S(2)}) collective-permute-start(bf16[160,576]{1,0:T(8,128)(2,1)S(1)} %get-tuple-element.30), channel_id=1, source_target_pairs={{0,4},{1,5},{2,6},{3,7},{4,0},{5,1},{6,2},{7,3},{8,12},{9,13},{10,... | collective-permute-start | bytes 552968 | tf_op jit(solution)/shard_map/ppermute | solution.py:67
  32.8 8.0 %collective-permute-start.15 = (bf16[160,576]{1,0:T(8,128)(2,1)S(1)}, bf16[160,576]{1,0:T(8,128)(2,1)S(1)}, u32[]{:S(2)}, u32[]{:S(2)}) collective-permute-start(bf16[160,576]{1,0:T(8,128)(2,1)S(1)} %get-tuple-element.27), channel_id=1, source_target_pairs={{0,2},{1,3},{2,0},{3,1},{4,6},{5,7},{6,4},{7,5},{8,10},{9,11},{10,... | collective-permute-start | bytes 552968 | tf_op jit(solution)/shard_map/ppermute | solution.py:67
  34.0 7.7 %collective-permute-start.20 = (bf16[160,576]{1,0:T(8,128)(2,1)S(1)}, bf16[160,576]{1,0:T(8,128)(2,1)S(1)}, u32[]{:S(2)}, u32[]{:S(2)}) collective-permute-start(bf16[160,576]{1,0:T(8,128)(2,1)S(1)} %get-tuple-element.31), channel_id=1, source_target_pairs={{0,5},{1,4},{2,7},{3,6},{4,1},{5,0},{6,3},{7,2},{8,13},{9,12},{10,... | collective-permute-start | bytes 552968 | tf_op jit(solution)/shard_map/ppermute | solution.py:67
  34.7 10.5 %collective-permute-start.14 = (bf16[160,576]{1,0:T(8,128)(2,1)S(1)}, bf16[160,576]{1,0:T(8,128)(2,1)S(1)}, u32[]{:S(2)}, u32[]{:S(2)}) collective-permute-start(bf16[160,576]{1,0:T(8,128)(2,1)S(1)} %get-tuple-element.25), channel_id=1, source_target_pairs={{0,2},{1,3},{2,0},{3,1},{4,6},{5,7},{6,4},{7,5},{8,10},{9,11},{10,... | collective-permute-start | bytes 552968 | tf_op jit(solution)/shard_map/ppermute | solution.py:67
  36.9 8.3 %collective-permute-start.17 = (bf16[160,576]{1,0:T(8,128)(2,1)S(1)}, bf16[160,576]{1,0:T(8,128)(2,1)S(1)}, u32[]{:S(2)}, u32[]{:S(2)}) collective-permute-start(bf16[160,576]{1,0:T(8,128)(2,1)S(1)} %get-tuple-element.28), channel_id=1, source_target_pairs={{0,1},{1,0},{2,3},{3,2},{4,5},{5,4},{6,7},{7,6},{8,9},{9,8},{10,11... | collective-permute-start | bytes 552968 | tf_op jit(solution)/shard_map/ppermute | solution.py:67
  39.3 7.5 %collective-permute-start.19 = (bf16[160,576]{1,0:T(8,128)(2,1)S(1)}, bf16[160,576]{1,0:T(8,128)(2,1)S(1)}, u32[]{:S(2)}, u32[]{:S(2)}) collective-permute-start(bf16[160,576]{1,0:T(8,128)(2,1)S(1)} %shard_map.75), channel_id=1, source_target_pairs={{0,3},{1,2},{2,1},{3,0},{4,7},{5,6},{6,5},{7,4},{8,11},{9,10},{10,... | collective-permute-start | bytes 552968 | tf_op jit(solution)/shard_map/ppermute | solution.py:67
  40.9 6.1 %collective-permute-start.16 = (bf16[160,576]{1,0:T(8,128)(2,1)S(1)}, bf16[160,576]{1,0:T(8,128)(2,1)S(1)}, u32[]{:S(2)}, u32[]{:S(2)}) collective-permute-start(bf16[160,576]{1,0:T(8,128)(2,1)S(1)} %shard_map.74), channel_id=1, source_target_pairs={{0,4},{1,5},{2,6},{3,7},{4,0},{5,1},{6,2},{7,3},{8,12},{9,13},{10,... | collective-permute-start | bytes 552968 | tf_op jit(solution)/shard_map/ppermute | solution.py:67
where the time goes:
time: 48.7 us; the launch traced here: 47.9 us
  starting transfers between devices  19.6 us (40%)
  waiting for transfers between devices  18.9 us (39%)
  Pallas kernels  4.43 us (9%)
  local copies, waits for them, and re-layouts  2.35 us (5%)
  other arithmetic  1.97 us (4%)
  between operations  0.72 us (1%)
    ppermute x18, waiting for transfers between devices, to_peer(): lax.ppermute(value, 'latent', [(i, i ^ offset) for i in range(lax.axis_si...  17 us
    ppermute x18, starting transfers between devices, to_peer(): lax.ppermute(value, 'latent', [(i, i ^ offset) for i in range(lax.axis_si...  13.4 us
    ppermute x3, starting transfers between devices, other_layers(): received.append(lax.ppermute(value, 'section', pairs))  6.2 us
    pallas_call x4, Pallas kernels, decode_chip(): call(functools.partial(decode_chip_kernel, chip_offset), (shape, shape))  2.53 us
    ppermute x3, waiting for transfers between devices, other_layers(): received.append(lax.ppermute(value, 'section', pairs))  1.88 us
    unnamed x4, local copies, waits for them, and re-layouts  1.27 us
    squeeze x1, local copies, waits for them, and re-layouts, shards(): lax.dynamic_index_in_dim(halves, place + half, 0, keepdims=False)  1.06 us
  transfers between devices with their start and end apart: 21, of which 12 were waited for; matrix products, arithmetic and copies ran while one was open for 6% of the time, Pallas kernels for 6%

commit v1 on v0

--- a/solution.py
+++ b/solution.py
@@ -28,8 +28,11 @@
     received = []
     for offset in layer_offsets(reach):
         wanted = {layer for layer in range(LAYERS) if 0 < layer - (layer ^ offset) < reach}
-        pairs = [(index, index ^ offset * group_size) for index in range(lax.axis_size("section"))]
-        pairs = [pair for pair in pairs if wanted & {end // group_size for end in pair}]
+        wanted |= {layer ^ offset for layer in wanted}
+        pairs = [
+            (index, index ^ offset * group_size if index // group_size in wanted else index)
+            for index in range(lax.axis_size("section"))
+        ]
         received.append(lax.ppermute(value, "section", pairs))
     return received
 

time: 48.7 us -> 48.7 us (level)
  no operation moved by 1% of the time
where the time goes in v1:
time: 48.7 us; the launch traced here: 47.9 us
  starting transfers between devices  19.6 us (40%)
  waiting for transfers between devices  18.9 us (39%)
  Pallas kernels  4.43 us (9%)
  local copies, waits for them, and re-layouts  2.35 us (5%)
  other arithmetic  1.97 us (4%)
  between operations  0.72 us (1%)
    ppermute x18, waiting for transfers between devices, to_peer(): lax.ppermute(value, 'latent', [(i, i ^ offset) for i in range(lax.axis_si...  17 us
    ppermute x18, starting transfers between devices, to_peer(): lax.ppermute(value, 'latent', [(i, i ^ offset) for i in range(lax.axis_si...  13.4 us
    ppermute x3, starting transfers between devices, other_layers(): received.append(lax.ppermute(value, 'section', pairs))  6.2 us
    pallas_call x4, Pallas kernels, decode_chip(): call(functools.partial(decode_chip_kernel, chip_offset), (shape, shape))  2.53 us
    ppermute x3, waiting for transfers between devices, other_layers(): received.append(lax.ppermute(value, 'section', pairs))  1.88 us
    unnamed x4, local copies, waits for them, and re-layouts  1.27 us
    squeeze x1, local copies, waits for them, and re-layouts, shards(): lax.dynamic_index_in_dim(halves, place + half, 0, keepdims=False)  1.06 us
  transfers between devices with their start and end apart: 21, of which 12 were waited for; matrix products, arithmetic and copies ran while one was open for 6% of the time, Pallas kernels for 6%

profile of v1, /device:TPU:0, one launch (start us, length us, event | category | flops | bytes accessed | tf_op | source)
XLA Modules:
  0.0 47.9 jit_solution(1004616157248908728)
XLA Ops:
  0.6 0.5 %collective-permute-start.4 = (bf16[4608,128]{1,0:T(8,128)(2,1)}, bf16[4608,128]{1,0:T(8,128)(2,1)S(1)}, u32[]{:S(2)}, u32[]{:S(2)}) collective-permute-start(bf16[4608,128]{1,0:T(8,128)(2,1)} %bitcast.17), channel_id=1, source_target_pairs={{0,1},{1,0},{2,3},{3,2},{4,5},{5,4},{6,7},{7,6},{8,9},{9,8},{10,11... | collective-permute-start | bytes 3538952 | tf_op jit(solution)/shard_map/ppermute | solution.py:70
  1.1 1.1 %dynamic-slice_bitcast_fusion = (bf16[160,576]{1,0:T(8,128)(2,1)S(1)}, bf16[160,576]{1,0:T(8,128)(2,1)S(1)}) fusion(bf16[8,160,576]{2,1,0:T(8,128)(2,1)} %bitcast.20, s32[]{:T(128)S(6)} %select_n.36, s32[]{:T(128)S(6)} %select_n.35), kind=kLoop, calls=%fused_computation | loop fusion | bytes 737288 | tf_op jit(solution)/shard_map/jit(dynamic_index_in_dim)/squeeze | solution.py:239
  2.2 2.6 %collective-permute-start = (bf16[160,576]{1,0:T(8,128)(2,1)S(1)}, bf16[160,576]{1,0:T(8,128)(2,1)S(1)}, u32[]{:S(2)}, u32[]{:S(2)}) collective-permute-start(bf16[160,576]{1,0:T(8,128)(2,1)S(1)} %get-tuple-element.33.refs_0_), channel_id=1, source_target_pairs={{0,2},{1,3},{2,0},{3,1},{4,6},{5,7},{6,4},{7,5},{8,10},{9,11},{10,... | collective-permute-start | bytes 552968 | tf_op jit(solution)/shard_map/ppermute | solution.py:70
  4.8 1.3 %collective-permute-start.3 = (bf16[160,576]{1,0:T(8,128)(2,1)S(1)}, bf16[160,576]{1,0:T(8,128)(2,1)S(1)}, u32[]{:S(2)}, u32[]{:S(2)}) collective-permute-start(bf16[160,576]{1,0:T(8,128)(2,1)S(1)} %get-tuple-element.17), channel_id=1, source_target_pairs={{0,5},{1,4},{2,7},{3,6},{4,1},{5,0},{6,3},{7,2},{8,13},{9,12},{10,... | collective-permute-start | bytes 552968 | tf_op jit(solution)/shard_map/ppermute | solution.py:70
  6.7 4.1 %collective-permute-done.refs_1_ = bf16[160,576]{1,0:T(8,128)(2,1)S(1)} collective-permute-done((bf16[160,576]{1,0:T(8,128)(2,1)S(1)}, bf16[160,576]{1,0:T(8,128)(2,1)S(1)}, u32[]{:S(2)}, u32[]{:S(2)}) %collective-permute-start) | collective-permute-done | bytes 184352 | tf_op jit(solution)/shard_map/ppermute | solution.py:70
  10.7 2.0 %collective-permute-start.7 = (bf16[160,576]{1,0:T(8,128)(2,1)S(1)}, bf16[160,576]{1,0:T(8,128)(2,1)S(1)}, u32[]{:S(2)}, u32[]{:S(2)}) collective-permute-start(bf16[160,576]{1,0:T(8,128)(2,1)S(1)} %collective-permute-done.refs_1_), channel_id=1, source_target_pairs={{0,4},{1,5},{2,6},{3,7},{4,0},{5,1},{6,2},{7,3},{8,12},{9,13},{10,... | collective-permute-start | bytes 552968 | tf_op jit(solution)/shard_map/ppermute | solution.py:70
  12.7 1.5 %collective-permute-start.8 = (bf16[160,576]{1,0:T(8,128)(2,1)S(1)}, bf16[160,576]{1,0:T(8,128)(2,1)S(1)}, u32[]{:S(2)}, u32[]{:S(2)}) collective-permute-start(bf16[160,576]{1,0:T(8,128)(2,1)S(1)} %collective-permute-done.3.refs_4_), channel_id=1, source_target_pairs={{0,2},{1,3},{2,0},{3,1},{4,6},{5,7},{6,4},{7,5},{8,10},{9,11},{10,... | collective-permute-start | bytes 552968 | tf_op jit(solution)/shard_map/ppermute | solution.py:70
  14.2 0.7 %add_multiply_fusion = f32[1,128]{1,0:T(1,128)S(1)} fusion(s32[1,128]{1,0:T(1,128)} %param.8), kind=kLoop, calls=%fused_computation.5 | loop fusion | flops 384 | bytes 1024 | tf_op jit(solution)/shard_map/mul | solution.py:240
  14.9 0.7 %pad_maximum_fusion.refs_8_ = f32[2,128]{1,0:T(2,128)S(1)} fusion(f32[1,128]{1,0:T(1,128)S(1)} %add_multiply_fusion, f32[1,128]{1,0:T(1,128)} %param.7), kind=kLoop, calls=%fused_computation.4 | loop fusion | flops 256 | bytes 2048 | tf_op jit(solution)/shard_map/stack | solution.py:241
  15.5 0.6 %collective-permute-start.6 = (f32[2,128]{1,0:T(2,128)S(1)}, f32[2,128]{1,0:T(2,128)S(1)}, u32[]{:S(2)}, u32[]{:S(2)}) collective-permute-start(f32[2,128]{1,0:T(2,128)S(1)} %pad_maximum_fusion.refs_8_), channel_id=1, source_target_pairs={{0,1},{1,0},{2,3},{3,2},{4,5},{5,4},{6,7},{7,6},{8,9},{9,8},{10,11... | collective-permute-start | bytes 3080 | tf_op jit(solution)/shard_map/ppermute | solution.py:70
  16.1 0.7 %collective-permute-done.2.refs_3_ = bf16[160,576]{1,0:T(8,128)(2,1)S(1)} collective-permute-done((bf16[160,576]{1,0:T(8,128)(2,1)S(1)}, bf16[160,576]{1,0:T(8,128)(2,1)S(1)}, u32[]{:S(2)}, u32[]{:S(2)}) %collective-permute-start.2) | collective-permute-done | bytes 184352 | tf_op jit(solution)/shard_map/ppermute | solution.py:70
  16.9 1.3 %copy-done.1 = bf16[1,4608,128]{2,1,0:T(8,128)(2,1)S(1)} copy-done((bf16[1,4608,128]{2,1,0:T(8,128)(2,1)S(1)}, bf16[1,4608,128]{2,1,0:T(8,128)(2,1)}, u32[]{:S(2)}) %copy-start.1) | copy-done | bytes 1179672
  18.2 0.6 %shard_map.68 = (f32[160,256]{1,0:T(8,128)S(1)}, f32[1,256]{1,0:T(1,128)S(1)}, bf16[2,576,256]{2,1,0:T(8,128)(2,1)S(1)}) custom-call(bf16[160,576]{1,0:T(8,128)(2,1)S(1)} %get-tuple-element.33.refs_0_, bf16[160,576]{1,0:T(8,128)(2,1)S(1)} %collective-permute-done.refs_1_, bf16[160,576]{1,0:T(8,128)(2,1)S(1)} %collective-permute-done.1.refs_2_, ...), custom_call_target="tpu_custom_call" | custom-call | flops 283115520 | tf_op jit(solution)/shard_map/pallas_call | solution.py:111
  18.8 2.1 %collective-permute-done.7.refs_0_ = bf16[160,576]{1,0:T(8,128)(2,1)S(1)} collective-permute-done((bf16[160,576]{1,0:T(8,128)(2,1)S(1)}, bf16[160,576]{1,0:T(8,128)(2,1)S(1)}, u32[]{:S(2)}, u32[]{:S(2)}) %collective-permute-start.7) | collective-permute-done | bytes 184352 | tf_op jit(solution)/shard_map/ppermute | solution.py:70
  21.3 2.7 %collective-permute-start.10 = (bf16[160,256]{1,0:T(8,128)(2,1)S(1)}, bf16[160,256]{1,0:T(8,128)(2,1)S(1)}, u32[]{:S(2)}, u32[]{:S(2)}) collective-permute-start(bf16[160,256]{1,0:T(8,128)(2,1)S(1)} %shard_map.69.refs_0_), channel_id=1, source_target_pairs={{0,16},{8,24},{16,0},{24,8},{1,17},{9,25},{17,1},{25,9},{2,18},{10... | collective-permute-start | bytes 245768 | tf_op jit(solution)/shard_map/ppermute | solution.py:36
  23.9 0.7 %collective-permute-start.12 = (bf16[160,256]{1,0:T(8,128)(2,1)S(1)}, bf16[160,256]{1,0:T(8,128)(2,1)S(1)}, u32[]{:S(2)}, u32[]{:S(2)}) collective-permute-start(bf16[160,256]{1,0:T(8,128)(2,1)S(1)} %shard_map.69.refs_0_), channel_id=1, source_target_pairs={{0,0},{8,16},{16,8},{24,24},{1,1},{9,17},{17,9},{25,25},{2,2},{10,... | collective-permute-start | bytes 245768 | tf_op jit(solution)/shard_map/ppermute | solution.py:36
  24.6 2.9 %collective-permute-start.9 = (bf16[160,256]{1,0:T(8,128)(2,1)S(1)}, bf16[160,256]{1,0:T(8,128)(2,1)S(1)}, u32[]{:S(2)}, u32[]{:S(2)}) collective-permute-start(bf16[160,256]{1,0:T(8,128)(2,1)S(1)} %shard_map.69.refs_0_), channel_id=1, source_target_pairs={{0,8},{8,0},{16,24},{24,16},{1,9},{9,1},{17,25},{25,17},{2,10},{10... | collective-permute-start | bytes 245768 | tf_op jit(solution)/shard_map/ppermute | solution.py:36
  27.5 1.2 %collective-permute-done.11 = bf16[160,128]{1,0:T(8,128)(2,1)S(1)} collective-permute-done((bf16[160,128]{1,0:T(8,128)(2,1)S(1)}, bf16[160,128]{1,0:T(8,128)(2,1)S(1)}, u32[]{:S(2)}, u32[]{:S(2)}) %collective-permute-start.11) | collective-permute-done | bytes 40992 | tf_op jit(solution)/shard_map/ppermute | solution.py:70
  28.9 1.7 %collective-permute-done.9.refs_1_ = bf16[160,256]{1,0:T(8,128)(2,1)S(1)} collective-permute-done((bf16[160,256]{1,0:T(8,128)(2,1)S(1)}, bf16[160,256]{1,0:T(8,128)(2,1)S(1)}, u32[]{:S(2)}, u32[]{:S(2)}) %collective-permute-start.9) | collective-permute-done | bytes 81952 | tf_op jit(solution)/shard_map/ppermute | solution.py:36
  30.6 0.6 %shard_map.73 = (bf16[160,576]{1,0:T(8,128)(2,1)S(1)}, bf16[160,576]{1,0:T(8,128)(2,1)S(1)}) custom-call(bf16[160,256]{1,0:T(8,128)(2,1)S(1)} %shard_map.69.refs_0_, bf16[160,256]{1,0:T(8,128)(2,1)S(1)} %collective-permute-done.9.refs_1_, bf16[160,256]{1,0:T(8,128)(2,1)S(1)} %collective-permute-done.10.refs_2_, ...), custom_call_target="tpu_custom_call" | custom-call | tf_op jit(solution)/shard_map/pallas_call | solution.py:149
  31.2 1.6 %collective-permute-start.18 = (bf16[160,576]{1,0:T(8,128)(2,1)S(1)}, bf16[160,576]{1,0:T(8,128)(2,1)S(1)}, u32[]{:S(2)}, u32[]{:S(2)}) collective-permute-start(bf16[160,576]{1,0:T(8,128)(2,1)S(1)} %get-tuple-element.30), channel_id=1, source_target_pairs={{0,4},{1,5},{2,6},{3,7},{4,0},{5,1},{6,2},{7,3},{8,12},{9,13},{10,... | collective-permute-start | bytes 552968 | tf_op jit(solution)/shard_map/ppermute | solution.py:70
  32.8 0.5 %collective-permute-start.15 = (bf16[160,576]{1,0:T(8,128)(2,1)S(1)}, bf16[160,576]{1,0:T(8,128)(2,1)S(1)}, u32[]{:S(2)}, u32[]{:S(2)}) collective-permute-start(bf16[160,576]{1,0:T(8,128)(2,1)S(1)} %get-tuple-element.27), channel_id=1, source_target_pairs={{0,2},{1,3},{2,0},{3,1},{4,6},{5,7},{6,4},{7,5},{8,10},{9,11},{10,... | collective-permute-start | bytes 552968 | tf_op jit(solution)/shard_map/ppermute | solution.py:70
  33.3 0.6 %shard_map.72 = (bf16[160,576]{1,0:T(8,128)(2,1)S(1)}, bf16[160,576]{1,0:T(8,128)(2,1)S(1)}) custom-call(bf16[160,256]{1,0:T(8,128)(2,1)S(1)} %shard_map.69.refs_0_, bf16[160,256]{1,0:T(8,128)(2,1)S(1)} %collective-permute-done.9.refs_1_, bf16[160,256]{1,0:T(8,128)(2,1)S(1)} %collective-permute-done.10.refs_2_, ...), custom_call_target="tpu_custom_call" | custom-call | tf_op jit(solution)/shard_map/pallas_call | solution.py:149
  34.1 0.6 %shard_map.71 = (bf16[160,576]{1,0:T(8,128)(2,1)S(1)}, bf16[160,576]{1,0:T(8,128)(2,1)S(1)}) custom-call(bf16[160,256]{1,0:T(8,128)(2,1)S(1)} %shard_map.69.refs_0_, bf16[160,256]{1,0:T(8,128)(2,1)S(1)} %collective-permute-done.9.refs_1_, bf16[160,256]{1,0:T(8,128)(2,1)S(1)} %collective-permute-done.10.refs_2_, ...), custom_call_target="tpu_custom_call" | custom-call | tf_op jit(solution)/shard_map/pallas_call | solution.py:149
  34.7 1.6 %collective-permute-start.14 = (bf16[160,576]{1,0:T(8,128)(2,1)S(1)}, bf16[160,576]{1,0:T(8,128)(2,1)S(1)}, u32[]{:S(2)}, u32[]{:S(2)}) collective-permute-start(bf16[160,576]{1,0:T(8,128)(2,1)S(1)} %get-tuple-element.25), channel_id=1, source_target_pairs={{0,2},{1,3},{2,0},{3,1},{4,6},{5,7},{6,4},{7,5},{8,10},{9,11},{10,... | collective-permute-start | bytes 552968 | tf_op jit(solution)/shard_map/ppermute | solution.py:70
  36.3 0.6 %shard_map.70 = (bf16[160,576]{1,0:T(8,128)(2,1)S(1)}, bf16[160,576]{1,0:T(8,128)(2,1)S(1)}) custom-call(bf16[160,256]{1,0:T(8,128)(2,1)S(1)} %shard_map.69.refs_0_, bf16[160,256]{1,0:T(8,128)(2,1)S(1)} %collective-permute-done.9.refs_1_, bf16[160,256]{1,0:T(8,128)(2,1)S(1)} %collective-permute-done.10.refs_2_, ...), custom_call_target="tpu_custom_call" | custom-call | tf_op jit(solution)/shard_map/pallas_call | solution.py:149
  37.3 2.0 %collective-permute-done.18.b_ref = bf16[160,576]{1,0:T(8,128)(2,1)S(1)} collective-permute-done((bf16[160,576]{1,0:T(8,128)(2,1)S(1)}, bf16[160,576]{1,0:T(8,128)(2,1)S(1)}, u32[]{:S(2)}, u32[]{:S(2)}) %collective-permute-start.18) | collective-permute-done | bytes 184352 | tf_op jit(solution)/shard_map/ppermute | solution.py:70
  39.4 1.4 %collective-permute-done.15.b_ref = bf16[160,576]{1,0:T(8,128)(2,1)S(1)} collective-permute-done((bf16[160,576]{1,0:T(8,128)(2,1)S(1)}, bf16[160,576]{1,0:T(8,128)(2,1)S(1)}, u32[]{:S(2)}, u32[]{:S(2)}) %collective-permute-start.15) | collective-permute-done | bytes 184352 | tf_op jit(solution)/shard_map/ppermute | solution.py:70
  41.0 0.6 %maximum_select_fusion = bf16[2,160,128]{2,1,0:T(8,128)(2,1)} fusion(bf16[1,160,128]{2,1,0:T(8,128)(2,1)S(1)} %bitcast.22, bf16[1,160,128]{2,1,0:T(8,128)(2,1)S(1)} %get-tuple-element.34, pred[]{:T(512)S(6)} %eq.5), kind=kLoop, calls=%fused_computation.2 | loop fusion | flops 122880 | bytes 163841 | tf_op jit(solution)/shard_map/jit(_where)/select_n | solution.py:244
  41.7 3.5 %collective-permute-done.14.refs_1_ = bf16[160,576]{1,0:T(8,128)(2,1)S(1)} collective-permute-done((bf16[160,576]{1,0:T(8,128)(2,1)S(1)}, bf16[160,576]{1,0:T(8,128)(2,1)S(1)}, u32[]{:S(2)}, u32[]{:S(2)}) %collective-permute-start.14) | collective-permute-done | bytes 184352 | tf_op jit(solution)/shard_map/ppermute | solution.py:70
  45.2 1.6 %collective-permute-done.19.refs_4_ = bf16[160,576]{1,0:T(8,128)(2,1)S(1)} collective-permute-done((bf16[160,576]{1,0:T(8,128)(2,1)S(1)}, bf16[160,576]{1,0:T(8,128)(2,1)S(1)}, u32[]{:S(2)}, u32[]{:S(2)}) %collective-permute-start.19) | collective-permute-done | bytes 184352 | tf_op jit(solution)/shard_map/ppermute | solution.py:70
  47.0 0.9 %shard_map.76 = bf16[320,576]{1,0:T(8,128)(2,1)} custom-call(bf16[160,576]{1,0:T(8,128)(2,1)S(1)} %get-tuple-element.24.refs_0_, bf16[160,576]{1,0:T(8,128)(2,1)S(1)} %collective-permute-done.14.refs_1_, bf16[160,576]{1,0:T(8,128)(2,1)S(1)} %collective-permute-done.16.refs_2_, bf16[160,576]{1,0:T(8,128)(2,1)S(1)} %collective-permute-done.17.refs_3_, ...), custom_call_target="tpu_custom_call" | custom-call | tf_op jit(solution)/shard_map/pallas_call | solution.py:185
  (28 shorter events, 2.0 us)
Async XLA Ops:
  0.6 13.6 %collective-permute-start.4 = (bf16[4608,128]{1,0:T(8,128)(2,1)}, bf16[4608,128]{1,0:T(8,128)(2,1)S(1)}, u32[]{:S(2)}, u32[]{:S(2)}) collective-permute-start(bf16[4608,128]{1,0:T(8,128)(2,1)} %bitcast.17), channel_id=1, source_target_pairs={{0,1},{1,0},{2,3},{3,2},{4,5},{5,4},{6,7},{7,6},{8,9},{9,8},{10,11... | collective-permute-start | bytes 3538952 | tf_op jit(solution)/shard_map/ppermute | solution.py:70
  2.2 8.5 %collective-permute-start = (bf16[160,576]{1,0:T(8,128)(2,1)S(1)}, bf16[160,576]{1,0:T(8,128)(2,1)S(1)}, u32[]{:S(2)}, u32[]{:S(2)}) collective-permute-start(bf16[160,576]{1,0:T(8,128)(2,1)S(1)} %get-tuple-element.33.refs_0_), channel_id=1, source_target_pairs={{0,2},{1,3},{2,0},{3,1},{4,6},{5,7},{6,4},{7,5},{8,10},{9,11},{10,... | collective-permute-start | bytes 552968 | tf_op jit(solution)/shard_map/ppermute | solution.py:70
  4.8 7.9 %collective-permute-start.3 = (bf16[160,576]{1,0:T(8,128)(2,1)S(1)}, bf16[160,576]{1,0:T(8,128)(2,1)S(1)}, u32[]{:S(2)}, u32[]{:S(2)}) collective-permute-start(bf16[160,576]{1,0:T(8,128)(2,1)S(1)} %get-tuple-element.17), channel_id=1, source_target_pairs={{0,5},{1,4},{2,7},{3,6},{4,1},{5,0},{6,3},{7,2},{8,13},{9,12},{10,... | collective-permute-start | bytes 552968 | tf_op jit(solution)/shard_map/ppermute | solution.py:70
  6.1 9.4 %collective-permute-start.1 = (bf16[160,576]{1,0:T(8,128)(2,1)S(1)}, bf16[160,576]{1,0:T(8,128)(2,1)S(1)}, u32[]{:S(2)}, u32[]{:S(2)}) collective-permute-start(bf16[160,576]{1,0:T(8,128)(2,1)S(1)} %get-tuple-element.17), channel_id=1, source_target_pairs={{0,3},{1,2},{2,1},{3,0},{4,7},{5,6},{6,5},{7,4},{8,11},{9,10},{10,... | collective-permute-start | bytes 552968 | tf_op jit(solution)/shard_map/ppermute | solution.py:70
  6.6 10.3 %collective-permute-start.2 = (bf16[160,576]{1,0:T(8,128)(2,1)S(1)}, bf16[160,576]{1,0:T(8,128)(2,1)S(1)}, u32[]{:S(2)}, u32[]{:S(2)}) collective-permute-start(bf16[160,576]{1,0:T(8,128)(2,1)S(1)} %get-tuple-element.33.refs_0_), channel_id=1, source_target_pairs={{0,4},{1,5},{2,6},{3,7},{4,0},{5,1},{6,2},{7,3},{8,12},{9,13},{10,... | collective-permute-start | bytes 552968 | tf_op jit(solution)/shard_map/ppermute | solution.py:70
  10.7 10.2 %collective-permute-start.7 = (bf16[160,576]{1,0:T(8,128)(2,1)S(1)}, bf16[160,576]{1,0:T(8,128)(2,1)S(1)}, u32[]{:S(2)}, u32[]{:S(2)}) collective-permute-start(bf16[160,576]{1,0:T(8,128)(2,1)S(1)} %collective-permute-done.refs_1_), channel_id=1, source_target_pairs={{0,4},{1,5},{2,6},{3,7},{4,0},{5,1},{6,2},{7,3},{8,12},{9,13},{10,... | collective-permute-start | bytes 552968 | tf_op jit(solution)/shard_map/ppermute | solution.py:70
  12.7 8.2 %collective-permute-start.8 = (bf16[160,576]{1,0:T(8,128)(2,1)S(1)}, bf16[160,576]{1,0:T(8,128)(2,1)S(1)}, u32[]{:S(2)}, u32[]{:S(2)}) collective-permute-start(bf16[160,576]{1,0:T(8,128)(2,1)S(1)} %collective-permute-done.3.refs_4_), channel_id=1, source_target_pairs={{0,2},{1,3},{2,0},{3,1},{4,6},{5,7},{6,4},{7,5},{8,10},{9,11},{10,... | collective-permute-start | bytes 552968 | tf_op jit(solution)/shard_map/ppermute | solution.py:70
  14.2 2.7 %collective-permute-start.5 = (bf16[160,576]{1,0:T(8,128)(2,1)S(1)}, bf16[160,576]{1,0:T(8,128)(2,1)S(1)}, u32[]{:S(2)}, u32[]{:S(2)}) collective-permute-start(bf16[160,576]{1,0:T(8,128)(2,1)S(1)} %get-tuple-element.17), channel_id=1, source_target_pairs={{0,1},{1,0},{2,3},{3,2},{4,5},{5,4},{6,7},{7,6},{8,9},{9,8},{10,11... | collective-permute-start | bytes 552968 | tf_op jit(solution)/shard_map/ppermute | solution.py:70
  15.5 5.4 %copy-start = (bf16[1,3,128,4608]{3,2,1,0:T(8,128)(2,1)S(1)}, bf16[1,3,128,4608]{3,2,1,0:T(8,128)(2,1)}, u32[]{:S(2)}) copy-start(bf16[1,3,128,4608]{3,2,1,0:T(8,128)(2,1)} %param.9) | copy-start | bytes 10616836
  15.5 1.4 %collective-permute-start.6 = (f32[2,128]{1,0:T(2,128)S(1)}, f32[2,128]{1,0:T(2,128)S(1)}, u32[]{:S(2)}, u32[]{:S(2)}) collective-permute-start(f32[2,128]{1,0:T(2,128)S(1)} %pad_maximum_fusion.refs_8_), channel_id=1, source_target_pairs={{0,1},{1,0},{2,3},{3,2},{4,5},{5,4},{6,7},{7,6},{8,9},{9,8},{10,11... | collective-permute-start | bytes 3080 | tf_op jit(solution)/shard_map/ppermute | solution.py:70
  16.9 1.3 %copy-start.1 = (bf16[1,4608,128]{2,1,0:T(8,128)(2,1)S(1)}, bf16[1,4608,128]{2,1,0:T(8,128)(2,1)}, u32[]{:S(2)}) copy-start(bf16[1,4608,128]{2,1,0:T(8,128)(2,1)} %param.6) | copy-start | bytes 3538948
  21.0 9.6 %collective-permute-start.13 = (bf16[3,128,4608]{2,1,0:T(8,128)(2,1)S(1)}, bf16[3,128,4608]{2,1,0:T(8,128)(2,1)S(1)}, u32[]{:S(2)}, u32[]{:S(2)}) collective-permute-start(bf16[3,128,4608]{2,1,0:T(8,128)(2,1)S(1)} %bitcast.12), channel_id=1, source_target_pairs={{0,1},{1,0},{2,3},{3,2},{4,5},{5,4},{6,7},{7,6},{8,9},{9,8},{10,11... | collective-permute-start | bytes 10616840 | tf_op jit(solution)/shard_map/ppermute | solution.py:70
  21.3 7.6 %collective-permute-start.10 = (bf16[160,256]{1,0:T(8,128)(2,1)S(1)}, bf16[160,256]{1,0:T(8,128)(2,1)S(1)}, u32[]{:S(2)}, u32[]{:S(2)}) collective-permute-start(bf16[160,256]{1,0:T(8,128)(2,1)S(1)} %shard_map.69.refs_0_), channel_id=1, source_target_pairs={{0,16},{8,24},{16,0},{24,8},{1,17},{9,25},{17,1},{25,9},{2,18},{10... | collective-permute-start | bytes 245768 | tf_op jit(solution)/shard_map/ppermute | solution.py:36
  23.9 4.9 %collective-permute-start.12 = (bf16[160,256]{1,0:T(8,128)(2,1)S(1)}, bf16[160,256]{1,0:T(8,128)(2,1)S(1)}, u32[]{:S(2)}, u32[]{:S(2)}) collective-permute-start(bf16[160,256]{1,0:T(8,128)(2,1)S(1)} %shard_map.69.refs_0_), channel_id=1, source_target_pairs={{0,0},{8,16},{16,8},{24,24},{1,1},{9,17},{17,9},{25,25},{2,2},{10,... | collective-permute-start | bytes 245768 | tf_op jit(solution)/shard_map/ppermute | solution.py:36
  24.6 6.0 %collective-permute-start.9 = (bf16[160,256]{1,0:T(8,128)(2,1)S(1)}, bf16[160,256]{1,0:T(8,128)(2,1)S(1)}, u32[]{:S(2)}, u32[]{:S(2)}) collective-permute-start(bf16[160,256]{1,0:T(8,128)(2,1)S(1)} %shard_map.69.refs_0_), channel_id=1, source_target_pairs={{0,8},{8,0},{16,24},{24,16},{1,9},{9,1},{17,25},{25,17},{2,10},{10... | collective-permute-start | bytes 245768 | tf_op jit(solution)/shard_map/ppermute | solution.py:36
  27.5 1.2 %collective-permute-start.11 = (bf16[160,128]{1,0:T(8,128)(2,1)S(1)}, bf16[160,128]{1,0:T(8,128)(2,1)S(1)}, u32[]{:S(2)}, u32[]{:S(2)}) collective-permute-start(bf16[160,128]{1,0:T(8,128)(2,1)S(1)} %get-tuple-element.35), channel_id=1, source_target_pairs={{0,1},{1,0},{2,3},{3,2},{4,5},{5,4},{6,7},{7,6},{8,9},{9,8},{10,11... | collective-permute-start | bytes 122888 | tf_op jit(solution)/shard_map/ppermute | solution.py:70
  31.2 8.0 %collective-permute-start.18 = (bf16[160,576]{1,0:T(8,128)(2,1)S(1)}, bf16[160,576]{1,0:T(8,128)(2,1)S(1)}, u32[]{:S(2)}, u32[]{:S(2)}) collective-permute-start(bf16[160,576]{1,0:T(8,128)(2,1)S(1)} %get-tuple-element.30), channel_id=1, source_target_pairs={{0,4},{1,5},{2,6},{3,7},{4,0},{5,1},{6,2},{7,3},{8,12},{9,13},{10,... | collective-permute-start | bytes 552968 | tf_op jit(solution)/shard_map/ppermute | solution.py:70
  32.8 8.0 %collective-permute-start.15 = (bf16[160,576]{1,0:T(8,128)(2,1)S(1)}, bf16[160,576]{1,0:T(8,128)(2,1)S(1)}, u32[]{:S(2)}, u32[]{:S(2)}) collective-permute-start(bf16[160,576]{1,0:T(8,128)(2,1)S(1)} %get-tuple-element.27), channel_id=1, source_target_pairs={{0,2},{1,3},{2,0},{3,1},{4,6},{5,7},{6,4},{7,5},{8,10},{9,11},{10,... | collective-permute-start | bytes 552968 | tf_op jit(solution)/shard_map/ppermute | solution.py:70
  34.0 7.7 %collective-permute-start.20 = (bf16[160,576]{1,0:T(8,128)(2,1)S(1)}, bf16[160,576]{1,0:T(8,128)(2,1)S(1)}, u32[]{:S(2)}, u32[]{:S(2)}) collective-permute-start(bf16[160,576]{1,0:T(8,128)(2,1)S(1)} %get-tuple-element.31), channel_id=1, source_target_pairs={{0,5},{1,4},{2,7},{3,6},{4,1},{5,0},{6,3},{7,2},{8,13},{9,12},{10,... | collective-permute-start | bytes 552968 | tf_op jit(solution)/shard_map/ppermute | solution.py:70
  34.7 10.5 %collective-permute-start.14 = (bf16[160,576]{1,0:T(8,128)(2,1)S(1)}, bf16[160,576]{1,0:T(8,128)(2,1)S(1)}, u32[]{:S(2)}, u32[]{:S(2)}) collective-permute-start(bf16[160,576]{1,0:T(8,128)(2,1)S(1)} %get-tuple-element.25), channel_id=1, source_target_pairs={{0,2},{1,3},{2,0},{3,1},{4,6},{5,7},{6,4},{7,5},{8,10},{9,11},{10,... | collective-permute-start | bytes 552968 | tf_op jit(solution)/shard_map/ppermute | solution.py:70
  36.9 8.3 %collective-permute-start.17 = (bf16[160,576]{1,0:T(8,128)(2,1)S(1)}, bf16[160,576]{1,0:T(8,128)(2,1)S(1)}, u32[]{:S(2)}, u32[]{:S(2)}) collective-permute-start(bf16[160,576]{1,0:T(8,128)(2,1)S(1)} %get-tuple-element.28), channel_id=1, source_target_pairs={{0,1},{1,0},{2,3},{3,2},{4,5},{5,4},{6,7},{7,6},{8,9},{9,8},{10,11... | collective-permute-start | bytes 552968 | tf_op jit(solution)/shard_map/ppermute | solution.py:70
  39.3 7.5 %collective-permute-start.19 = (bf16[160,576]{1,0:T(8,128)(2,1)S(1)}, bf16[160,576]{1,0:T(8,128)(2,1)S(1)}, u32[]{:S(2)}, u32[]{:S(2)}) collective-permute-start(bf16[160,576]{1,0:T(8,128)(2,1)S(1)} %shard_map.75), channel_id=1, source_target_pairs={{0,3},{1,2},{2,1},{3,0},{4,7},{5,6},{6,5},{7,4},{8,11},{9,10},{10,... | collective-permute-start | bytes 552968 | tf_op jit(solution)/shard_map/ppermute | solution.py:70
  40.9 6.1 %collective-permute-start.16 = (bf16[160,576]{1,0:T(8,128)(2,1)S(1)}, bf16[160,576]{1,0:T(8,128)(2,1)S(1)}, u32[]{:S(2)}, u32[]{:S(2)}) collective-permute-start(bf16[160,576]{1,0:T(8,128)(2,1)S(1)} %shard_map.74), channel_id=1, source_target_pairs={{0,4},{1,5},{2,6},{3,7},{4,0},{5,1},{6,2},{7,3},{8,12},{9,13},{10,... | collective-permute-start | bytes 552968 | tf_op jit(solution)/shard_map/ppermute | solution.py:70

commit v2 on v0

--- a/solution.py
+++ b/solution.py
@@ -20,17 +20,20 @@
     return lax.optimization_barrier((value, *others))[0]
 
 
-def layer_offsets(reach):
-    return sorted({layer ^ (layer - hop) for hop in range(1, reach) for layer in range(hop, LAYERS)})
-
-
-def other_layers(value, reach, group_size):
-    received = []
-    for offset in layer_offsets(reach):
-        wanted = {layer for layer in range(LAYERS) if 0 < layer - (layer ^ offset) < reach}
-        pairs = [(index, index ^ offset * group_size) for index in range(lax.axis_size("section"))]
-        pairs = [pair for pair in pairs if wanted & {end // group_size for end in pair}]
-        received.append(lax.ppermute(value, "section", pairs))
+def traded(value, parity, group_size):
+    def partner(layer):
+        other = layer - 1 if layer % 2 == parity else layer + 1
+        return other if 0 <= other < LAYERS else layer
+
+    pairs = [(i, partner(i // group_size) * group_size + i % group_size) for i in range(lax.axis_size("section"))]
+    return lax.ppermute(value, "section", pairs)
+
+
+def earlier_layers(value, reach, group_size):
+    received, even, odd = [], value, value
+    for _ in range(1, reach):
+        even, odd = traded(odd, 0, group_size), traded(even, 1, group_size)
+        received += [even, odd]
     return received
 
 
@@ -39,12 +42,9 @@
     own, *received = acts
     yield own[...]
     for hop in range(1, reach):
-        source = jnp.zeros(own.shape, own.dtype)
-        for offset, arrived in zip(layer_offsets(reach), received):
-            for target in range(hop, LAYERS):
-                if target ^ offset == target - hop:
-                    source = jnp.where(layer == target, arrived[...], source)
-        yield source
+        even, odd = received[2 * hop - 2:2 * hop]
+        source = jnp.where(layer % 2 == 0, even[...], odd[...])
+        yield jnp.where(layer >= hop, source, jnp.zeros_like(source))
 
 
 def group_reduce(partial_rows, group_size):
@@ -240,8 +240,8 @@
     kept, passed = acts[:, :lat], to_peer(acts[:, lat:], 1)
     latent_acts = jnp.where(core == 0, jnp.stack([kept, passed]), jnp.stack([passed, kept])).reshape(tok, lat)
 
-    received = other_layers(acts, reach, group_size)
-    received[1] = after(received[1], passed)
+    received = earlier_layers(acts, reach, group_size)
+    received[-1] = after(received[-1], passed)
     out_type = jnp.bfloat16 if group_size == 1 else jnp.float32
     summed = decode_and_scatter([acts, *received], decoder[0], dec_sib, width, out_type)
     rebuilt = group_reduce(summed, group_size).astype(jnp.bfloat16)

time: 48.7 us -> 52.1 us (1.070)
  the two profiles are of different devices: /device:TPU:0 before, /device:TPU:9 now
where the time goes in v2:
time: 52.1 us; the launch traced here: 51.9 us
  starting transfers between devices  22.9 us (44%)
  waiting for transfers between devices  19.6 us (38%)
  Pallas kernels  4.43 us (9%)
  local copies, waits for them, and re-layouts  2.35 us (5%)
  other arithmetic  1.97 us (4%)
  between operations  0.73 us (1%)
    ppermute x18, starting transfers between devices, to_peer(): lax.ppermute(value, 'latent', [(i, i ^ offset) for i in range(lax.axis_si...  17.5 us
    ppermute x18, waiting for transfers between devices, to_peer(): lax.ppermute(value, 'latent', [(i, i ^ offset) for i in range(lax.axis_si...  15.1 us
    ppermute x4, starting transfers between devices, traded(): return lax.ppermute(value, 'section', pairs)  5.41 us
    ppermute x4, waiting for transfers between devices, traded(): return lax.ppermute(value, 'section', pairs)  4.49 us
    pallas_call x4, Pallas kernels, decode_chip(): call(functools.partial(decode_chip_kernel, chip_offset), (shape, shape))  2.51 us
    unnamed x4, local copies, waits for them, and re-layouts  1.28 us
    squeeze x1, local copies, waits for them, and re-layouts, shards(): lax.dynamic_index_in_dim(halves, place + half, 0, keepdims=False)  1.06 us
  transfers between devices with their start and end apart: 22, of which 12 were waited for; matrix products, arithmetic and copies ran while one was open for 6% of the time, Pallas kernels for 6%

profile of v2, /device:TPU:9, one launch (start us, length us, event | category | flops | bytes accessed | tf_op | source)
XLA Modules:
  0.0 51.9 jit_solution(18209028801441559734)
XLA Ops:
  0.6 0.7 %collective-permute-start.4 = (bf16[4608,128]{1,0:T(8,128)(2,1)}, bf16[4608,128]{1,0:T(8,128)(2,1)S(1)}, u32[]{:S(2)}, u32[]{:S(2)}) collective-permute-start(bf16[4608,128]{1,0:T(8,128)(2,1)} %bitcast.17), channel_id=1, source_target_pairs={{0,1},{1,0},{2,3},{3,2},{4,5},{5,4},{6,7},{7,6},{8,9},{9,8},{10,11... | collective-permute-start | bytes 3538952 | tf_op jit(solution)/shard_map/ppermute | solution.py:67
  1.4 1.1 %dynamic-slice_bitcast_fusion = (bf16[160,576]{1,0:T(8,128)(2,1)S(1)}, bf16[160,576]{1,0:T(8,128)(2,1)S(1)}) fusion(bf16[8,160,576]{2,1,0:T(8,128)(2,1)} %bitcast.20, s32[]{:T(128)S(6)} %select_n.36, s32[]{:T(128)S(6)} %select_n.35), kind=kLoop, calls=%fused_computation | loop fusion | bytes 737288 | tf_op jit(solution)/shard_map/jit(dynamic_index_in_dim)/squeeze | solution.py:236
  2.4 1.3 %collective-permute-start = (bf16[160,576]{1,0:T(8,128)(2,1)S(1)}, bf16[160,576]{1,0:T(8,128)(2,1)S(1)}, u32[]{:S(2)}, u32[]{:S(2)}) collective-permute-start(bf16[160,576]{1,0:T(8,128)(2,1)S(1)} %get-tuple-element.33.refs_0_), channel_id=1, source_target_pairs={{0,2},{1,3},{2,0},{3,1},{4,6},{5,7},{6,4},{7,5},{8,10},{9,11},{10,... | collective-permute-start | bytes 552968 | tf_op jit(solution)/shard_map/ppermute | solution.py:67
  3.7 1.4 %collective-permute-start.3 = (bf16[160,576]{1,0:T(8,128)(2,1)S(1)}, bf16[160,576]{1,0:T(8,128)(2,1)S(1)}, u32[]{:S(2)}, u32[]{:S(2)}) collective-permute-start(bf16[160,576]{1,0:T(8,128)(2,1)S(1)} %get-tuple-element.17), channel_id=1, source_target_pairs={{0,5},{1,4},{2,7},{3,6},{4,1},{5,0},{6,3},{7,2},{8,13},{9,12},{10,... | collective-permute-start | bytes 552968 | tf_op jit(solution)/shard_map/ppermute | solution.py:67
  5.7 3.5 %collective-permute-done.refs_1_ = bf16[160,576]{1,0:T(8,128)(2,1)S(1)} collective-permute-done((bf16[160,576]{1,0:T(8,128)(2,1)S(1)}, bf16[160,576]{1,0:T(8,128)(2,1)S(1)}, u32[]{:S(2)}, u32[]{:S(2)}) %collective-permute-start) | collective-permute-done | bytes 184352 | tf_op jit(solution)/shard_map/ppermute | solution.py:67
  9.2 1.2 %collective-permute-start.7 = (bf16[160,576]{1,0:T(8,128)(2,1)S(1)}, bf16[160,576]{1,0:T(8,128)(2,1)S(1)}, u32[]{:S(2)}, u32[]{:S(2)}) collective-permute-start(bf16[160,576]{1,0:T(8,128)(2,1)S(1)} %collective-permute-done.refs_1_), channel_id=1, source_target_pairs={{0,4},{1,5},{2,6},{3,7},{4,0},{5,1},{6,2},{7,3},{8,12},{9,13},{10,... | collective-permute-start | bytes 552968 | tf_op jit(solution)/shard_map/ppermute | solution.py:67
  10.4 0.9 %collective-permute-done.3.refs_4_ = bf16[160,576]{1,0:T(8,128)(2,1)S(1)} collective-permute-done((bf16[160,576]{1,0:T(8,128)(2,1)S(1)}, bf16[160,576]{1,0:T(8,128)(2,1)S(1)}, u32[]{:S(2)}, u32[]{:S(2)}) %collective-permute-start.3) | collective-permute-done | bytes 184352 | tf_op jit(solution)/shard_map/ppermute | solution.py:67
  11.6 1.8 %collective-permute-start.5 = (bf16[160,576]{1,0:T(8,128)(2,1)S(1)}, bf16[160,576]{1,0:T(8,128)(2,1)S(1)}, u32[]{:S(2)}, u32[]{:S(2)}) collective-permute-start(bf16[160,576]{1,0:T(8,128)(2,1)S(1)} %get-tuple-element.17), channel_id=1, source_target_pairs={{0,1},{1,0},{2,3},{3,2},{4,5},{5,4},{6,7},{7,6},{8,9},{9,8},{10,11... | collective-permute-start | bytes 552968 | tf_op jit(solution)/shard_map/ppermute | solution.py:67
  13.4 0.7 %add_multiply_fusion = f32[1,128]{1,0:T(1,128)S(1)} fusion(s32[1,128]{1,0:T(1,128)} %param.8), kind=kLoop, calls=%fused_computation.5 | loop fusion | flops 384 | bytes 1024 | tf_op jit(solution)/shard_map/mul | solution.py:237
  14.1 0.7 %pad_maximum_fusion.refs_8_ = f32[2,128]{1,0:T(2,128)S(1)} fusion(f32[1,128]{1,0:T(1,128)S(1)} %add_multiply_fusion, f32[1,128]{1,0:T(1,128)} %param.7), kind=kLoop, calls=%fused_computation.4 | loop fusion | flops 256 | bytes 2048 | tf_op jit(solution)/shard_map/stack | solution.py:238
  15.1 0.8 %collective-permute-done.6.refs_9_ = f32[2,128]{1,0:T(2,128)S(1)} collective-permute-done((f32[2,128]{1,0:T(2,128)S(1)}, f32[2,128]{1,0:T(2,128)S(1)}, u32[]{:S(2)}, u32[]{:S(2)}) %collective-permute-start.6) | collective-permute-done | bytes 1056 | tf_op jit(solution)/shard_map/ppermute | solution.py:67
  16.0 1.3 %copy-done.1 = bf16[1,4608,128]{2,1,0:T(8,128)(2,1)S(1)} copy-done((bf16[1,4608,128]{2,1,0:T(8,128)(2,1)S(1)}, bf16[1,4608,128]{2,1,0:T(8,128)(2,1)}, u32[]{:S(2)}) %copy-start.1) | copy-done | bytes 1179672
  17.9 1.7 %collective-permute-done.7.refs_0_ = bf16[160,576]{1,0:T(8,128)(2,1)S(1)} collective-permute-done((bf16[160,576]{1,0:T(8,128)(2,1)S(1)}, bf16[160,576]{1,0:T(8,128)(2,1)S(1)}, u32[]{:S(2)}, u32[]{:S(2)}) %collective-permute-start.7) | collective-permute-done | bytes 184352 | tf_op jit(solution)/shard_map/ppermute | solution.py:67
  19.5 0.7 %collective-permute-start.14 = (bf16[3,128,4608]{2,1,0:T(8,128)(2,1)S(1)}, bf16[3,128,4608]{2,1,0:T(8,128)(2,1)S(1)}, u32[]{:S(2)}, u32[]{:S(2)}) collective-permute-start(bf16[3,128,4608]{2,1,0:T(8,128)(2,1)S(1)} %bitcast.12), channel_id=1, source_target_pairs={{0,1},{1,0},{2,3},{3,2},{4,5},{5,4},{6,7},{7,6},{8,9},{9,8},{10,11... | collective-permute-start | bytes 10616840 | tf_op jit(solution)/shard_map/ppermute | solution.py:67
  20.5 3.2 %collective-permute-start.9 = (bf16[160,256]{1,0:T(8,128)(2,1)S(1)}, bf16[160,256]{1,0:T(8,128)(2,1)S(1)}, u32[]{:S(2)}, u32[]{:S(2)}) collective-permute-start(bf16[160,256]{1,0:T(8,128)(2,1)S(1)} %shard_map.69.refs_0_), channel_id=1, source_target_pairs={{0,0},{8,16},{16,8},{24,24},{1,1},{9,17},{17,9},{25,25},{2,2},{10,... | collective-permute-start | bytes 245768 | tf_op jit(solution)/shard_map/ppermute | solution.py:29
  23.8 2.7 %collective-permute-done.9.refs_1_ = bf16[160,256]{1,0:T(8,128)(2,1)S(1)} collective-permute-done((bf16[160,256]{1,0:T(8,128)(2,1)S(1)}, bf16[160,256]{1,0:T(8,128)(2,1)S(1)}, u32[]{:S(2)}, u32[]{:S(2)}) %collective-permute-start.9) | collective-permute-done | bytes 81952 | tf_op jit(solution)/shard_map/ppermute | solution.py:29
  26.5 1.1 %collective-permute-done.10.refs_2_ = bf16[160,256]{1,0:T(8,128)(2,1)S(1)} collective-permute-done((bf16[160,256]{1,0:T(8,128)(2,1)S(1)}, bf16[160,256]{1,0:T(8,128)(2,1)S(1)}, u32[]{:S(2)}, u32[]{:S(2)}) %collective-permute-start.10) | collective-permute-done | bytes 81952 | tf_op jit(solution)/shard_map/ppermute | solution.py:29
  27.5 2.1 %collective-permute-start.11 = (bf16[160,256]{1,0:T(8,128)(2,1)S(1)}, bf16[160,256]{1,0:T(8,128)(2,1)S(1)}, u32[]{:S(2)}, u32[]{:S(2)}) collective-permute-start(bf16[160,256]{1,0:T(8,128)(2,1)S(1)} %collective-permute-done.10.refs_2_), channel_id=1, source_target_pairs={{0,0},{8,16},{16,8},{24,24},{1,1},{9,17},{17,9},{25,25},{2,2},{10,... | collective-permute-start | bytes 245768 | tf_op jit(solution)/shard_map/ppermute | solution.py:29
  29.7 1.4 %collective-permute-start.13 = (bf16[160,128]{1,0:T(8,128)(2,1)S(1)}, bf16[160,128]{1,0:T(8,128)(2,1)S(1)}, u32[]{:S(2)}, u32[]{:S(2)}) collective-permute-start(bf16[160,128]{1,0:T(8,128)(2,1)S(1)} %get-tuple-element.35), channel_id=1, source_target_pairs={{0,1},{1,0},{2,3},{3,2},{4,5},{5,4},{6,7},{7,6},{8,9},{9,8},{10,11... | collective-permute-start | bytes 122888 | tf_op jit(solution)/shard_map/ppermute | solution.py:67
  31.1 0.9 %collective-permute-done.13 = bf16[160,128]{1,0:T(8,128)(2,1)S(1)} collective-permute-done((bf16[160,128]{1,0:T(8,128)(2,1)S(1)}, bf16[160,128]{1,0:T(8,128)(2,1)S(1)}, u32[]{:S(2)}, u32[]{:S(2)}) %collective-permute-start.13) | collective-permute-done | bytes 40992 | tf_op jit(solution)/shard_map/ppermute | solution.py:67
  31.9 0.8 %collective-permute-done.11.refs_3_ = bf16[160,256]{1,0:T(8,128)(2,1)S(1)} collective-permute-done((bf16[160,256]{1,0:T(8,128)(2,1)S(1)}, bf16[160,256]{1,0:T(8,128)(2,1)S(1)}, u32[]{:S(2)}, u32[]{:S(2)}) %collective-permute-start.11) | collective-permute-done | bytes 81952 | tf_op jit(solution)/shard_map/ppermute | solution.py:29
  32.7 0.6 %shard_map.73 = (bf16[160,576]{1,0:T(8,128)(2,1)S(1)}, bf16[160,576]{1,0:T(8,128)(2,1)S(1)}) custom-call(bf16[160,256]{1,0:T(8,128)(2,1)S(1)} %shard_map.69.refs_0_, bf16[160,256]{1,0:T(8,128)(2,1)S(1)} %collective-permute-done.9.refs_1_, bf16[160,256]{1,0:T(8,128)(2,1)S(1)} %collective-permute-done.10.refs_2_, ...), custom_call_target="tpu_custom_call" | custom-call | tf_op jit(solution)/shard_map/pallas_call | solution.py:146
  33.3 1.3 %collective-permute-start.19 = (bf16[160,576]{1,0:T(8,128)(2,1)S(1)}, bf16[160,576]{1,0:T(8,128)(2,1)S(1)}, u32[]{:S(2)}, u32[]{:S(2)}) collective-permute-start(bf16[160,576]{1,0:T(8,128)(2,1)S(1)} %get-tuple-element.30), channel_id=1, source_target_pairs={{0,4},{1,5},{2,6},{3,7},{4,0},{5,1},{6,2},{7,3},{8,12},{9,13},{10,... | collective-permute-start | bytes 552968 | tf_op jit(solution)/shard_map/ppermute | solution.py:67
  34.9 0.6 %shard_map.72 = (bf16[160,576]{1,0:T(8,128)(2,1)S(1)}, bf16[160,576]{1,0:T(8,128)(2,1)S(1)}) custom-call(bf16[160,256]{1,0:T(8,128)(2,1)S(1)} %shard_map.69.refs_0_, bf16[160,256]{1,0:T(8,128)(2,1)S(1)} %collective-permute-done.9.refs_1_, bf16[160,256]{1,0:T(8,128)(2,1)S(1)} %collective-permute-done.10.refs_2_, ...), custom_call_target="tpu_custom_call" | custom-call | tf_op jit(solution)/shard_map/pallas_call | solution.py:146
  35.5 3.0 %collective-permute-start.21 = (bf16[160,576]{1,0:T(8,128)(2,1)S(1)}, bf16[160,576]{1,0:T(8,128)(2,1)S(1)}, u32[]{:S(2)}, u32[]{:S(2)}) collective-permute-start(bf16[160,576]{1,0:T(8,128)(2,1)S(1)} %get-tuple-element.31), channel_id=1, source_target_pairs={{0,5},{1,4},{2,7},{3,6},{4,1},{5,0},{6,3},{7,2},{8,13},{9,12},{10,... | collective-permute-start | bytes 552968 | tf_op jit(solution)/shard_map/ppermute | solution.py:67
  39.1 1.3 %collective-permute-start.15 = (bf16[160,576]{1,0:T(8,128)(2,1)S(1)}, bf16[160,576]{1,0:T(8,128)(2,1)S(1)}, u32[]{:S(2)}, u32[]{:S(2)}) collective-permute-start(bf16[160,576]{1,0:T(8,128)(2,1)S(1)} %get-tuple-element.25), channel_id=1, source_target_pairs={{0,2},{1,3},{2,0},{3,1},{4,6},{5,7},{6,4},{7,5},{8,10},{9,11},{10,... | collective-permute-start | bytes 552968 | tf_op jit(solution)/shard_map/ppermute | solution.py:67
  42.0 1.3 %collective-permute-start.17 = (bf16[160,576]{1,0:T(8,128)(2,1)S(1)}, bf16[160,576]{1,0:T(8,128)(2,1)S(1)}, u32[]{:S(2)}, u32[]{:S(2)}) collective-permute-start(bf16[160,576]{1,0:T(8,128)(2,1)S(1)} %shard_map.74), channel_id=1, source_target_pairs={{0,4},{1,5},{2,6},{3,7},{4,0},{5,1},{6,2},{7,3},{8,12},{9,13},{10,... | collective-permute-start | bytes 552968 | tf_op jit(solution)/shard_map/ppermute | solution.py:67
  43.3 0.6 %maximum_select_fusion = bf16[2,160,128]{2,1,0:T(8,128)(2,1)} fusion(bf16[1,160,128]{2,1,0:T(8,128)(2,1)S(1)} %bitcast.22, bf16[1,160,128]{2,1,0:T(8,128)(2,1)S(1)} %get-tuple-element.34, pred[]{:T(512)S(6)} %eq.5), kind=kLoop, calls=%fused_computation.2 | loop fusion | flops 122880 | bytes 163841 | tf_op jit(solution)/shard_map/jit(_where)/select_n | solution.py:241
  43.9 1.4 %collective-permute-done.21.refs_5_ = bf16[160,576]{1,0:T(8,128)(2,1)S(1)} collective-permute-done((bf16[160,576]{1,0:T(8,128)(2,1)S(1)}, bf16[160,576]{1,0:T(8,128)(2,1)S(1)}, u32[]{:S(2)}, u32[]{:S(2)}) %collective-permute-start.21) | collective-permute-done | bytes 184352 | tf_op jit(solution)/shard_map/ppermute | solution.py:67
  45.3 1.0 %collective-permute-done.15.refs_1_ = bf16[160,576]{1,0:T(8,128)(2,1)S(1)} collective-permute-done((bf16[160,576]{1,0:T(8,128)(2,1)S(1)}, bf16[160,576]{1,0:T(8,128)(2,1)S(1)}, u32[]{:S(2)}, u32[]{:S(2)}) %collective-permute-start.15) | collective-permute-done | bytes 184352 | tf_op jit(solution)/shard_map/ppermute | solution.py:67
  46.4 4.6 %collective-permute-done.20.refs_4_ = bf16[160,576]{1,0:T(8,128)(2,1)S(1)} collective-permute-done((bf16[160,576]{1,0:T(8,128)(2,1)S(1)}, bf16[160,576]{1,0:T(8,128)(2,1)S(1)}, u32[]{:S(2)}, u32[]{:S(2)}) %collective-permute-start.20) | collective-permute-done | bytes 184352 | tf_op jit(solution)/shard_map/ppermute | solution.py:67
  51.0 0.9 %shard_map.76 = bf16[320,576]{1,0:T(8,128)(2,1)} custom-call(bf16[160,576]{1,0:T(8,128)(2,1)S(1)} %get-tuple-element.24.refs_0_, bf16[160,576]{1,0:T(8,128)(2,1)S(1)} %collective-permute-done.15.refs_1_, bf16[160,576]{1,0:T(8,128)(2,1)S(1)} %collective-permute-done.17.refs_2_, bf16[160,576]{1,0:T(8,128)(2,1)S(1)} %collective-permute-done.18.refs_3_, ...), custom_call_target="tpu_custom_call" | custom-call | tf_op jit(solution)/shard_map/pallas_call | solution.py:182
  (30 shorter events, 4.6 us)
Async XLA Ops:
  0.6 11.0 %collective-permute-start.4 = (bf16[4608,128]{1,0:T(8,128)(2,1)}, bf16[4608,128]{1,0:T(8,128)(2,1)S(1)}, u32[]{:S(2)}, u32[]{:S(2)}) collective-permute-start(bf16[4608,128]{1,0:T(8,128)(2,1)} %bitcast.17), channel_id=1, source_target_pairs={{0,1},{1,0},{2,3},{3,2},{4,5},{5,4},{6,7},{7,6},{8,9},{9,8},{10,11... | collective-permute-start | bytes 3538952 | tf_op jit(solution)/shard_map/ppermute | solution.py:67
  2.4 6.7 %collective-permute-start = (bf16[160,576]{1,0:T(8,128)(2,1)S(1)}, bf16[160,576]{1,0:T(8,128)(2,1)S(1)}, u32[]{:S(2)}, u32[]{:S(2)}) collective-permute-start(bf16[160,576]{1,0:T(8,128)(2,1)S(1)} %get-tuple-element.33.refs_0_), channel_id=1, source_target_pairs={{0,2},{1,3},{2,0},{3,1},{4,6},{5,7},{6,4},{7,5},{8,10},{9,11},{10,... | collective-permute-start | bytes 552968 | tf_op jit(solution)/shard_map/ppermute | solution.py:67
  3.7 7.6 %collective-permute-start.3 = (bf16[160,576]{1,0:T(8,128)(2,1)S(1)}, bf16[160,576]{1,0:T(8,128)(2,1)S(1)}, u32[]{:S(2)}, u32[]{:S(2)}) collective-permute-start(bf16[160,576]{1,0:T(8,128)(2,1)S(1)} %get-tuple-element.17), channel_id=1, source_target_pairs={{0,5},{1,4},{2,7},{3,6},{4,1},{5,0},{6,3},{7,2},{8,13},{9,12},{10,... | collective-permute-start | bytes 552968 | tf_op jit(solution)/shard_map/ppermute | solution.py:67
  5.2 9.6 %collective-permute-start.1 = (bf16[160,576]{1,0:T(8,128)(2,1)S(1)}, bf16[160,576]{1,0:T(8,128)(2,1)S(1)}, u32[]{:S(2)}, u32[]{:S(2)}) collective-permute-start(bf16[160,576]{1,0:T(8,128)(2,1)S(1)} %get-tuple-element.17), channel_id=1, source_target_pairs={{0,3},{1,2},{2,1},{3,0},{4,7},{5,6},{6,5},{7,4},{8,11},{9,10},{10,... | collective-permute-start | bytes 552968 | tf_op jit(solution)/shard_map/ppermute | solution.py:67
  5.5 9.6 %collective-permute-start.2 = (bf16[160,576]{1,0:T(8,128)(2,1)S(1)}, bf16[160,576]{1,0:T(8,128)(2,1)S(1)}, u32[]{:S(2)}, u32[]{:S(2)}) collective-permute-start(bf16[160,576]{1,0:T(8,128)(2,1)S(1)} %get-tuple-element.33.refs_0_), channel_id=1, source_target_pairs={{0,4},{1,5},{2,6},{3,7},{4,0},{5,1},{6,2},{7,3},{8,12},{9,13},{10,... | collective-permute-start | bytes 552968 | tf_op jit(solution)/shard_map/ppermute | solution.py:67
  9.2 10.4 %collective-permute-start.7 = (bf16[160,576]{1,0:T(8,128)(2,1)S(1)}, bf16[160,576]{1,0:T(8,128)(2,1)S(1)}, u32[]{:S(2)}, u32[]{:S(2)}) collective-permute-start(bf16[160,576]{1,0:T(8,128)(2,1)S(1)} %collective-permute-done.refs_1_), channel_id=1, source_target_pairs={{0,4},{1,5},{2,6},{3,7},{4,0},{5,1},{6,2},{7,3},{8,12},{9,13},{10,... | collective-permute-start | bytes 552968 | tf_op jit(solution)/shard_map/ppermute | solution.py:67
  11.3 8.2 %collective-permute-start.8 = (bf16[160,576]{1,0:T(8,128)(2,1)S(1)}, bf16[160,576]{1,0:T(8,128)(2,1)S(1)}, u32[]{:S(2)}, u32[]{:S(2)}) collective-permute-start(bf16[160,576]{1,0:T(8,128)(2,1)S(1)} %collective-permute-done.3.refs_4_), channel_id=1, source_target_pairs={{0,2},{1,3},{2,0},{3,1},{4,6},{5,7},{6,4},{7,5},{8,10},{9,11},{10,... | collective-permute-start | bytes 552968 | tf_op jit(solution)/shard_map/ppermute | solution.py:67
  11.6 4.4 %collective-permute-start.5 = (bf16[160,576]{1,0:T(8,128)(2,1)S(1)}, bf16[160,576]{1,0:T(8,128)(2,1)S(1)}, u32[]{:S(2)}, u32[]{:S(2)}) collective-permute-start(bf16[160,576]{1,0:T(8,128)(2,1)S(1)} %get-tuple-element.17), channel_id=1, source_target_pairs={{0,1},{1,0},{2,3},{3,2},{4,5},{5,4},{6,7},{7,6},{8,9},{9,8},{10,11... | collective-permute-start | bytes 552968 | tf_op jit(solution)/shard_map/ppermute | solution.py:67
  14.8 4.8 %copy-start = (bf16[1,3,128,4608]{3,2,1,0:T(8,128)(2,1)S(1)}, bf16[1,3,128,4608]{3,2,1,0:T(8,128)(2,1)}, u32[]{:S(2)}) copy-start(bf16[1,3,128,4608]{3,2,1,0:T(8,128)(2,1)} %param.9) | copy-start | bytes 10616836
  14.8 1.2 %collective-permute-start.6 = (f32[2,128]{1,0:T(2,128)S(1)}, f32[2,128]{1,0:T(2,128)S(1)}, u32[]{:S(2)}, u32[]{:S(2)}) collective-permute-start(f32[2,128]{1,0:T(2,128)S(1)} %pad_maximum_fusion.refs_8_), channel_id=1, source_target_pairs={{0,1},{1,0},{2,3},{3,2},{4,5},{5,4},{6,7},{7,6},{8,9},{9,8},{10,11... | collective-permute-start | bytes 3080 | tf_op jit(solution)/shard_map/ppermute | solution.py:67
  16.0 1.3 %copy-start.1 = (bf16[1,4608,128]{2,1,0:T(8,128)(2,1)S(1)}, bf16[1,4608,128]{2,1,0:T(8,128)(2,1)}, u32[]{:S(2)}) copy-start(bf16[1,4608,128]{2,1,0:T(8,128)(2,1)} %param.6) | copy-start | bytes 3538948
  19.5 13.2 %collective-permute-start.14 = (bf16[3,128,4608]{2,1,0:T(8,128)(2,1)S(1)}, bf16[3,128,4608]{2,1,0:T(8,128)(2,1)S(1)}, u32[]{:S(2)}, u32[]{:S(2)}) collective-permute-start(bf16[3,128,4608]{2,1,0:T(8,128)(2,1)S(1)} %bitcast.12), channel_id=1, source_target_pairs={{0,1},{1,0},{2,3},{3,2},{4,5},{5,4},{6,7},{7,6},{8,9},{9,8},{10,11... | collective-permute-start | bytes 10616840 | tf_op jit(solution)/shard_map/ppermute | solution.py:67
  20.5 6.0 %collective-permute-start.9 = (bf16[160,256]{1,0:T(8,128)(2,1)S(1)}, bf16[160,256]{1,0:T(8,128)(2,1)S(1)}, u32[]{:S(2)}, u32[]{:S(2)}) collective-permute-start(bf16[160,256]{1,0:T(8,128)(2,1)S(1)} %shard_map.69.refs_0_), channel_id=1, source_target_pairs={{0,0},{8,16},{16,8},{24,24},{1,1},{9,17},{17,9},{25,25},{2,2},{10,... | collective-permute-start | bytes 245768 | tf_op jit(solution)/shard_map/ppermute | solution.py:29
  23.7 3.8 %collective-permute-start.10 = (bf16[160,256]{1,0:T(8,128)(2,1)S(1)}, bf16[160,256]{1,0:T(8,128)(2,1)S(1)}, u32[]{:S(2)}, u32[]{:S(2)}) collective-permute-start(bf16[160,256]{1,0:T(8,128)(2,1)S(1)} %shard_map.69.refs_0_), channel_id=1, source_target_pairs={{0,8},{8,0},{16,24},{24,16},{1,9},{9,1},{17,25},{25,17},{2,10},{10... | collective-permute-start | bytes 245768 | tf_op jit(solution)/shard_map/ppermute | solution.py:29
  26.5 5.5 %collective-permute-start.12 = (bf16[160,256]{1,0:T(8,128)(2,1)S(1)}, bf16[160,256]{1,0:T(8,128)(2,1)S(1)}, u32[]{:S(2)}, u32[]{:S(2)}) collective-permute-start(bf16[160,256]{1,0:T(8,128)(2,1)S(1)} %collective-permute-done.9.refs_1_), channel_id=1, source_target_pairs={{0,8},{8,0},{16,24},{24,16},{1,9},{9,1},{17,25},{25,17},{2,10},{10... | collective-permute-start | bytes 245768 | tf_op jit(solution)/shard_map/ppermute | solution.py:29
  27.5 5.2 %collective-permute-start.11 = (bf16[160,256]{1,0:T(8,128)(2,1)S(1)}, bf16[160,256]{1,0:T(8,128)(2,1)S(1)}, u32[]{:S(2)}, u32[]{:S(2)}) collective-permute-start(bf16[160,256]{1,0:T(8,128)(2,1)S(1)} %collective-permute-done.10.refs_2_), channel_id=1, source_target_pairs={{0,0},{8,16},{16,8},{24,24},{1,1},{9,17},{17,9},{25,25},{2,2},{10,... | collective-permute-start | bytes 245768 | tf_op jit(solution)/shard_map/ppermute | solution.py:29
  29.7 2.3 %collective-permute-start.13 = (bf16[160,128]{1,0:T(8,128)(2,1)S(1)}, bf16[160,128]{1,0:T(8,128)(2,1)S(1)}, u32[]{:S(2)}, u32[]{:S(2)}) collective-permute-start(bf16[160,128]{1,0:T(8,128)(2,1)S(1)} %get-tuple-element.35), channel_id=1, source_target_pairs={{0,1},{1,0},{2,3},{3,2},{4,5},{5,4},{6,7},{7,6},{8,9},{9,8},{10,11... | collective-permute-start | bytes 122888 | tf_op jit(solution)/shard_map/ppermute | solution.py:67
  33.3 8.0 %collective-permute-start.19 = (bf16[160,576]{1,0:T(8,128)(2,1)S(1)}, bf16[160,576]{1,0:T(8,128)(2,1)S(1)}, u32[]{:S(2)}, u32[]{:S(2)}) collective-permute-start(bf16[160,576]{1,0:T(8,128)(2,1)S(1)} %get-tuple-element.30), channel_id=1, source_target_pairs={{0,4},{1,5},{2,6},{3,7},{4,0},{5,1},{6,2},{7,3},{8,12},{9,13},{10,... | collective-permute-start | bytes 552968 | tf_op jit(solution)/shard_map/ppermute | solution.py:67
  34.6 7.3 %collective-permute-start.16 = (bf16[160,576]{1,0:T(8,128)(2,1)S(1)}, bf16[160,576]{1,0:T(8,128)(2,1)S(1)}, u32[]{:S(2)}, u32[]{:S(2)}) collective-permute-start(bf16[160,576]{1,0:T(8,128)(2,1)S(1)} %get-tuple-element.27), channel_id=1, source_target_pairs={{0,2},{1,3},{2,0},{3,1},{4,6},{5,7},{6,4},{7,5},{8,10},{9,11},{10,... | collective-permute-start | bytes 552968 | tf_op jit(solution)/shard_map/ppermute | solution.py:67
  35.5 9.8 %collective-permute-start.21 = (bf16[160,576]{1,0:T(8,128)(2,1)S(1)}, bf16[160,576]{1,0:T(8,128)(2,1)S(1)}, u32[]{:S(2)}, u32[]{:S(2)}) collective-permute-start(bf16[160,576]{1,0:T(8,128)(2,1)S(1)} %get-tuple-element.31), channel_id=1, source_target_pairs={{0,5},{1,4},{2,7},{3,6},{4,1},{5,0},{6,3},{7,2},{8,13},{9,12},{10,... | collective-permute-start | bytes 552968 | tf_op jit(solution)/shard_map/ppermute | solution.py:67
  39.1 7.2 %collective-permute-start.15 = (bf16[160,576]{1,0:T(8,128)(2,1)S(1)}, bf16[160,576]{1,0:T(8,128)(2,1)S(1)}, u32[]{:S(2)}, u32[]{:S(2)}) collective-permute-start(bf16[160,576]{1,0:T(8,128)(2,1)S(1)} %get-tuple-element.25), channel_id=1, source_target_pairs={{0,2},{1,3},{2,0},{3,1},{4,6},{5,7},{6,4},{7,5},{8,10},{9,11},{10,... | collective-permute-start | bytes 552968 | tf_op jit(solution)/shard_map/ppermute | solution.py:67
  41.0 5.3 %collective-permute-start.18 = (bf16[160,576]{1,0:T(8,128)(2,1)S(1)}, bf16[160,576]{1,0:T(8,128)(2,1)S(1)}, u32[]{:S(2)}, u32[]{:S(2)}) collective-permute-start(bf16[160,576]{1,0:T(8,128)(2,1)S(1)} %get-tuple-element.28), channel_id=1, source_target_pairs={{0,1},{1,0},{2,3},{3,2},{4,5},{5,4},{6,7},{7,6},{8,9},{9,8},{10,11... | collective-permute-start | bytes 552968 | tf_op jit(solution)/shard_map/ppermute | solution.py:67
  41.4 9.6 %collective-permute-start.20 = (bf16[160,576]{1,0:T(8,128)(2,1)S(1)}, bf16[160,576]{1,0:T(8,128)(2,1)S(1)}, u32[]{:S(2)}, u32[]{:S(2)}) collective-permute-start(bf16[160,576]{1,0:T(8,128)(2,1)S(1)} %shard_map.75), channel_id=1, source_target_pairs={{0,3},{1,2},{2,1},{3,0},{4,7},{5,6},{6,5},{7,4},{8,11},{9,10},{10,... | collective-permute-start | bytes 552968 | tf_op jit(solution)/shard_map/ppermute | solution.py:67
  42.0 9.1 %collective-permute-start.17 = (bf16[160,576]{1,0:T(8,128)(2,1)S(1)}, bf16[160,576]{1,0:T(8,128)(2,1)S(1)}, u32[]{:S(2)}, u32[]{:S(2)}) collective-permute-start(bf16[160,576]{1,0:T(8,128)(2,1)S(1)} %shard_map.74), channel_id=1, source_target_pairs={{0,4},{1,5},{2,6},{3,7},{4,0},{5,1},{6,2},{7,3},{8,12},{9,13},{10,... | collective-permute-start | bytes 552968 | tf_op jit(solution)/shard_map/ppermute | solution.py:67

commit v3 on v2

--- a/solution.py
+++ b/solution.py
@@ -20,31 +20,16 @@
     return lax.optimization_barrier((value, *others))[0]
 
 
-def traded(value, parity, group_size):
-    def partner(layer):
-        other = layer - 1 if layer % 2 == parity else layer + 1
-        return other if 0 <= other < LAYERS else layer
-
-    pairs = [(i, partner(i // group_size) * group_size + i % group_size) for i in range(lax.axis_size("section"))]
-    return lax.ppermute(value, "section", pairs)
-
-
 def earlier_layers(value, reach, group_size):
-    received, even, odd = [], value, value
-    for _ in range(1, reach):
-        even, odd = traded(odd, 0, group_size), traded(even, 1, group_size)
-        received += [even, odd]
-    return received
+    count = lax.axis_size("section")
+    shifts = [hop * group_size for hop in range(1, reach)]
+    return [lax.ppermute(value, "section", [(i, (i + shift) % count) for i in range(count)]) for shift in shifts]
 
 
 def by_hop(acts, reach):
     layer = lax.axis_index("section") // (lax.axis_size("section") // LAYERS)
-    own, *received = acts
-    yield own[...]
-    for hop in range(1, reach):
-        even, odd = received[2 * hop - 2:2 * hop]
-        source = jnp.where(layer % 2 == 0, even[...], odd[...])
-        yield jnp.where(layer >= hop, source, jnp.zeros_like(source))
+    for hop, values in enumerate(acts[:reach]):
+        yield jnp.where(layer >= hop, values[...], jnp.zeros(values.shape, values.dtype)) if hop else values[...]
 
 
 def group_reduce(partial_rows, group_size):
@@ -166,20 +151,32 @@
 
 
 def finish_kernel(*refs):
-    *parts, out_ref = refs
+    *parts, out_ref, sums, sems = refs
     half = len(parts) // 2
     rows = parts[0].shape[0]
     core = lax.axis_index("latent") % 2
-    for place, group in ((core, parts[:half]), (1 - core, parts[half:])):
+    copies = []
+    for index, (place, group) in enumerate(((core, parts[:half]), (1 - core, parts[half:]))):
         total = group[0][...].astype(jnp.float32)
         for part in group[1:]:
             total += part[...].astype(jnp.float32)
-        out_ref[pl.ds(pl.multiple_of(place * rows, 16), rows), :] = total.astype(out_ref.dtype)
+        sums[index] = total.astype(out_ref.dtype)
+        target = out_ref.at[pl.ds(pl.multiple_of(place * rows, 16), rows), :]
+        copies.append(pltpu.make_async_copy(sums.at[index], target, sems.at[index]))
+        copies[-1].start()
+    for copy in copies:
+        copy.wait()
 
 
 def finish(mine, other, dtype):
     rows, width = mine[0].shape
-    return call(finish_kernel, jax.ShapeDtypeStruct((2 * rows, width), dtype))(*mine, *other)
+    return pl.pallas_call(
+        finish_kernel,
+        out_shape=jax.ShapeDtypeStruct((2 * rows, width), dtype),
+        out_specs=pl.BlockSpec(memory_space=pl.ANY),
+        scratch_shapes=[pltpu.VMEM((2, rows, width), dtype), pltpu.SemaphoreType.DMA((2,))],
+        compiler_params=pltpu.CompilerParams(vmem_limit_bytes=VMEM_LIMIT),
+    )(*mine, *other)
 
 
 def gather_and_encode(mine, other, gates, encoder, decoder):

time: 52.1 us -> 47.9 us (0.919)
  the two profiles are of different devices: /device:TPU:9 before, /device:TPU:0 now
where the time goes in v3:
time: 47.9 us; the launch traced here: 47.6 us
  waiting for transfers between devices  19.5 us (41%)
  starting transfers between devices  18.7 us (39%)
  Pallas kernels  4.35 us (9%)
  local copies, waits for them, and re-layouts  2.35 us (5%)
  other arithmetic  1.97 us (4%)
  between operations  0.72 us (2%)
    ppermute x18, waiting for transfers between devices, to_peer(): lax.ppermute(value, 'latent', [(i, i ^ offset) for i in range(lax.axis_si...  16.2 us
    ppermute x18, starting transfers between devices, to_peer(): lax.ppermute(value, 'latent', [(i, i ^ offset) for i in range(lax.axis_si...  14.4 us
    ppermute x2, starting transfers between devices, earlier_layers(): lax.ppermute(value, 'section', [(i, (i + shift) % count) for i in range(c...  4.23 us
    ppermute x2, waiting for transfers between devices, earlier_layers(): lax.ppermute(value, 'section', [(i, (i + shift) % count) for i in range(c...  3.34 us
    pallas_call x4, Pallas kernels, decode_chip(): call(functools.partial(decode_chip_kernel, chip_offset), (shape, shape))  2.51 us
    unnamed x4, local copies, waits for them, and re-layouts  1.27 us
    squeeze x1, local copies, waits for them, and re-layouts, shards(): lax.dynamic_index_in_dim(halves, place + half, 0, keepdims=False)  1.06 us
  transfers between devices with their start and end apart: 20, of which 11 were waited for; matrix products, arithmetic and copies ran while one was open for 6% of the time, Pallas kernels for 6%

profile of v3, /device:TPU:0, one launch (start us, length us, event | category | flops | bytes accessed | tf_op | source)
XLA Modules:
  0.0 47.6 jit_solution(2194057921395567695)
XLA Ops:
  0.6 0.5 %collective-permute-start.4 = (bf16[4608,128]{1,0:T(8,128)(2,1)}, bf16[4608,128]{1,0:T(8,128)(2,1)S(1)}, u32[]{:S(2)}, u32[]{:S(2)}) collective-permute-start(bf16[4608,128]{1,0:T(8,128)(2,1)} %bitcast.17), channel_id=1, source_target_pairs={{0,1},{1,0},{2,3},{3,2},{4,5},{5,4},{6,7},{7,6},{8,9},{9,8},{10,11... | collective-permute-start | bytes 3538952 | tf_op jit(solution)/shard_map/ppermute | solution.py:52
  1.1 1.1 %dynamic-slice_bitcast_fusion = (bf16[160,576]{1,0:T(8,128)(2,1)S(1)}, bf16[160,576]{1,0:T(8,128)(2,1)S(1)}) fusion(bf16[8,160,576]{2,1,0:T(8,128)(2,1)} %bitcast.20, s32[]{:T(128)S(6)} %select_n.36, s32[]{:T(128)S(6)} %select_n.35), kind=kLoop, calls=%fused_computation | loop fusion | bytes 737288 | tf_op jit(solution)/shard_map/jit(dynamic_index_in_dim)/squeeze | solution.py:233
  2.2 2.6 %collective-permute-start = (bf16[160,576]{1,0:T(8,128)(2,1)S(1)}, bf16[160,576]{1,0:T(8,128)(2,1)S(1)}, u32[]{:S(2)}, u32[]{:S(2)}) collective-permute-start(bf16[160,576]{1,0:T(8,128)(2,1)S(1)} %get-tuple-element.33.refs_0_), channel_id=1, source_target_pairs={{0,2},{1,3},{2,0},{3,1},{4,6},{5,7},{6,4},{7,5},{8,10},{9,11},{10,... | collective-permute-start | bytes 552968 | tf_op jit(solution)/shard_map/ppermute | solution.py:52
  4.8 1.3 %collective-permute-start.3 = (bf16[160,576]{1,0:T(8,128)(2,1)S(1)}, bf16[160,576]{1,0:T(8,128)(2,1)S(1)}, u32[]{:S(2)}, u32[]{:S(2)}) collective-permute-start(bf16[160,576]{1,0:T(8,128)(2,1)S(1)} %get-tuple-element.17), channel_id=1, source_target_pairs={{0,5},{1,4},{2,7},{3,6},{4,1},{5,0},{6,3},{7,2},{8,13},{9,12},{10,... | collective-permute-start | bytes 552968 | tf_op jit(solution)/shard_map/ppermute | solution.py:52
  6.7 4.1 %collective-permute-done.refs_1_ = bf16[160,576]{1,0:T(8,128)(2,1)S(1)} collective-permute-done((bf16[160,576]{1,0:T(8,128)(2,1)S(1)}, bf16[160,576]{1,0:T(8,128)(2,1)S(1)}, u32[]{:S(2)}, u32[]{:S(2)}) %collective-permute-start) | collective-permute-done | bytes 184352 | tf_op jit(solution)/shard_map/ppermute | solution.py:52
  10.7 2.0 %collective-permute-start.7 = (bf16[160,576]{1,0:T(8,128)(2,1)S(1)}, bf16[160,576]{1,0:T(8,128)(2,1)S(1)}, u32[]{:S(2)}, u32[]{:S(2)}) collective-permute-start(bf16[160,576]{1,0:T(8,128)(2,1)S(1)} %collective-permute-done.refs_1_), channel_id=1, source_target_pairs={{0,4},{1,5},{2,6},{3,7},{4,0},{5,1},{6,2},{7,3},{8,12},{9,13},{10,... | collective-permute-start | bytes 552968 | tf_op jit(solution)/shard_map/ppermute | solution.py:52
  12.7 1.5 %collective-permute-start.8 = (bf16[160,576]{1,0:T(8,128)(2,1)S(1)}, bf16[160,576]{1,0:T(8,128)(2,1)S(1)}, u32[]{:S(2)}, u32[]{:S(2)}) collective-permute-start(bf16[160,576]{1,0:T(8,128)(2,1)S(1)} %collective-permute-done.3.refs_4_), channel_id=1, source_target_pairs={{0,2},{1,3},{2,0},{3,1},{4,6},{5,7},{6,4},{7,5},{8,10},{9,11},{10,... | collective-permute-start | bytes 552968 | tf_op jit(solution)/shard_map/ppermute | solution.py:52
  14.2 0.7 %add_multiply_fusion = f32[1,128]{1,0:T(1,128)S(1)} fusion(s32[1,128]{1,0:T(1,128)} %param.8), kind=kLoop, calls=%fused_computation.5 | loop fusion | flops 384 | bytes 1024 | tf_op jit(solution)/shard_map/mul | solution.py:234
  14.9 0.7 %pad_maximum_fusion.refs_8_ = f32[2,128]{1,0:T(2,128)S(1)} fusion(f32[1,128]{1,0:T(1,128)S(1)} %add_multiply_fusion, f32[1,128]{1,0:T(1,128)} %param.7), kind=kLoop, calls=%fused_computation.4 | loop fusion | flops 256 | bytes 2048 | tf_op jit(solution)/shard_map/stack | solution.py:235
  15.5 0.6 %collective-permute-start.6 = (f32[2,128]{1,0:T(2,128)S(1)}, f32[2,128]{1,0:T(2,128)S(1)}, u32[]{:S(2)}, u32[]{:S(2)}) collective-permute-start(f32[2,128]{1,0:T(2,128)S(1)} %pad_maximum_fusion.refs_8_), channel_id=1, source_target_pairs={{0,1},{1,0},{2,3},{3,2},{4,5},{5,4},{6,7},{7,6},{8,9},{9,8},{10,11... | collective-permute-start | bytes 3080 | tf_op jit(solution)/shard_map/ppermute | solution.py:52
  16.1 0.7 %collective-permute-done.2.refs_3_ = bf16[160,576]{1,0:T(8,128)(2,1)S(1)} collective-permute-done((bf16[160,576]{1,0:T(8,128)(2,1)S(1)}, bf16[160,576]{1,0:T(8,128)(2,1)S(1)}, u32[]{:S(2)}, u32[]{:S(2)}) %collective-permute-start.2) | collective-permute-done | bytes 184352 | tf_op jit(solution)/shard_map/ppermute | solution.py:52
  16.9 1.3 %copy-done.1 = bf16[1,4608,128]{2,1,0:T(8,128)(2,1)S(1)} copy-done((bf16[1,4608,128]{2,1,0:T(8,128)(2,1)S(1)}, bf16[1,4608,128]{2,1,0:T(8,128)(2,1)}, u32[]{:S(2)}) %copy-start.1) | copy-done | bytes 1179672
  18.2 0.6 %shard_map.68 = (f32[160,256]{1,0:T(8,128)S(1)}, f32[1,256]{1,0:T(1,128)S(1)}, bf16[2,576,256]{2,1,0:T(8,128)(2,1)S(1)}) custom-call(bf16[160,576]{1,0:T(8,128)(2,1)S(1)} %get-tuple-element.33.refs_0_, bf16[160,576]{1,0:T(8,128)(2,1)S(1)} %collective-permute-done.refs_1_, bf16[160,576]{1,0:T(8,128)(2,1)S(1)} %collective-permute-done.1.refs_2_, ...), custom_call_target="tpu_custom_call" | custom-call | flops 283115520 | tf_op jit(solution)/shard_map/pallas_call | solution.py:93
  18.8 2.1 %collective-permute-done.7.refs_0_ = bf16[160,576]{1,0:T(8,128)(2,1)S(1)} collective-permute-done((bf16[160,576]{1,0:T(8,128)(2,1)S(1)}, bf16[160,576]{1,0:T(8,128)(2,1)S(1)}, u32[]{:S(2)}, u32[]{:S(2)}) %collective-permute-start.7) | collective-permute-done | bytes 184352 | tf_op jit(solution)/shard_map/ppermute | solution.py:52
  21.3 2.7 %collective-permute-start.10 = (bf16[160,256]{1,0:T(8,128)(2,1)S(1)}, bf16[160,256]{1,0:T(8,128)(2,1)S(1)}, u32[]{:S(2)}, u32[]{:S(2)}) collective-permute-start(bf16[160,256]{1,0:T(8,128)(2,1)S(1)} %shard_map.69.refs_0_), channel_id=1, source_target_pairs={{0,16},{8,24},{16,0},{24,8},{1,17},{9,25},{17,1},{25,9},{2,18},{10... | collective-permute-start | bytes 245768 | tf_op jit(solution)/shard_map/ppermute | solution.py:26
  23.9 1.6 %collective-permute-start.9 = (bf16[160,256]{1,0:T(8,128)(2,1)S(1)}, bf16[160,256]{1,0:T(8,128)(2,1)S(1)}, u32[]{:S(2)}, u32[]{:S(2)}) collective-permute-start(bf16[160,256]{1,0:T(8,128)(2,1)S(1)} %shard_map.69.refs_0_), channel_id=1, source_target_pairs={{0,8},{8,16},{16,24},{24,0},{1,9},{9,17},{17,25},{25,1},{2,10},{10... | collective-permute-start | bytes 245768 | tf_op jit(solution)/shard_map/ppermute | solution.py:26
  25.5 1.7 %collective-permute-done.11 = bf16[160,128]{1,0:T(8,128)(2,1)S(1)} collective-permute-done((bf16[160,128]{1,0:T(8,128)(2,1)S(1)}, bf16[160,128]{1,0:T(8,128)(2,1)S(1)}, u32[]{:S(2)}, u32[]{:S(2)}) %collective-permute-start.11) | collective-permute-done | bytes 40992 | tf_op jit(solution)/shard_map/ppermute | solution.py:52
  27.3 3.3 %collective-permute-done.10.refs_2_ = bf16[160,256]{1,0:T(8,128)(2,1)S(1)} collective-permute-done((bf16[160,256]{1,0:T(8,128)(2,1)S(1)}, bf16[160,256]{1,0:T(8,128)(2,1)S(1)}, u32[]{:S(2)}, u32[]{:S(2)}) %collective-permute-start.10) | collective-permute-done | bytes 81952 | tf_op jit(solution)/shard_map/ppermute | solution.py:26
  30.6 0.6 %shard_map.73 = (bf16[160,576]{1,0:T(8,128)(2,1)S(1)}, bf16[160,576]{1,0:T(8,128)(2,1)S(1)}) custom-call(bf16[160,256]{1,0:T(8,128)(2,1)S(1)} %shard_map.69.refs_0_, bf16[160,256]{1,0:T(8,128)(2,1)S(1)} %collective-permute-done.9.refs_1_, bf16[160,256]{1,0:T(8,128)(2,1)S(1)} %collective-permute-done.10.refs_2_, bf16[3,128,4608]{2,1,0:T(8,128)(2,1)S(1)} %bitcast.13, ...), custom_call_target="tpu_custom_call" | custom-call | tf_op jit(solution)/shard_map/pallas_call | solution.py:131
  31.2 1.6 %collective-permute-start.17 = (bf16[160,576]{1,0:T(8,128)(2,1)S(1)}, bf16[160,576]{1,0:T(8,128)(2,1)S(1)}, u32[]{:S(2)}, u32[]{:S(2)}) collective-permute-start(bf16[160,576]{1,0:T(8,128)(2,1)S(1)} %get-tuple-element.30), channel_id=1, source_target_pairs={{0,4},{1,5},{2,6},{3,7},{4,0},{5,1},{6,2},{7,3},{8,12},{9,13},{10,... | collective-permute-start | bytes 552968 | tf_op jit(solution)/shard_map/ppermute | solution.py:52
  32.8 0.5 %collective-permute-start.14 = (bf16[160,576]{1,0:T(8,128)(2,1)S(1)}, bf16[160,576]{1,0:T(8,128)(2,1)S(1)}, u32[]{:S(2)}, u32[]{:S(2)}) collective-permute-start(bf16[160,576]{1,0:T(8,128)(2,1)S(1)} %get-tuple-element.27), channel_id=1, source_target_pairs={{0,2},{1,3},{2,0},{3,1},{4,6},{5,7},{6,4},{7,5},{8,10},{9,11},{10,... | collective-permute-start | bytes 552968 | tf_op jit(solution)/shard_map/ppermute | solution.py:52
  33.3 0.6 %shard_map.72 = (bf16[160,576]{1,0:T(8,128)(2,1)S(1)}, bf16[160,576]{1,0:T(8,128)(2,1)S(1)}) custom-call(bf16[160,256]{1,0:T(8,128)(2,1)S(1)} %shard_map.69.refs_0_, bf16[160,256]{1,0:T(8,128)(2,1)S(1)} %collective-permute-done.9.refs_1_, bf16[160,256]{1,0:T(8,128)(2,1)S(1)} %collective-permute-done.10.refs_2_, bf16[3,128,4608]{2,1,0:T(8,128)(2,1)S(1)} %bitcast.14, ...), custom_call_target="tpu_custom_call" | custom-call | tf_op jit(solution)/shard_map/pallas_call | solution.py:131
  34.1 0.6 %shard_map.71 = (bf16[160,576]{1,0:T(8,128)(2,1)S(1)}, bf16[160,576]{1,0:T(8,128)(2,1)S(1)}) custom-call(bf16[160,256]{1,0:T(8,128)(2,1)S(1)} %shard_map.69.refs_0_, bf16[160,256]{1,0:T(8,128)(2,1)S(1)} %collective-permute-done.9.refs_1_, bf16[160,256]{1,0:T(8,128)(2,1)S(1)} %collective-permute-done.10.refs_2_, bf16[3,128,4608]{2,1,0:T(8,128)(2,1)S(1)} %bitcast.15, ...), custom_call_target="tpu_custom_call" | custom-call | tf_op jit(solution)/shard_map/pallas_call | solution.py:131
  34.7 1.5 %collective-permute-start.13 = (bf16[160,576]{1,0:T(8,128)(2,1)S(1)}, bf16[160,576]{1,0:T(8,128)(2,1)S(1)}, u32[]{:S(2)}, u32[]{:S(2)}) collective-permute-start(bf16[160,576]{1,0:T(8,128)(2,1)S(1)} %get-tuple-element.25), channel_id=1, source_target_pairs={{0,2},{1,3},{2,0},{3,1},{4,6},{5,7},{6,4},{7,5},{8,10},{9,11},{10,... | collective-permute-start | bytes 552968 | tf_op jit(solution)/shard_map/ppermute | solution.py:52
  36.2 0.6 %shard_map.70 = (bf16[160,576]{1,0:T(8,128)(2,1)S(1)}, bf16[160,576]{1,0:T(8,128)(2,1)S(1)}) custom-call(bf16[160,256]{1,0:T(8,128)(2,1)S(1)} %shard_map.69.refs_0_, bf16[160,256]{1,0:T(8,128)(2,1)S(1)} %collective-permute-done.9.refs_1_, bf16[160,256]{1,0:T(8,128)(2,1)S(1)} %collective-permute-done.10.refs_2_, bf16[3,128,4608]{2,1,0:T(8,128)(2,1)S(1)} %bitcast.16, ...), custom_call_target="tpu_custom_call" | custom-call | tf_op jit(solution)/shard_map/pallas_call | solution.py:131
  37.2 0.6 %collective-permute-done.17.b_ref = bf16[160,576]{1,0:T(8,128)(2,1)S(1)} collective-permute-done((bf16[160,576]{1,0:T(8,128)(2,1)S(1)}, bf16[160,576]{1,0:T(8,128)(2,1)S(1)}, u32[]{:S(2)}, u32[]{:S(2)}) %collective-permute-start.17) | collective-permute-done | bytes 184352 | tf_op jit(solution)/shard_map/ppermute | solution.py:52
  37.9 1.3 %collective-permute-done.14.b_ref = bf16[160,576]{1,0:T(8,128)(2,1)S(1)} collective-permute-done((bf16[160,576]{1,0:T(8,128)(2,1)S(1)}, bf16[160,576]{1,0:T(8,128)(2,1)S(1)}, u32[]{:S(2)}, u32[]{:S(2)}) %collective-permute-start.14) | collective-permute-done | bytes 184352 | tf_op jit(solution)/shard_map/ppermute | solution.py:52
  39.3 1.2 %collective-permute-start.15 = (bf16[160,576]{1,0:T(8,128)(2,1)S(1)}, bf16[160,576]{1,0:T(8,128)(2,1)S(1)}, u32[]{:S(2)}, u32[]{:S(2)}) collective-permute-start(bf16[160,576]{1,0:T(8,128)(2,1)S(1)} %shard_map.74), channel_id=1, source_target_pairs={{0,4},{1,5},{2,6},{3,7},{4,0},{5,1},{6,2},{7,3},{8,12},{9,13},{10,... | collective-permute-start | bytes 552968 | tf_op jit(solution)/shard_map/ppermute | solution.py:52
  40.6 0.6 %maximum_select_fusion = bf16[2,160,128]{2,1,0:T(8,128)(2,1)} fusion(bf16[1,160,128]{2,1,0:T(8,128)(2,1)S(1)} %bitcast.22, bf16[1,160,128]{2,1,0:T(8,128)(2,1)S(1)} %get-tuple-element.34, pred[]{:T(512)S(6)} %eq.5), kind=kLoop, calls=%fused_computation.2 | loop fusion | flops 122880 | bytes 163841 | tf_op jit(solution)/shard_map/jit(_where)/select_n | solution.py:238
  41.5 2.2 %collective-permute-done.13.refs_1_ = bf16[160,576]{1,0:T(8,128)(2,1)S(1)} collective-permute-done((bf16[160,576]{1,0:T(8,128)(2,1)S(1)}, bf16[160,576]{1,0:T(8,128)(2,1)S(1)}, u32[]{:S(2)}, u32[]{:S(2)}) %collective-permute-start.13) | collective-permute-done | bytes 184352 | tf_op jit(solution)/shard_map/ppermute | solution.py:52
  43.7 3.1 %collective-permute-done.18.refs_4_ = bf16[160,576]{1,0:T(8,128)(2,1)S(1)} collective-permute-done((bf16[160,576]{1,0:T(8,128)(2,1)S(1)}, bf16[160,576]{1,0:T(8,128)(2,1)S(1)}, u32[]{:S(2)}, u32[]{:S(2)}) %collective-permute-start.18) | collective-permute-done | bytes 184352 | tf_op jit(solution)/shard_map/ppermute | solution.py:52
  46.7 0.8 %shard_map.76 = bf16[320,576]{1,0:T(8,128)(2,1)} custom-call(bf16[160,576]{1,0:T(8,128)(2,1)S(1)} %get-tuple-element.24.refs_0_, bf16[160,576]{1,0:T(8,128)(2,1)S(1)} %collective-permute-done.13.refs_1_, bf16[160,576]{1,0:T(8,128)(2,1)S(1)} %collective-permute-done.15.refs_2_, bf16[160,576]{1,0:T(8,128)(2,1)S(1)} %collective-permute-done.16.refs_3_, ...), custom_call_target="tpu_custom_call" | custom-call | tf_op jit(solution)/shard_map/pallas_call | solution.py:173
  (26 shorter events, 1.8 us)
Async XLA Ops:
  0.6 13.6 %collective-permute-start.4 = (bf16[4608,128]{1,0:T(8,128)(2,1)}, bf16[4608,128]{1,0:T(8,128)(2,1)S(1)}, u32[]{:S(2)}, u32[]{:S(2)}) collective-permute-start(bf16[4608,128]{1,0:T(8,128)(2,1)} %bitcast.17), channel_id=1, source_target_pairs={{0,1},{1,0},{2,3},{3,2},{4,5},{5,4},{6,7},{7,6},{8,9},{9,8},{10,11... | collective-permute-start | bytes 3538952 | tf_op jit(solution)/shard_map/ppermute | solution.py:52
  2.2 8.5 %collective-permute-start = (bf16[160,576]{1,0:T(8,128)(2,1)S(1)}, bf16[160,576]{1,0:T(8,128)(2,1)S(1)}, u32[]{:S(2)}, u32[]{:S(2)}) collective-permute-start(bf16[160,576]{1,0:T(8,128)(2,1)S(1)} %get-tuple-element.33.refs_0_), channel_id=1, source_target_pairs={{0,2},{1,3},{2,0},{3,1},{4,6},{5,7},{6,4},{7,5},{8,10},{9,11},{10,... | collective-permute-start | bytes 552968 | tf_op jit(solution)/shard_map/ppermute | solution.py:52
  4.8 7.9 %collective-permute-start.3 = (bf16[160,576]{1,0:T(8,128)(2,1)S(1)}, bf16[160,576]{1,0:T(8,128)(2,1)S(1)}, u32[]{:S(2)}, u32[]{:S(2)}) collective-permute-start(bf16[160,576]{1,0:T(8,128)(2,1)S(1)} %get-tuple-element.17), channel_id=1, source_target_pairs={{0,5},{1,4},{2,7},{3,6},{4,1},{5,0},{6,3},{7,2},{8,13},{9,12},{10,... | collective-permute-start | bytes 552968 | tf_op jit(solution)/shard_map/ppermute | solution.py:52
  6.1 9.4 %collective-permute-start.1 = (bf16[160,576]{1,0:T(8,128)(2,1)S(1)}, bf16[160,576]{1,0:T(8,128)(2,1)S(1)}, u32[]{:S(2)}, u32[]{:S(2)}) collective-permute-start(bf16[160,576]{1,0:T(8,128)(2,1)S(1)} %get-tuple-element.17), channel_id=1, source_target_pairs={{0,3},{1,2},{2,1},{3,0},{4,7},{5,6},{6,5},{7,4},{8,11},{9,10},{10,... | collective-permute-start | bytes 552968 | tf_op jit(solution)/shard_map/ppermute | solution.py:52
  6.6 10.3 %collective-permute-start.2 = (bf16[160,576]{1,0:T(8,128)(2,1)S(1)}, bf16[160,576]{1,0:T(8,128)(2,1)S(1)}, u32[]{:S(2)}, u32[]{:S(2)}) collective-permute-start(bf16[160,576]{1,0:T(8,128)(2,1)S(1)} %get-tuple-element.33.refs_0_), channel_id=1, source_target_pairs={{0,4},{1,5},{2,6},{3,7},{4,0},{5,1},{6,2},{7,3},{8,12},{9,13},{10,... | collective-permute-start | bytes 552968 | tf_op jit(solution)/shard_map/ppermute | solution.py:52
  10.7 10.2 %collective-permute-start.7 = (bf16[160,576]{1,0:T(8,128)(2,1)S(1)}, bf16[160,576]{1,0:T(8,128)(2,1)S(1)}, u32[]{:S(2)}, u32[]{:S(2)}) collective-permute-start(bf16[160,576]{1,0:T(8,128)(2,1)S(1)} %collective-permute-done.refs_1_), channel_id=1, source_target_pairs={{0,4},{1,5},{2,6},{3,7},{4,0},{5,1},{6,2},{7,3},{8,12},{9,13},{10,... | collective-permute-start | bytes 552968 | tf_op jit(solution)/shard_map/ppermute | solution.py:52
  12.7 8.2 %collective-permute-start.8 = (bf16[160,576]{1,0:T(8,128)(2,1)S(1)}, bf16[160,576]{1,0:T(8,128)(2,1)S(1)}, u32[]{:S(2)}, u32[]{:S(2)}) collective-permute-start(bf16[160,576]{1,0:T(8,128)(2,1)S(1)} %collective-permute-done.3.refs_4_), channel_id=1, source_target_pairs={{0,2},{1,3},{2,0},{3,1},{4,6},{5,7},{6,4},{7,5},{8,10},{9,11},{10,... | collective-permute-start | bytes 552968 | tf_op jit(solution)/shard_map/ppermute | solution.py:52
  14.2 2.7 %collective-permute-start.5 = (bf16[160,576]{1,0:T(8,128)(2,1)S(1)}, bf16[160,576]{1,0:T(8,128)(2,1)S(1)}, u32[]{:S(2)}, u32[]{:S(2)}) collective-permute-start(bf16[160,576]{1,0:T(8,128)(2,1)S(1)} %get-tuple-element.17), channel_id=1, source_target_pairs={{0,1},{1,0},{2,3},{3,2},{4,5},{5,4},{6,7},{7,6},{8,9},{9,8},{10,11... | collective-permute-start | bytes 552968 | tf_op jit(solution)/shard_map/ppermute | solution.py:52
  15.5 5.4 %copy-start = (bf16[1,3,128,4608]{3,2,1,0:T(8,128)(2,1)S(1)}, bf16[1,3,128,4608]{3,2,1,0:T(8,128)(2,1)}, u32[]{:S(2)}) copy-start(bf16[1,3,128,4608]{3,2,1,0:T(8,128)(2,1)} %param.9) | copy-start | bytes 10616836
  15.5 1.4 %collective-permute-start.6 = (f32[2,128]{1,0:T(2,128)S(1)}, f32[2,128]{1,0:T(2,128)S(1)}, u32[]{:S(2)}, u32[]{:S(2)}) collective-permute-start(f32[2,128]{1,0:T(2,128)S(1)} %pad_maximum_fusion.refs_8_), channel_id=1, source_target_pairs={{0,1},{1,0},{2,3},{3,2},{4,5},{5,4},{6,7},{7,6},{8,9},{9,8},{10,11... | collective-permute-start | bytes 3080 | tf_op jit(solution)/shard_map/ppermute | solution.py:52
  16.9 1.3 %copy-start.1 = (bf16[1,4608,128]{2,1,0:T(8,128)(2,1)S(1)}, bf16[1,4608,128]{2,1,0:T(8,128)(2,1)}, u32[]{:S(2)}) copy-start(bf16[1,4608,128]{2,1,0:T(8,128)(2,1)} %param.6) | copy-start | bytes 3538948
  21.0 9.6 %collective-permute-start.12 = (bf16[3,128,4608]{2,1,0:T(8,128)(2,1)S(1)}, bf16[3,128,4608]{2,1,0:T(8,128)(2,1)S(1)}, u32[]{:S(2)}, u32[]{:S(2)}) collective-permute-start(bf16[3,128,4608]{2,1,0:T(8,128)(2,1)S(1)} %bitcast.12), channel_id=1, source_target_pairs={{0,1},{1,0},{2,3},{3,2},{4,5},{5,4},{6,7},{7,6},{8,9},{9,8},{10,11... | collective-permute-start | bytes 10616840 | tf_op jit(solution)/shard_map/ppermute | solution.py:52
  21.3 9.3 %collective-permute-start.10 = (bf16[160,256]{1,0:T(8,128)(2,1)S(1)}, bf16[160,256]{1,0:T(8,128)(2,1)S(1)}, u32[]{:S(2)}, u32[]{:S(2)}) collective-permute-start(bf16[160,256]{1,0:T(8,128)(2,1)S(1)} %shard_map.69.refs_0_), channel_id=1, source_target_pairs={{0,16},{8,24},{16,0},{24,8},{1,17},{9,25},{17,1},{25,9},{2,18},{10... | collective-permute-start | bytes 245768 | tf_op jit(solution)/shard_map/ppermute | solution.py:26
  23.9 6.7 %collective-permute-start.9 = (bf16[160,256]{1,0:T(8,128)(2,1)S(1)}, bf16[160,256]{1,0:T(8,128)(2,1)S(1)}, u32[]{:S(2)}, u32[]{:S(2)}) collective-permute-start(bf16[160,256]{1,0:T(8,128)(2,1)S(1)} %shard_map.69.refs_0_), channel_id=1, source_target_pairs={{0,8},{8,16},{16,24},{24,0},{1,9},{9,17},{17,25},{25,1},{2,10},{10... | collective-permute-start | bytes 245768 | tf_op jit(solution)/shard_map/ppermute | solution.py:26
  25.5 1.7 %collective-permute-start.11 = (bf16[160,128]{1,0:T(8,128)(2,1)S(1)}, bf16[160,128]{1,0:T(8,128)(2,1)S(1)}, u32[]{:S(2)}, u32[]{:S(2)}) collective-permute-start(bf16[160,128]{1,0:T(8,128)(2,1)S(1)} %get-tuple-element.35), channel_id=1, source_target_pairs={{0,1},{1,0},{2,3},{3,2},{4,5},{5,4},{6,7},{7,6},{8,9},{9,8},{10,11... | collective-permute-start | bytes 122888 | tf_op jit(solution)/shard_map/ppermute | solution.py:52
  31.2 6.6 %collective-permute-start.17 = (bf16[160,576]{1,0:T(8,128)(2,1)S(1)}, bf16[160,576]{1,0:T(8,128)(2,1)S(1)}, u32[]{:S(2)}, u32[]{:S(2)}) collective-permute-start(bf16[160,576]{1,0:T(8,128)(2,1)S(1)} %get-tuple-element.30), channel_id=1, source_target_pairs={{0,4},{1,5},{2,6},{3,7},{4,0},{5,1},{6,2},{7,3},{8,12},{9,13},{10,... | collective-permute-start | bytes 552968 | tf_op jit(solution)/shard_map/ppermute | solution.py:52
  32.8 6.5 %collective-permute-start.14 = (bf16[160,576]{1,0:T(8,128)(2,1)S(1)}, bf16[160,576]{1,0:T(8,128)(2,1)S(1)}, u32[]{:S(2)}, u32[]{:S(2)}) collective-permute-start(bf16[160,576]{1,0:T(8,128)(2,1)S(1)} %get-tuple-element.27), channel_id=1, source_target_pairs={{0,2},{1,3},{2,0},{3,1},{4,6},{5,7},{6,4},{7,5},{8,10},{9,11},{10,... | collective-permute-start | bytes 552968 | tf_op jit(solution)/shard_map/ppermute | solution.py:52
  34.0 7.5 %collective-permute-start.19 = (bf16[160,576]{1,0:T(8,128)(2,1)S(1)}, bf16[160,576]{1,0:T(8,128)(2,1)S(1)}, u32[]{:S(2)}, u32[]{:S(2)}) collective-permute-start(bf16[160,576]{1,0:T(8,128)(2,1)S(1)} %get-tuple-element.31), channel_id=1, source_target_pairs={{0,5},{1,4},{2,7},{3,6},{4,1},{5,0},{6,3},{7,2},{8,13},{9,12},{10,... | collective-permute-start | bytes 552968 | tf_op jit(solution)/shard_map/ppermute | solution.py:52
  34.7 9.0 %collective-permute-start.13 = (bf16[160,576]{1,0:T(8,128)(2,1)S(1)}, bf16[160,576]{1,0:T(8,128)(2,1)S(1)}, u32[]{:S(2)}, u32[]{:S(2)}) collective-permute-start(bf16[160,576]{1,0:T(8,128)(2,1)S(1)} %get-tuple-element.25), channel_id=1, source_target_pairs={{0,2},{1,3},{2,0},{3,1},{4,6},{5,7},{6,4},{7,5},{8,10},{9,11},{10,... | collective-permute-start | bytes 552968 | tf_op jit(solution)/shard_map/ppermute | solution.py:52
  36.9 6.8 %collective-permute-start.16 = (bf16[160,576]{1,0:T(8,128)(2,1)S(1)}, bf16[160,576]{1,0:T(8,128)(2,1)S(1)}, u32[]{:S(2)}, u32[]{:S(2)}) collective-permute-start(bf16[160,576]{1,0:T(8,128)(2,1)S(1)} %get-tuple-element.28), channel_id=1, source_target_pairs={{0,1},{1,0},{2,3},{3,2},{4,5},{5,4},{6,7},{7,6},{8,9},{9,8},{10,11... | collective-permute-start | bytes 552968 | tf_op jit(solution)/shard_map/ppermute | solution.py:52
  37.9 8.9 %collective-permute-start.18 = (bf16[160,576]{1,0:T(8,128)(2,1)S(1)}, bf16[160,576]{1,0:T(8,128)(2,1)S(1)}, u32[]{:S(2)}, u32[]{:S(2)}) collective-permute-start(bf16[160,576]{1,0:T(8,128)(2,1)S(1)} %shard_map.75), channel_id=1, source_target_pairs={{0,3},{1,2},{2,1},{3,0},{4,7},{5,6},{6,5},{7,4},{8,11},{9,10},{10,... | collective-permute-start | bytes 552968 | tf_op jit(solution)/shard_map/ppermute | solution.py:52
  39.3 7.4 %collective-permute-start.15 = (bf16[160,576]{1,0:T(8,128)(2,1)S(1)}, bf16[160,576]{1,0:T(8,128)(2,1)S(1)}, u32[]{:S(2)}, u32[]{:S(2)}) collective-permute-start(bf16[160,576]{1,0:T(8,128)(2,1)S(1)} %shard_map.74), channel_id=1, source_target_pairs={{0,4},{1,5},{2,6},{3,7},{4,0},{5,1},{6,2},{7,3},{8,12},{9,13},{10,... | collective-permute-start | bytes 552968 | tf_op jit(solution)/shard_map/ppermute | solution.py:52

commit v4 on v3

--- a/solution.py
+++ b/solution.py
@@ -9,6 +9,7 @@
 from jax.sharding import PartitionSpec as P
 
 LAYERS = 4
+CHUNKS = (96, 64)
 VMEM_LIMIT = 16 * 1024 * 1024
 
 
@@ -62,7 +63,8 @@
 
 
 def encode_near_kernel(offsets, far_offsets, *refs):
-    *x_refs, own_ref, sib_ref, gates_ref, gates_sib_ref, out_ref, thr_ref, far_ref = refs
+    x_refs = refs[:len(offsets)]
+    own_ref, sib_ref, gates_ref, gates_sib_ref, *out_refs, thr_ref, far_ref = refs[len(offsets):]
     depth = x_refs[0].shape[1]
     place = lax.axis_index("latent")
 
@@ -71,26 +73,29 @@
         return jnp.concatenate([own_ref[rows, :], sib_ref[rows, :]], axis=1)
 
     bias, thr = (jnp.concatenate([gates_ref[i:i + 1, :], gates_sib_ref[i:i + 1, :]], axis=1) for i in (0, 1))
-    total = jnp.broadcast_to(bias, out_ref.shape)
+    total = bias
     for offset, x_ref in zip(offsets, x_refs):
-        total += jnp.dot(x_ref[...], weights(offset), preferred_element_type=jnp.float32)
-    out_ref[...] = total
+        total = total + jnp.dot(x_ref[...], weights(offset), preferred_element_type=jnp.float32)
+    first = 0
+    for out_ref in out_refs:
+        out_ref[...] = total[first:first + out_ref.shape[0]]
+        first += out_ref.shape[0]
     thr_ref[...] = thr
     for index, offset in enumerate(far_offsets):
         far_ref[index] = weights(offset)
 
 
-def encode_near(pieces, far_offsets, own, sib, gates, gates_sib):
+def encode_near(pieces, far_offsets, chunks, own, sib, gates, gates_sib):
     rows, depth = next(iter(pieces.values())).shape
     lat = 2 * own.shape[1]
-    shapes = (
-        jax.ShapeDtypeStruct((rows, lat), jnp.float32),
+    shapes = [jax.ShapeDtypeStruct((chunk, lat), jnp.float32) for chunk in chunks] + [
         jax.ShapeDtypeStruct((1, lat), jnp.float32),
         jax.ShapeDtypeStruct((len(far_offsets), depth, lat), own.dtype),
-    )
+    ]
     cost = pl.CostEstimate(2 * len(pieces) * rows * depth * lat, 4 * own.size, 0)
     kernel = functools.partial(encode_near_kernel, tuple(pieces), far_offsets)
-    return call(kernel, shapes, cost=cost)(*pieces.values(), own, sib, gates, gates_sib)
+    *sums, thr, weights = call(kernel, shapes, cost=cost)(*pieces.values(), own, sib, gates, gates_sib)
+    return sums, thr, weights
 
 
 def encode_kernel(near_ref, thr_ref, weights_ref, *refs):
@@ -102,14 +107,30 @@
 
 
 def encode(near, thr, weights, pieces):
-    return call(encode_kernel, jax.ShapeDtypeStruct(near.shape, jnp.bfloat16))(near, thr, weights, *pieces)
+    cost = pl.CostEstimate(2 * near.shape[0] * weights.size, 2 * weights.size, 0)
+    return call(encode_kernel, jax.ShapeDtypeStruct(near.shape, jnp.bfloat16), cost)(near, thr, weights, *pieces)
+
+
+def split_kernel(whole_ref, *out_refs):
+    first = 0
+    for out_ref in out_refs:
+        out_ref[...] = whole_ref[first:first + out_ref.shape[0], :]
+        first += out_ref.shape[0]
+
+
+def split(whole, chunks):
+    if len(chunks) == 1:
+        return [whole]
+    return call(split_kernel, [jax.ShapeDtypeStruct((rows, whole.shape[1]), whole.dtype) for rows in chunks])(whole)
 
 
 def decoded(acts, own_ref, sib_ref, columns):
     total = None
-    for hop, values in enumerate(by_hop(acts, own_ref.shape[0])):
+    reach = own_ref.shape[0]
+    chunks = [by_hop(acts[first:first + reach], reach) for first in range(0, len(acts), reach)]
+    for hop, values in enumerate(zip(*chunks)):
         weights = jnp.concatenate([own_ref[hop, :, columns], sib_ref[hop, :, columns]], axis=0)
-        part = jnp.dot(values, weights, preferred_element_type=jnp.float32)
+        part = jnp.dot(jnp.concatenate(values, axis=0), weights, preferred_element_type=jnp.float32)
         total = part if total is None else total + part
     return total
 
@@ -127,7 +148,8 @@
 
 
 def decode_chip(chip_offset, acts, own, sib, width):
-    shape = jax.ShapeDtypeStruct((acts[0].shape[0], width), jnp.bfloat16)
+    rows = sum(chunk.shape[0] for chunk in acts[::own.shape[0]])
+    shape = jax.ShapeDtypeStruct((rows, width), jnp.bfloat16)
     return call(functools.partial(decode_chip_kernel, chip_offset), (shape, shape))(*acts, own, sib)
 
 
@@ -180,6 +202,7 @@
 
 
 def gather_and_encode(mine, other, gates, encoder, decoder):
+    rows = mine.shape[0]
     count = lax.axis_size("latent")
     if count != 8:
         core = lax.axis_index("latent") % 2
@@ -188,18 +211,22 @@
         everyone = lax.all_to_all(outgoing, "latent", 0, 0, tiled=True)
         place = lax.axis_index("latent")
         pieces = {i: lax.dynamic_index_in_dim(everyone, place ^ i, 0, keepdims=False) for i in range(count)}
-        near, far = {i: pieces[i] for i in range(count // 2)}, {i: pieces[i] for i in range(count // 2, count)}
+        chunks = (rows,)
+        near, far = {i: pieces[i] for i in range(count // 2)}, {i: [pieces[i]] for i in range(count // 2, count)}
         enc_sib, gates_sib, dec_sib = (to_peer(value, 1) for value in (encoder, gates, decoder))
-        near_sum, *rest = encode_near(near, tuple(far), encoder, enc_sib, gates, gates_sib)
     else:
-        near = {0: mine, 2: to_peer(mine, 2), 3: to_peer(other, 3), 4: to_peer(mine, 4), 5: to_peer(other, 5)}
-        enc_sib = to_peer(encoder, 1)
-        far = {6: to_peer(near[2], 4), 7: to_peer(near[5], 2)}
-        near[1] = to_peer(after(other, enc_sib), 1)
-        gates_sib = to_peer(after(gates, enc_sib), 1)
-        near_sum, *rest = encode_near(near, tuple(far), encoder, enc_sib, gates, gates_sib)
-        dec_sib = to_peer(after(decoder, far[6], far[7], near_sum), 1)
-    return encode(near_sum, *rest, far.values()), dec_sib
+        chunks = CHUNKS
+        near = {0: mine, 1: to_peer(other, 1), 2: to_peer(mine, 2), 5: to_peer(other, 5)}
+        enc_sib, dec_sib = to_peer(encoder, 1), to_peer(decoder, 1)
+        near[3], near[4] = to_peer(after(other, near[1]), 3), to_peer(after(mine, enc_sib), 4)
+        far = {}
+        for place, value, offset in ((6, near[2], 4), (7, near[5], 2)):
+            first, *later = split(value, chunks)
+            later = [after(part, near[3], near[4]) for part in later]
+            far[place] = [to_peer(part, offset) for part in (first, *later)]
+        gates_sib = after(to_peer(after(gates, near[2]), 1), dec_sib)
+    sums, thr, weights = encode_near(near, tuple(far), chunks, encoder, enc_sib, gates, gates_sib)
+    return [encode(part, thr, weights, far_parts) for part, *far_parts in zip(sums, *far.values())], dec_sib
 
 
 def decode_and_scatter(acts, own, sib, width, dtype):
@@ -234,13 +261,14 @@
     threshold = 10000.0 * (gate_code[0].astype(jnp.float32) - 1.0)
     gates_own = jnp.stack([enc_bias[0], threshold])
     acts, dec_sib = gather_and_encode(mine, other, gates_own, encoder[0], decoder[0])
-    kept, passed = acts[:, :lat], to_peer(acts[:, lat:], 1)
+    whole = jnp.concatenate(acts, axis=0)
+    kept, passed = whole[:, :lat], to_peer(whole[:, lat:], 1)
     latent_acts = jnp.where(core == 0, jnp.stack([kept, passed]), jnp.stack([passed, kept])).reshape(tok, lat)
 
-    received = earlier_layers(acts, reach, group_size)
-    received[-1] = after(received[-1], passed)
+    sources = [value for chunk in acts for value in (chunk, *earlier_layers(chunk, reach, group_size))]
+    sources[-1] = after(sources[-1], passed)
     out_type = jnp.bfloat16 if group_size == 1 else jnp.float32
-    summed = decode_and_scatter([acts, *received], decoder[0], dec_sib, width, out_type)
+    summed = decode_and_scatter(sources, decoder[0], dec_sib, width, out_type)
     rebuilt = group_reduce(summed, group_size).astype(jnp.bfloat16)
     return (rebuilt[None], latent_acts[None])
 

time: 47.9 us -> 56.2 us (1.17)
  starting transfers between devices: 18.7 us -> 26.1 us
  waiting for transfers between devices: 19.5 us -> 12.6 us
  Pallas kernels: 4.35 us -> 9.08 us
  local copies, waits for them, and re-layouts: 2.35 us -> 3.94 us
  other arithmetic: 1.97 us -> 3.45 us
    ppermute x18 -> x20, waiting for transfers between devices: 16.2 us -> 8.43 us  [to_peer(): lax.ppermute(value, 'latent', [(i, i ^ offset) for i in range(lax.axis_si...]
    ppermute x18 -> x20, starting transfers between devices: 14.4 us -> 19.9 us  [to_peer(): lax.ppermute(value, 'latent', [(i, i ^ offset) for i in range(lax.axis_si...]
    pallas_call x4, Pallas kernels: 2.51 us -> 4.54 us  [decode_chip(): call(functools.partial(decode_chip_kernel, chip_offset), (shape, shape))]
    ppermute x2 -> x4, starting transfers between devices: 4.23 us -> 6.13 us  [earlier_layers(): lax.ppermute(value, 'section', [(i, (i + shift) % count) for i in range(c...]
    unnamed x4 -> x10, local copies, waits for them, and re-layouts: 1.27 us -> 2.87 us
    pallas_call x1, Pallas kernels: 0.6 us -> 2.04 us  [encode_near(): call(kernel, shapes, cost=cost)]
    pallas_call x1, Pallas kernels: 0.85 us -> 1.89 us  [finish(): pl.pallas_call(finish_kernel, out_shape=jax.ShapeDtypeStruct((2 * rows, w...]
    select_n x1, other arithmetic: 0.65 us -> 1.51 us  [shards(): jnp.where(core == 0, jnp.stack([kept, passed]), jnp.stack([passed, kept]))]
  transfers between devices with their start and end apart: 20 -> 24, of which waited for: 11 -> 9; matrix products, arithmetic and copies ran while one was open for 6% -> 8% of each run, Pallas kernels for 6% -> 12%
where the time goes in v4:
time: 56.2 us; the launch traced here: 55.9 us
  starting transfers between devices  26.1 us (46%)
  waiting for transfers between devices  12.6 us (22%)
  Pallas kernels  9.08 us (16%)
  local copies, waits for them, and re-layouts  3.94 us (7%)
  other arithmetic  3.45 us (6%)
  between operations  0.75 us (1%)
    ppermute x20, starting transfers between devices, to_peer(): lax.ppermute(value, 'latent', [(i, i ^ offset) for i in range(lax.axis_si...  19.9 us
    ppermute x20, waiting for transfers between devices, to_peer(): lax.ppermute(value, 'latent', [(i, i ^ offset) for i in range(lax.axis_si...  8.43 us
    ppermute x4, starting transfers between devices, earlier_layers(): lax.ppermute(value, 'section', [(i, (i + shift) % count) for i in range(c...  6.13 us
    pallas_call x4, Pallas kernels, decode_chip(): call(functools.partial(decode_chip_kernel, chip_offset), (shape, shape))  4.54 us
    ppermute x4, waiting for transfers between devices, earlier_layers(): lax.ppermute(value, 'section', [(i, (i + shift) % count) for i in range(c...  4.14 us
    unnamed x10, local copies, waits for them, and re-layouts  2.87 us
    pallas_call x1, Pallas kernels, encode_near(): call(kernel, shapes, cost=cost)  2.04 us
    pallas_call x1, Pallas kernels, finish(): pl.pallas_call(finish_kernel, out_shape=jax.ShapeDtypeStruct((2 * rows, w...  1.89 us
  transfers between devices with their start and end apart: 24, of which 9 were waited for; matrix products, arithmetic and copies ran while one was open for 8% of the time, Pallas kernels for 12%

profile of v4, /device:TPU:0, one launch (start us, length us, event | category | flops | bytes accessed | tf_op | source)
XLA Modules:
  0.0 55.9 jit_solution(7577334193198226369)
XLA Ops:
  1.2 1.1 %dynamic-slice_bitcast_fusion = (bf16[160,576]{1,0:T(8,128)(2,1)S(1)}, bf16[160,576]{1,0:T(8,128)(2,1)S(1)}) fusion(bf16[8,160,576]{2,1,0:T(8,128)(2,1)} %bitcast.20, s32[]{:T(128)S(6)} %select_n.36, s32[]{:T(128)S(6)} %select_n.35), kind=kLoop, calls=%fused_computation | loop fusion | bytes 737288 | tf_op jit(solution)/shard_map/jit(dynamic_index_in_dim)/squeeze | solution.py:260
  2.8 2.6 %collective-permute-start.2 = (bf16[160,576]{1,0:T(8,128)(2,1)S(1)}, bf16[160,576]{1,0:T(8,128)(2,1)S(1)}, u32[]{:S(2)}, u32[]{:S(2)}) collective-permute-start(bf16[160,576]{1,0:T(8,128)(2,1)S(1)} %get-tuple-element.25), channel_id=1, source_target_pairs={{0,5},{1,4},{2,7},{3,6},{4,1},{5,0},{6,3},{7,2},{8,13},{9,12},{10,... | collective-permute-start | bytes 552968 | tf_op jit(solution)/shard_map/ppermute | solution.py:53
  5.4 1.5 %collective-permute-start.1 = (bf16[160,576]{1,0:T(8,128)(2,1)S(1)}, bf16[160,576]{1,0:T(8,128)(2,1)S(1)}, u32[]{:S(2)}, u32[]{:S(2)}) collective-permute-start(bf16[160,576]{1,0:T(8,128)(2,1)S(1)} %get-tuple-element.26.refs_0_), channel_id=1, source_target_pairs={{0,2},{1,3},{2,0},{3,1},{4,6},{5,7},{6,4},{7,5},{8,10},{9,11},{10,... | collective-permute-start | bytes 552968 | tf_op jit(solution)/shard_map/ppermute | solution.py:53
  6.9 1.1 %collective-permute-done.refs_1_ = bf16[160,576]{1,0:T(8,128)(2,1)S(1)} collective-permute-done((bf16[160,576]{1,0:T(8,128)(2,1)S(1)}, bf16[160,576]{1,0:T(8,128)(2,1)S(1)}, u32[]{:S(2)}, u32[]{:S(2)}) %collective-permute-start) | collective-permute-done | bytes 184352 | tf_op jit(solution)/shard_map/ppermute | solution.py:53
  8.0 2.1 %collective-permute-start.3 = (bf16[160,576]{1,0:T(8,128)(2,1)S(1)}, bf16[160,576]{1,0:T(8,128)(2,1)S(1)}, u32[]{:S(2)}, u32[]{:S(2)}) collective-permute-start(bf16[160,576]{1,0:T(8,128)(2,1)S(1)} %get-tuple-element.25), channel_id=1, source_target_pairs={{0,3},{1,2},{2,1},{3,0},{4,7},{5,6},{6,5},{7,4},{8,11},{9,10},{10,... | collective-permute-start | bytes 552968 | tf_op jit(solution)/shard_map/ppermute | solution.py:53
  10.1 1.8 %collective-permute-start.5 = (bf16[160,576]{1,0:T(8,128)(2,1)S(1)}, bf16[160,576]{1,0:T(8,128)(2,1)S(1)}, u32[]{:S(2)}, u32[]{:S(2)}) collective-permute-start(bf16[160,576]{1,0:T(8,128)(2,1)S(1)} %get-tuple-element.26.refs_0_), channel_id=1, source_target_pairs={{0,4},{1,5},{2,6},{3,7},{4,0},{5,1},{6,2},{7,3},{8,12},{9,13},{10,... | collective-permute-start | bytes 552968 | tf_op jit(solution)/shard_map/ppermute | solution.py:53
  11.9 0.7 %add_multiply_fusion = f32[1,128]{1,0:T(1,128)S(1)} fusion(s32[1,128]{1,0:T(1,128)} %param.8), kind=kLoop, calls=%fused_computation.9 | loop fusion | flops 384 | bytes 1024 | tf_op jit(solution)/shard_map/mul | solution.py:261
  12.5 0.9 %collective-permute-done.1.refs_2_.whole_ref = bf16[160,576]{1,0:T(8,128)(2,1)S(1)} collective-permute-done((bf16[160,576]{1,0:T(8,128)(2,1)S(1)}, bf16[160,576]{1,0:T(8,128)(2,1)S(1)}, u32[]{:S(2)}, u32[]{:S(2)}) %collective-permute-start.1) | collective-permute-done | bytes 184352 | tf_op jit(solution)/shard_map/ppermute | solution.py:53
  13.5 1.5 %collective-permute-start.9 = (bf16[96,576]{1,0:T(8,128)(2,1)S(1)}, bf16[96,576]{1,0:T(8,128)(2,1)S(1)}, u32[]{:S(2)}, u32[]{:S(2)}) collective-permute-start(bf16[96,576]{1,0:T(8,128)(2,1)S(1)} %get-tuple-element.33), channel_id=1, source_target_pairs={{0,2},{1,3},{2,0},{3,1},{4,6},{5,7},{6,4},{7,5},{8,10},{9,11},{10,... | collective-permute-start | bytes 331784 | tf_op jit(solution)/shard_map/ppermute | solution.py:53
  15.0 0.7 %pad_maximum_fusion.1.refs_8_ = f32[2,128]{1,0:T(2,128)S(1)} fusion(f32[1,128]{1,0:T(1,128)S(1)} %add_multiply_fusion, f32[1,128]{1,0:T(1,128)} %param.7), kind=kLoop, calls=%fused_computation.8 | loop fusion | flops 256 | bytes 2048 | tf_op jit(solution)/shard_map/stack | solution.py:262
  15.6 1.0 %collective-permute-done.3.refs_4_ = bf16[160,576]{1,0:T(8,128)(2,1)S(1)} collective-permute-done((bf16[160,576]{1,0:T(8,128)(2,1)S(1)}, bf16[160,576]{1,0:T(8,128)(2,1)S(1)}, u32[]{:S(2)}, u32[]{:S(2)}) %collective-permute-start.3) | collective-permute-done | bytes 184352 | tf_op jit(solution)/shard_map/ppermute | solution.py:53
  16.7 1.2 %collective-permute-start.6 = (f32[2,128]{1,0:T(2,128)S(1)}, f32[2,128]{1,0:T(2,128)S(1)}, u32[]{:S(2)}, u32[]{:S(2)}) collective-permute-start(f32[2,128]{1,0:T(2,128)S(1)} %pad_maximum_fusion.1.refs_8_), channel_id=1, source_target_pairs={{0,1},{1,0},{2,3},{3,2},{4,5},{5,4},{6,7},{7,6},{8,9},{9,8},{10,11... | collective-permute-start | bytes 3080 | tf_op jit(solution)/shard_map/ppermute | solution.py:53
  18.0 1.8 %collective-permute-start.12 = (bf16[64,576]{1,0:T(8,128)(2,1)S(1)}, bf16[64,576]{1,0:T(8,128)(2,1)S(1)}, u32[]{:S(2)}, u32[]{:S(2)}) collective-permute-start(bf16[64,576]{1,0:T(8,128)(2,1)S(1)} %get-tuple-element.36), channel_id=1, source_target_pairs={{0,4},{1,5},{2,6},{3,7},{4,0},{5,1},{6,2},{7,3},{8,12},{9,13},{10,... | collective-permute-start | bytes 221192 | tf_op jit(solution)/shard_map/ppermute | solution.py:53
  19.8 1.5 %collective-permute-start.13 = (bf16[64,576]{1,0:T(8,128)(2,1)S(1)}, bf16[64,576]{1,0:T(8,128)(2,1)S(1)}, u32[]{:S(2)}, u32[]{:S(2)}) collective-permute-start(bf16[64,576]{1,0:T(8,128)(2,1)S(1)} %get-tuple-element.38), channel_id=1, source_target_pairs={{0,2},{1,3},{2,0},{3,1},{4,6},{5,7},{6,4},{7,5},{8,10},{9,11},{10,... | collective-permute-start | bytes 221192 | tf_op jit(solution)/shard_map/ppermute | solution.py:53
  21.3 1.3 %copy-done.3 = bf16[1,4608,128]{2,1,0:T(8,128)(2,1)S(1)} copy-done((bf16[1,4608,128]{2,1,0:T(8,128)(2,1)S(1)}, bf16[1,4608,128]{2,1,0:T(8,128)(2,1)}, u32[]{:S(2)}) %copy-start.3) | copy-done | bytes 1179672
  22.5 2.0 %shard_map.68 = (f32[96,256]{1,0:T(8,128)S(1)}, f32[64,256]{1,0:T(8,128)S(1)}, f32[1,256]{1,0:T(1,128)S(1)}, bf16[2,576,256]{2,1,0:T(8,128)(2,1)S(1)}) custom-call(bf16[160,576]{1,0:T(8,128)(2,1)S(1)} %get-tuple-element.26.refs_0_, bf16[160,576]{1,0:T(8,128)(2,1)S(1)} %collective-permute-done.refs_1_, ...), custom_call_target="tpu_custom_call" | custom-call | flops 283115520 | tf_op jit(solution)/shard_map/pallas_call | solution.py:97
  24.8 1.6 %collective-permute-start.10 = (bf16[96,256]{1,0:T(8,128)(2,1)S(1)}, bf16[96,256]{1,0:T(8,128)(2,1)S(1)}, u32[]{:S(2)}, u32[]{:S(2)}) collective-permute-start(bf16[96,256]{1,0:T(8,128)(2,1)S(1)} %shard_map.71.refs_0_), channel_id=1, source_target_pairs={{0,8},{8,16},{16,24},{24,0},{1,9},{9,17},{17,25},{25,1},{2,10},{10... | collective-permute-start | bytes 147464 | tf_op jit(solution)/shard_map/ppermute | solution.py:27
  26.5 2.6 %collective-permute-start.11 = (bf16[96,256]{1,0:T(8,128)(2,1)S(1)}, bf16[96,256]{1,0:T(8,128)(2,1)S(1)}, u32[]{:S(2)}, u32[]{:S(2)}) collective-permute-start(bf16[96,256]{1,0:T(8,128)(2,1)S(1)} %shard_map.71.refs_0_), channel_id=1, source_target_pairs={{0,16},{8,24},{16,0},{24,8},{1,17},{9,25},{17,1},{25,9},{2,18},{10... | collective-permute-start | bytes 147464 | tf_op jit(solution)/shard_map/ppermute | solution.py:27
  30.3 1.6 %collective-permute-start.14 = (bf16[64,256]{1,0:T(8,128)(2,1)S(1)}, bf16[64,256]{1,0:T(8,128)(2,1)S(1)}, u32[]{:S(2)}, u32[]{:S(2)}) collective-permute-start(bf16[64,256]{1,0:T(8,128)(2,1)S(1)} %shard_map.72.refs_3_), channel_id=1, source_target_pairs={{0,8},{8,16},{16,24},{24,0},{1,9},{9,17},{17,25},{25,1},{2,10},{10... | collective-permute-start | bytes 98312 | tf_op jit(solution)/shard_map/ppermute | solution.py:27
  31.8 3.5 %collective-permute-done.15.refs_5_ = bf16[64,256]{1,0:T(8,128)(2,1)S(1)} collective-permute-done((bf16[64,256]{1,0:T(8,128)(2,1)S(1)}, bf16[64,256]{1,0:T(8,128)(2,1)S(1)}, u32[]{:S(2)}, u32[]{:S(2)}) %collective-permute-start.15) | collective-permute-done | bytes 32800 | tf_op jit(solution)/shard_map/ppermute | solution.py:27
  36.0 0.6 %shard_map.76 = (bf16[160,576]{1,0:T(8,128)(2,1)S(1)}, bf16[160,576]{1,0:T(8,128)(2,1)S(1)}) custom-call(bf16[96,256]{1,0:T(8,128)(2,1)S(1)} %shard_map.71.refs_0_, bf16[96,256]{1,0:T(8,128)(2,1)S(1)} %collective-permute-done.10.refs_1_, bf16[96,256]{1,0:T(8,128)(2,1)S(1)} %collective-permute-done.11.refs_2_, bf16[64,256]{1,0:T(8,128)(2,1)S(1)} %shard_map.72.refs_3_, ...), custom_call_target="tpu_custom_call" | custom-call | tf_op jit(solution)/shard_map/pallas_call | solution.py:153
  37.7 1.3 %shard_map.75 = (bf16[160,576]{1,0:T(8,128)(2,1)S(1)}, bf16[160,576]{1,0:T(8,128)(2,1)}) custom-call(bf16[96,256]{1,0:T(8,128)(2,1)S(1)} %shard_map.71.refs_0_, bf16[96,256]{1,0:T(8,128)(2,1)S(1)} %collective-permute-done.10.refs_1_, bf16[96,256]{1,0:T(8,128)(2,1)S(1)} %collective-permute-done.11.refs_2_, bf16[64,256]{1,0:T(8,128)(2,1)S(1)} %shard_map.72.refs_3_, ...), custom_call_target="tpu_custom_call" | custom-call | tf_op jit(solution)/shard_map/pallas_call | solution.py:153
  39.1 1.3 %shard_map.74 = (bf16[160,576]{1,0:T(8,128)(2,1)}, bf16[160,576]{1,0:T(8,128)(2,1)S(1)}) custom-call(bf16[96,256]{1,0:T(8,128)(2,1)S(1)} %shard_map.71.refs_0_, bf16[96,256]{1,0:T(8,128)(2,1)S(1)} %collective-permute-done.10.refs_1_, bf16[96,256]{1,0:T(8,128)(2,1)S(1)} %collective-permute-done.11.refs_2_, bf16[64,256]{1,0:T(8,128)(2,1)S(1)} %shard_map.72.refs_3_, ...), custom_call_target="tpu_custom_call" | custom-call | tf_op jit(solution)/shard_map/pallas_call | solution.py:153
  40.4 1.5 %collective-permute-start.17 = (bf16[160,576]{1,0:T(8,128)(2,1)}, bf16[160,576]{1,0:T(8,128)(2,1)}, u32[]{:S(2)}, u32[]{:S(2)}) collective-permute-start(bf16[160,576]{1,0:T(8,128)(2,1)} %get-tuple-element.41), channel_id=1, source_target_pairs={{0,2},{1,3},{2,0},{3,1},{4,6},{5,7},{6,4},{7,5},{8,10},{9,11},{10,... | collective-permute-start | bytes 552968 | tf_op jit(solution)/shard_map/ppermute | solution.py:53
  41.9 1.3 %shard_map.73 = (bf16[160,576]{1,0:T(8,128)(2,1)S(1)}, bf16[160,576]{1,0:T(8,128)(2,1)}) custom-call(bf16[96,256]{1,0:T(8,128)(2,1)S(1)} %shard_map.71.refs_0_, bf16[96,256]{1,0:T(8,128)(2,1)S(1)} %collective-permute-done.10.refs_1_, bf16[96,256]{1,0:T(8,128)(2,1)S(1)} %collective-permute-done.11.refs_2_, bf16[64,256]{1,0:T(8,128)(2,1)S(1)} %shard_map.72.refs_3_, ...), custom_call_target="tpu_custom_call" | custom-call | tf_op jit(solution)/shard_map/pallas_call | solution.py:153
  43.2 0.7 %copy-done.1 = bf16[160,576]{1,0:T(8,128)(2,1)} copy-done((bf16[160,576]{1,0:T(8,128)(2,1)}, bf16[160,576]{1,0:T(8,128)(2,1)S(1)}, u32[]{:S(2)}) %copy-start.1) | copy-done | bytes 184344
  43.9 1.3 %collective-permute-start.20 = (bf16[160,576]{1,0:T(8,128)(2,1)}, bf16[160,576]{1,0:T(8,128)(2,1)S(1)}, u32[]{:S(2)}, u32[]{:S(2)}) collective-permute-start(bf16[160,576]{1,0:T(8,128)(2,1)} %get-tuple-element.44), channel_id=1, source_target_pairs={{0,1},{1,0},{2,3},{3,2},{4,5},{5,4},{6,7},{7,6},{8,9},{9,8},{10,11... | collective-permute-start | bytes 552968 | tf_op jit(solution)/shard_map/ppermute | solution.py:53
  45.5 0.7 %collective-permute-start.19 = (bf16[160,576]{1,0:T(8,128)(2,1)S(1)}, bf16[160,576]{1,0:T(8,128)(2,1)S(1)}, u32[]{:S(2)}, u32[]{:S(2)}) collective-permute-start(bf16[160,576]{1,0:T(8,128)(2,1)S(1)} %shard_map.77), channel_id=1, source_target_pairs={{0,4},{1,5},{2,6},{3,7},{4,0},{5,1},{6,2},{7,3},{8,12},{9,13},{10,... | collective-permute-start | bytes 552968 | tf_op jit(solution)/shard_map/ppermute | solution.py:53
  46.2 1.5 %maximum_select_fusion = bf16[2,160,128]{2,1,0:T(8,128)(2,1)} fusion(bf16[1,160,128]{2,1,0:T(8,128)(2,1)} %bitcast.22, bf16[1,160,128]{2,1,0:T(8,128)(2,1)} %get-tuple-element.50, pred[]{:T(512)S(6)} %eq.5), kind=kLoop, calls=%fused_computation.4 | loop fusion | flops 122880 | bytes 163841 | tf_op jit(solution)/shard_map/jit(_where)/select_n | solution.py:266
  48.1 4.8 %collective-permute-done.22.refs_4_ = bf16[160,576]{1,0:T(8,128)(2,1)S(1)} collective-permute-done((bf16[160,576]{1,0:T(8,128)(2,1)S(1)}, bf16[160,576]{1,0:T(8,128)(2,1)S(1)}, u32[]{:S(2)}, u32[]{:S(2)}) %collective-permute-start.22) | collective-permute-done | bytes 184352 | tf_op jit(solution)/shard_map/ppermute | solution.py:53
  53.0 0.9 %copy-done.2 = bf16[160,576]{1,0:T(8,128)(2,1)S(1)} copy-done((bf16[160,576]{1,0:T(8,128)(2,1)S(1)}, bf16[160,576]{1,0:T(8,128)(2,1)}, u32[]{:S(2)}) %copy-start.2) | copy-done | bytes 184344
  54.0 1.9 %shard_map.79 = bf16[320,576]{1,0:T(8,128)(2,1)} custom-call(bf16[160,576]{1,0:T(8,128)(2,1)S(1)} %copy-done.2, bf16[160,576]{1,0:T(8,128)(2,1)} %collective-permute-done.17.refs_1_, bf16[160,576]{1,0:T(8,128)(2,1)S(1)} %collective-permute-done.19.refs_2_, bf16[160,576]{1,0:T(8,128)(2,1)S(1)} %collective-permute-done.20.refs_3_, ...), custom_call_target="tpu_custom_call" | custom-call | tf_op jit(solution)/shard_map/pallas_call | solution.py:195
  (43 shorter events, 5.4 us)
Async XLA Ops:
  0.6 20.6 %collective-permute-start.7 = (bf16[3,128,4608]{2,1,0:T(8,128)(2,1)}, bf16[3,128,4608]{2,1,0:T(8,128)(2,1)S(1)}, u32[]{:S(2)}, u32[]{:S(2)}) collective-permute-start(bf16[3,128,4608]{2,1,0:T(8,128)(2,1)} %bitcast.12), channel_id=1, source_target_pairs={{0,1},{1,0},{2,3},{3,2},{4,5},{5,4},{6,7},{7,6},{8,9},{9,8},{10,11... | collective-permute-start | bytes 10616840 | tf_op jit(solution)/shard_map/ppermute | solution.py:53
  1.1 8.9 %collective-permute-start.4 = (bf16[4608,128]{1,0:T(8,128)(2,1)}, bf16[4608,128]{1,0:T(8,128)(2,1)}, u32[]{:S(2)}, u32[]{:S(2)}) collective-permute-start(bf16[4608,128]{1,0:T(8,128)(2,1)} %bitcast.17), channel_id=1, source_target_pairs={{0,1},{1,0},{2,3},{3,2},{4,5},{5,4},{6,7},{7,6},{8,9},{9,8},{10,11... | collective-permute-start | bytes 3538952 | tf_op jit(solution)/shard_map/ppermute | solution.py:53
  2.3 5.7 %collective-permute-start = (bf16[160,576]{1,0:T(8,128)(2,1)S(1)}, bf16[160,576]{1,0:T(8,128)(2,1)S(1)}, u32[]{:S(2)}, u32[]{:S(2)}) collective-permute-start(bf16[160,576]{1,0:T(8,128)(2,1)S(1)} %get-tuple-element.25), channel_id=1, source_target_pairs={{0,1},{1,0},{2,3},{3,2},{4,5},{5,4},{6,7},{7,6},{8,9},{9,8},{10,11... | collective-permute-start | bytes 552968 | tf_op jit(solution)/shard_map/ppermute | solution.py:53
  2.8 10.7 %collective-permute-start.2 = (bf16[160,576]{1,0:T(8,128)(2,1)S(1)}, bf16[160,576]{1,0:T(8,128)(2,1)S(1)}, u32[]{:S(2)}, u32[]{:S(2)}) collective-permute-start(bf16[160,576]{1,0:T(8,128)(2,1)S(1)} %get-tuple-element.25), channel_id=1, source_target_pairs={{0,5},{1,4},{2,7},{3,6},{4,1},{5,0},{6,3},{7,2},{8,13},{9,12},{10,... | collective-permute-start | bytes 552968 | tf_op jit(solution)/shard_map/ppermute | solution.py:53
  5.4 7.9 %collective-permute-start.1 = (bf16[160,576]{1,0:T(8,128)(2,1)S(1)}, bf16[160,576]{1,0:T(8,128)(2,1)S(1)}, u32[]{:S(2)}, u32[]{:S(2)}) collective-permute-start(bf16[160,576]{1,0:T(8,128)(2,1)S(1)} %get-tuple-element.26.refs_0_), channel_id=1, source_target_pairs={{0,2},{1,3},{2,0},{3,1},{4,6},{5,7},{6,4},{7,5},{8,10},{9,11},{10,... | collective-permute-start | bytes 552968 | tf_op jit(solution)/shard_map/ppermute | solution.py:53
  8.0 8.6 %collective-permute-start.3 = (bf16[160,576]{1,0:T(8,128)(2,1)S(1)}, bf16[160,576]{1,0:T(8,128)(2,1)S(1)}, u32[]{:S(2)}, u32[]{:S(2)}) collective-permute-start(bf16[160,576]{1,0:T(8,128)(2,1)S(1)} %get-tuple-element.25), channel_id=1, source_target_pairs={{0,3},{1,2},{2,1},{3,0},{4,7},{5,6},{6,5},{7,4},{8,11},{9,10},{10,... | collective-permute-start | bytes 552968 | tf_op jit(solution)/shard_map/ppermute | solution.py:53
  10.1 7.9 %collective-permute-start.5 = (bf16[160,576]{1,0:T(8,128)(2,1)S(1)}, bf16[160,576]{1,0:T(8,128)(2,1)S(1)}, u32[]{:S(2)}, u32[]{:S(2)}) collective-permute-start(bf16[160,576]{1,0:T(8,128)(2,1)S(1)} %get-tuple-element.26.refs_0_), channel_id=1, source_target_pairs={{0,4},{1,5},{2,6},{3,7},{4,0},{5,1},{6,2},{7,3},{8,12},{9,13},{10,... | collective-permute-start | bytes 552968 | tf_op jit(solution)/shard_map/ppermute | solution.py:53
  13.4 11.2 %collective-permute-start.8 = (bf16[96,576]{1,0:T(8,128)(2,1)S(1)}, bf16[96,576]{1,0:T(8,128)(2,1)S(1)}, u32[]{:S(2)}, u32[]{:S(2)}) collective-permute-start(bf16[96,576]{1,0:T(8,128)(2,1)S(1)} %get-tuple-element.32), channel_id=1, source_target_pairs={{0,4},{1,5},{2,6},{3,7},{4,0},{5,1},{6,2},{7,3},{8,12},{9,13},{10,... | collective-permute-start | bytes 331784 | tf_op jit(solution)/shard_map/ppermute | solution.py:53
  13.5 11.1 %collective-permute-start.9 = (bf16[96,576]{1,0:T(8,128)(2,1)S(1)}, bf16[96,576]{1,0:T(8,128)(2,1)S(1)}, u32[]{:S(2)}, u32[]{:S(2)}) collective-permute-start(bf16[96,576]{1,0:T(8,128)(2,1)S(1)} %get-tuple-element.33), channel_id=1, source_target_pairs={{0,2},{1,3},{2,0},{3,1},{4,6},{5,7},{6,4},{7,5},{8,10},{9,11},{10,... | collective-permute-start | bytes 331784 | tf_op jit(solution)/shard_map/ppermute | solution.py:53
  16.7 3.1 %collective-permute-start.6 = (f32[2,128]{1,0:T(2,128)S(1)}, f32[2,128]{1,0:T(2,128)S(1)}, u32[]{:S(2)}, u32[]{:S(2)}) collective-permute-start(f32[2,128]{1,0:T(2,128)S(1)} %pad_maximum_fusion.1.refs_8_), channel_id=1, source_target_pairs={{0,1},{1,0},{2,3},{3,2},{4,5},{5,4},{6,7},{7,6},{8,9},{9,8},{10,11... | collective-permute-start | bytes 3080 | tf_op jit(solution)/shard_map/ppermute | solution.py:53
  18.0 11.1 %collective-permute-start.12 = (bf16[64,576]{1,0:T(8,128)(2,1)S(1)}, bf16[64,576]{1,0:T(8,128)(2,1)S(1)}, u32[]{:S(2)}, u32[]{:S(2)}) collective-permute-start(bf16[64,576]{1,0:T(8,128)(2,1)S(1)} %get-tuple-element.36), channel_id=1, source_target_pairs={{0,4},{1,5},{2,6},{3,7},{4,0},{5,1},{6,2},{7,3},{8,12},{9,13},{10,... | collective-permute-start | bytes 221192 | tf_op jit(solution)/shard_map/ppermute | solution.py:53
  19.8 9.3 %collective-permute-start.13 = (bf16[64,576]{1,0:T(8,128)(2,1)S(1)}, bf16[64,576]{1,0:T(8,128)(2,1)S(1)}, u32[]{:S(2)}, u32[]{:S(2)}) collective-permute-start(bf16[64,576]{1,0:T(8,128)(2,1)S(1)} %get-tuple-element.38), channel_id=1, source_target_pairs={{0,2},{1,3},{2,0},{3,1},{4,6},{5,7},{6,4},{7,5},{8,10},{9,11},{10,... | collective-permute-start | bytes 221192 | tf_op jit(solution)/shard_map/ppermute | solution.py:53
  21.2 1.3 %copy-start.3 = (bf16[1,4608,128]{2,1,0:T(8,128)(2,1)S(1)}, bf16[1,4608,128]{2,1,0:T(8,128)(2,1)}, u32[]{:S(2)}) copy-start(bf16[1,4608,128]{2,1,0:T(8,128)(2,1)} %param.6) | copy-start | bytes 3538948
  22.5 13.5 %copy-start = (bf16[1,3,128,4608]{3,2,1,0:T(8,128)(2,1)S(1)}, bf16[1,3,128,4608]{3,2,1,0:T(8,128)(2,1)}, u32[]{:S(2)}) copy-start(bf16[1,3,128,4608]{3,2,1,0:T(8,128)(2,1)} %param.9) | copy-start | bytes 10616836
  24.8 11.1 %collective-permute-start.10 = (bf16[96,256]{1,0:T(8,128)(2,1)S(1)}, bf16[96,256]{1,0:T(8,128)(2,1)S(1)}, u32[]{:S(2)}, u32[]{:S(2)}) collective-permute-start(bf16[96,256]{1,0:T(8,128)(2,1)S(1)} %shard_map.71.refs_0_), channel_id=1, source_target_pairs={{0,8},{8,16},{16,24},{24,0},{1,9},{9,17},{17,25},{25,1},{2,10},{10... | collective-permute-start | bytes 147464 | tf_op jit(solution)/shard_map/ppermute | solution.py:27
  26.5 9.5 %collective-permute-start.11 = (bf16[96,256]{1,0:T(8,128)(2,1)S(1)}, bf16[96,256]{1,0:T(8,128)(2,1)S(1)}, u32[]{:S(2)}, u32[]{:S(2)}) collective-permute-start(bf16[96,256]{1,0:T(8,128)(2,1)S(1)} %shard_map.71.refs_0_), channel_id=1, source_target_pairs={{0,16},{8,24},{16,0},{24,8},{1,17},{9,25},{17,1},{25,9},{2,18},{10... | collective-permute-start | bytes 147464 | tf_op jit(solution)/shard_map/ppermute | solution.py:27
  29.9 5.4 %collective-permute-start.16 = (bf16[160,128]{1,0:T(8,128)(2,1)S(1)}, bf16[160,128]{1,0:T(8,128)(2,1)S(1)}, u32[]{:S(2)}, u32[]{:S(2)}) collective-permute-start(bf16[160,128]{1,0:T(8,128)(2,1)S(1)} %get-tuple-element.51), channel_id=1, source_target_pairs={{0,1},{1,0},{2,3},{3,2},{4,5},{5,4},{6,7},{7,6},{8,9},{9,8},{10,11... | collective-permute-start | bytes 122888 | tf_op jit(solution)/shard_map/ppermute | solution.py:53
  29.9 5.4 %collective-permute-start.15 = (bf16[64,256]{1,0:T(8,128)(2,1)S(1)}, bf16[64,256]{1,0:T(8,128)(2,1)S(1)}, u32[]{:S(2)}, u32[]{:S(2)}) collective-permute-start(bf16[64,256]{1,0:T(8,128)(2,1)S(1)} %shard_map.72.refs_3_), channel_id=1, source_target_pairs={{0,16},{8,24},{16,0},{24,8},{1,17},{9,25},{17,1},{25,9},{2,18},{10... | collective-permute-start | bytes 98312 | tf_op jit(solution)/shard_map/ppermute | solution.py:27
  30.3 5.7 %collective-permute-start.14 = (bf16[64,256]{1,0:T(8,128)(2,1)S(1)}, bf16[64,256]{1,0:T(8,128)(2,1)S(1)}, u32[]{:S(2)}, u32[]{:S(2)}) collective-permute-start(bf16[64,256]{1,0:T(8,128)(2,1)S(1)} %shard_map.72.refs_3_), channel_id=1, source_target_pairs={{0,8},{8,16},{16,24},{24,0},{1,9},{9,17},{17,25},{25,1},{2,10},{10... | collective-permute-start | bytes 98312 | tf_op jit(solution)/shard_map/ppermute | solution.py:27
  35.3 0.6 %copy-start.4 = (bf16[160,128]{1,0:T(8,128)(2,1)}, bf16[160,128]{1,0:T(8,128)(2,1)S(1)}, u32[]{:S(2)}) copy-start(bf16[160,128]{1,0:T(8,128)(2,1)S(1)} %collective-permute-done.16) | copy-start | bytes 122884
  36.6 8.5 %collective-permute-start.21 = (bf16[160,576]{1,0:T(8,128)(2,1)S(1)}, bf16[160,576]{1,0:T(8,128)(2,1)S(1)}, u32[]{:S(2)}, u32[]{:S(2)}) collective-permute-start(bf16[160,576]{1,0:T(8,128)(2,1)S(1)} %get-tuple-element.46), channel_id=1, source_target_pairs={{0,4},{1,5},{2,6},{3,7},{4,0},{5,1},{6,2},{7,3},{8,12},{9,13},{10,... | collective-permute-start | bytes 552968 | tf_op jit(solution)/shard_map/ppermute | solution.py:53
  37.2 8.2 %collective-permute-start.18 = (bf16[160,576]{1,0:T(8,128)(2,1)S(1)}, bf16[160,576]{1,0:T(8,128)(2,1)S(1)}, u32[]{:S(2)}, u32[]{:S(2)}) collective-permute-start(bf16[160,576]{1,0:T(8,128)(2,1)S(1)} %get-tuple-element.43), channel_id=1, source_target_pairs={{0,2},{1,3},{2,0},{3,1},{4,6},{5,7},{6,4},{7,5},{8,10},{9,11},{10,... | collective-permute-start | bytes 552968 | tf_op jit(solution)/shard_map/ppermute | solution.py:53
  39.1 8.7 %collective-permute-start.23 = (bf16[160,576]{1,0:T(8,128)(2,1)}, bf16[160,576]{1,0:T(8,128)(2,1)}, u32[]{:S(2)}, u32[]{:S(2)}) collective-permute-start(bf16[160,576]{1,0:T(8,128)(2,1)} %get-tuple-element.47), channel_id=1, source_target_pairs={{0,5},{1,4},{2,7},{3,6},{4,1},{5,0},{6,3},{7,2},{8,13},{9,12},{10,... | collective-permute-start | bytes 552968 | tf_op jit(solution)/shard_map/ppermute | solution.py:53
  40.4 7.7 %collective-permute-start.17 = (bf16[160,576]{1,0:T(8,128)(2,1)}, bf16[160,576]{1,0:T(8,128)(2,1)}, u32[]{:S(2)}, u32[]{:S(2)}) collective-permute-start(bf16[160,576]{1,0:T(8,128)(2,1)} %get-tuple-element.41), channel_id=1, source_target_pairs={{0,2},{1,3},{2,0},{3,1},{4,6},{5,7},{6,4},{7,5},{8,10},{9,11},{10,... | collective-permute-start | bytes 552968 | tf_op jit(solution)/shard_map/ppermute | solution.py:53
  43.2 0.7 %copy-start.1 = (bf16[160,576]{1,0:T(8,128)(2,1)}, bf16[160,576]{1,0:T(8,128)(2,1)S(1)}, u32[]{:S(2)}) copy-start(bf16[160,576]{1,0:T(8,128)(2,1)S(1)} %get-tuple-element.40.refs_0_) | copy-start | bytes 552964
  43.9 4.3 %collective-permute-start.20 = (bf16[160,576]{1,0:T(8,128)(2,1)}, bf16[160,576]{1,0:T(8,128)(2,1)S(1)}, u32[]{:S(2)}, u32[]{:S(2)}) collective-permute-start(bf16[160,576]{1,0:T(8,128)(2,1)} %get-tuple-element.44), channel_id=1, source_target_pairs={{0,1},{1,0},{2,3},{3,2},{4,5},{5,4},{6,7},{7,6},{8,9},{9,8},{10,11... | collective-permute-start | bytes 552968 | tf_op jit(solution)/shard_map/ppermute | solution.py:53
  45.2 7.7 %collective-permute-start.22 = (bf16[160,576]{1,0:T(8,128)(2,1)S(1)}, bf16[160,576]{1,0:T(8,128)(2,1)S(1)}, u32[]{:S(2)}, u32[]{:S(2)}) collective-permute-start(bf16[160,576]{1,0:T(8,128)(2,1)S(1)} %shard_map.78), channel_id=1, source_target_pairs={{0,3},{1,2},{2,1},{3,0},{4,7},{5,6},{6,5},{7,4},{8,11},{9,10},{10,... | collective-permute-start | bytes 552968 | tf_op jit(solution)/shard_map/ppermute | solution.py:53
  45.5 7.6 %collective-permute-start.19 = (bf16[160,576]{1,0:T(8,128)(2,1)S(1)}, bf16[160,576]{1,0:T(8,128)(2,1)S(1)}, u32[]{:S(2)}, u32[]{:S(2)}) collective-permute-start(bf16[160,576]{1,0:T(8,128)(2,1)S(1)} %shard_map.77), channel_id=1, source_target_pairs={{0,4},{1,5},{2,6},{3,7},{4,0},{5,1},{6,2},{7,3},{8,12},{9,13},{10,... | collective-permute-start | bytes 552968 | tf_op jit(solution)/shard_map/ppermute | solution.py:53
  53.0 0.9 %copy-start.2 = (bf16[160,576]{1,0:T(8,128)(2,1)S(1)}, bf16[160,576]{1,0:T(8,128)(2,1)}, u32[]{:S(2)}) copy-start(bf16[160,576]{1,0:T(8,128)(2,1)} %copy-done.1) | copy-start | bytes 552964

commit v5 on v3

--- a/solution.py
+++ b/solution.py
@@ -238,7 +238,7 @@
     latent_acts = jnp.where(core == 0, jnp.stack([kept, passed]), jnp.stack([passed, kept])).reshape(tok, lat)
 
     received = earlier_layers(acts, reach, group_size)
-    received[-1] = after(received[-1], passed)
+    received[0] = after(received[0], passed)
     out_type = jnp.bfloat16 if group_size == 1 else jnp.float32
     summed = decode_and_scatter([acts, *received], decoder[0], dec_sib, width, out_type)
     rebuilt = group_reduce(summed, group_size).astype(jnp.bfloat16)

time: 47.9 us -> 49.7 us (1.038)
  waiting for transfers between devices: 19.5 us -> 21.9 us
  starting transfers between devices: 18.7 us -> 17.6 us
    ppermute x18, waiting for transfers between devices: 16.2 us -> 17.6 us  [to_peer(): lax.ppermute(value, 'latent', [(i, i ^ offset) for i in range(lax.axis_si...]
    ppermute x18, starting transfers between devices: 14.4 us -> 13.4 us  [to_peer(): lax.ppermute(value, 'latent', [(i, i ^ offset) for i in range(lax.axis_si...]
    ppermute x2, waiting for transfers between devices: 3.34 us -> 4.29 us  [earlier_layers(): lax.ppermute(value, 'section', [(i, (i + shift) % count) for i in range(c...]
  transfers between devices with their start and end apart: 20 -> 20, of which waited for: 11 -> 12; matrix products, arithmetic and copies ran while one was open for 6% -> 6% of each run, Pallas kernels for 6% -> 6%
where the time goes in v5:
time: 49.7 us; the launch traced here: 48.9 us
  waiting for transfers between devices  21.9 us (44%)
  starting transfers between devices  17.6 us (35%)
  Pallas kernels  4.35 us (9%)
  local copies, waits for them, and re-layouts  2.35 us (5%)
  other arithmetic  1.97 us (4%)
  between operations  0.72 us (1%)
    ppermute x18, waiting for transfers between devices, to_peer(): lax.ppermute(value, 'latent', [(i, i ^ offset) for i in range(lax.axis_si...  17.6 us
    ppermute x18, starting transfers between devices, to_peer(): lax.ppermute(value, 'latent', [(i, i ^ offset) for i in range(lax.axis_si...  13.4 us
    ppermute x2, waiting for transfers between devices, earlier_layers(): lax.ppermute(value, 'section', [(i, (i + shift) % count) for i in range(c...  4.29 us
    ppermute x2, starting transfers between devices, earlier_layers(): lax.ppermute(value, 'section', [(i, (i + shift) % count) for i in range(c...  4.22 us
    pallas_call x4, Pallas kernels, decode_chip(): call(functools.partial(decode_chip_kernel, chip_offset), (shape, shape))  2.51 us
    unnamed x4, local copies, waits for them, and re-layouts  1.27 us
    squeeze x1, local copies, waits for them, and re-layouts, shards(): lax.dynamic_index_in_dim(halves, place + half, 0, keepdims=False)  1.06 us
  transfers between devices with their start and end apart: 20, of which 12 were waited for; matrix products, arithmetic and copies ran while one was open for 6% of the time, Pallas kernels for 6%

profile of v5, /device:TPU:0, one launch (start us, length us, event | category | flops | bytes accessed | tf_op | source)
XLA Modules:
  0.0 48.9 jit_solution(9971835729042305276)
XLA Ops:
  0.6 0.5 %collective-permute-start.4 = (bf16[4608,128]{1,0:T(8,128)(2,1)}, bf16[4608,128]{1,0:T(8,128)(2,1)S(1)}, u32[]{:S(2)}, u32[]{:S(2)}) collective-permute-start(bf16[4608,128]{1,0:T(8,128)(2,1)} %bitcast.17), channel_id=1, source_target_pairs={{0,1},{1,0},{2,3},{3,2},{4,5},{5,4},{6,7},{7,6},{8,9},{9,8},{10,11... | collective-permute-start | bytes 3538952 | tf_op jit(solution)/shard_map/ppermute | solution.py:52
  1.1 1.1 %dynamic-slice_bitcast_fusion = (bf16[160,576]{1,0:T(8,128)(2,1)S(1)}, bf16[160,576]{1,0:T(8,128)(2,1)S(1)}) fusion(bf16[8,160,576]{2,1,0:T(8,128)(2,1)} %bitcast.20, s32[]{:T(128)S(6)} %select_n.36, s32[]{:T(128)S(6)} %select_n.35), kind=kLoop, calls=%fused_computation | loop fusion | bytes 737288 | tf_op jit(solution)/shard_map/jit(dynamic_index_in_dim)/squeeze | solution.py:233
  2.2 2.6 %collective-permute-start = (bf16[160,576]{1,0:T(8,128)(2,1)S(1)}, bf16[160,576]{1,0:T(8,128)(2,1)S(1)}, u32[]{:S(2)}, u32[]{:S(2)}) collective-permute-start(bf16[160,576]{1,0:T(8,128)(2,1)S(1)} %get-tuple-element.33.refs_0_), channel_id=1, source_target_pairs={{0,2},{1,3},{2,0},{3,1},{4,6},{5,7},{6,4},{7,5},{8,10},{9,11},{10,... | collective-permute-start | bytes 552968 | tf_op jit(solution)/shard_map/ppermute | solution.py:52
  4.8 1.3 %collective-permute-start.3 = (bf16[160,576]{1,0:T(8,128)(2,1)S(1)}, bf16[160,576]{1,0:T(8,128)(2,1)S(1)}, u32[]{:S(2)}, u32[]{:S(2)}) collective-permute-start(bf16[160,576]{1,0:T(8,128)(2,1)S(1)} %get-tuple-element.17), channel_id=1, source_target_pairs={{0,5},{1,4},{2,7},{3,6},{4,1},{5,0},{6,3},{7,2},{8,13},{9,12},{10,... | collective-permute-start | bytes 552968 | tf_op jit(solution)/shard_map/ppermute | solution.py:52
  6.7 4.1 %collective-permute-done.refs_1_ = bf16[160,576]{1,0:T(8,128)(2,1)S(1)} collective-permute-done((bf16[160,576]{1,0:T(8,128)(2,1)S(1)}, bf16[160,576]{1,0:T(8,128)(2,1)S(1)}, u32[]{:S(2)}, u32[]{:S(2)}) %collective-permute-start) | collective-permute-done | bytes 184352 | tf_op jit(solution)/shard_map/ppermute | solution.py:52
  10.7 2.0 %collective-permute-start.7 = (bf16[160,576]{1,0:T(8,128)(2,1)S(1)}, bf16[160,576]{1,0:T(8,128)(2,1)S(1)}, u32[]{:S(2)}, u32[]{:S(2)}) collective-permute-start(bf16[160,576]{1,0:T(8,128)(2,1)S(1)} %collective-permute-done.refs_1_), channel_id=1, source_target_pairs={{0,4},{1,5},{2,6},{3,7},{4,0},{5,1},{6,2},{7,3},{8,12},{9,13},{10,... | collective-permute-start | bytes 552968 | tf_op jit(solution)/shard_map/ppermute | solution.py:52
  12.7 1.5 %collective-permute-start.8 = (bf16[160,576]{1,0:T(8,128)(2,1)S(1)}, bf16[160,576]{1,0:T(8,128)(2,1)S(1)}, u32[]{:S(2)}, u32[]{:S(2)}) collective-permute-start(bf16[160,576]{1,0:T(8,128)(2,1)S(1)} %collective-permute-done.3.refs_4_), channel_id=1, source_target_pairs={{0,2},{1,3},{2,0},{3,1},{4,6},{5,7},{6,4},{7,5},{8,10},{9,11},{10,... | collective-permute-start | bytes 552968 | tf_op jit(solution)/shard_map/ppermute | solution.py:52
  14.2 0.7 %add_multiply_fusion = f32[1,128]{1,0:T(1,128)S(1)} fusion(s32[1,128]{1,0:T(1,128)} %param.8), kind=kLoop, calls=%fused_computation.5 | loop fusion | flops 384 | bytes 1024 | tf_op jit(solution)/shard_map/mul | solution.py:234
  14.9 0.7 %pad_maximum_fusion.refs_8_ = f32[2,128]{1,0:T(2,128)S(1)} fusion(f32[1,128]{1,0:T(1,128)S(1)} %add_multiply_fusion, f32[1,128]{1,0:T(1,128)} %param.7), kind=kLoop, calls=%fused_computation.4 | loop fusion | flops 256 | bytes 2048 | tf_op jit(solution)/shard_map/stack | solution.py:235
  15.5 0.6 %collective-permute-start.6 = (f32[2,128]{1,0:T(2,128)S(1)}, f32[2,128]{1,0:T(2,128)S(1)}, u32[]{:S(2)}, u32[]{:S(2)}) collective-permute-start(f32[2,128]{1,0:T(2,128)S(1)} %pad_maximum_fusion.refs_8_), channel_id=1, source_target_pairs={{0,1},{1,0},{2,3},{3,2},{4,5},{5,4},{6,7},{7,6},{8,9},{9,8},{10,11... | collective-permute-start | bytes 3080 | tf_op jit(solution)/shard_map/ppermute | solution.py:52
  16.1 0.7 %collective-permute-done.2.refs_3_ = bf16[160,576]{1,0:T(8,128)(2,1)S(1)} collective-permute-done((bf16[160,576]{1,0:T(8,128)(2,1)S(1)}, bf16[160,576]{1,0:T(8,128)(2,1)S(1)}, u32[]{:S(2)}, u32[]{:S(2)}) %collective-permute-start.2) | collective-permute-done | bytes 184352 | tf_op jit(solution)/shard_map/ppermute | solution.py:52
  16.9 1.3 %copy-done.1 = bf16[1,4608,128]{2,1,0:T(8,128)(2,1)S(1)} copy-done((bf16[1,4608,128]{2,1,0:T(8,128)(2,1)S(1)}, bf16[1,4608,128]{2,1,0:T(8,128)(2,1)}, u32[]{:S(2)}) %copy-start.1) | copy-done | bytes 1179672
  18.2 0.6 %shard_map.68 = (f32[160,256]{1,0:T(8,128)S(1)}, f32[1,256]{1,0:T(1,128)S(1)}, bf16[2,576,256]{2,1,0:T(8,128)(2,1)S(1)}) custom-call(bf16[160,576]{1,0:T(8,128)(2,1)S(1)} %get-tuple-element.33.refs_0_, bf16[160,576]{1,0:T(8,128)(2,1)S(1)} %collective-permute-done.refs_1_, bf16[160,576]{1,0:T(8,128)(2,1)S(1)} %collective-permute-done.1.refs_2_, ...), custom_call_target="tpu_custom_call" | custom-call | flops 283115520 | tf_op jit(solution)/shard_map/pallas_call | solution.py:93
  18.8 2.1 %collective-permute-done.7.refs_0_ = bf16[160,576]{1,0:T(8,128)(2,1)S(1)} collective-permute-done((bf16[160,576]{1,0:T(8,128)(2,1)S(1)}, bf16[160,576]{1,0:T(8,128)(2,1)S(1)}, u32[]{:S(2)}, u32[]{:S(2)}) %collective-permute-start.7) | collective-permute-done | bytes 184352 | tf_op jit(solution)/shard_map/ppermute | solution.py:52
  21.3 1.6 %collective-permute-start.9 = (bf16[160,256]{1,0:T(8,128)(2,1)S(1)}, bf16[160,256]{1,0:T(8,128)(2,1)S(1)}, u32[]{:S(2)}, u32[]{:S(2)}) collective-permute-start(bf16[160,256]{1,0:T(8,128)(2,1)S(1)} %shard_map.69.refs_0_), channel_id=1, source_target_pairs={{0,8},{8,16},{16,24},{24,0},{1,9},{9,17},{17,25},{25,1},{2,10},{10... | collective-permute-start | bytes 245768 | tf_op jit(solution)/shard_map/ppermute | solution.py:26
  22.9 2.6 %collective-permute-start.11 = (bf16[160,256]{1,0:T(8,128)(2,1)S(1)}, bf16[160,256]{1,0:T(8,128)(2,1)S(1)}, u32[]{:S(2)}, u32[]{:S(2)}) collective-permute-start(bf16[160,256]{1,0:T(8,128)(2,1)S(1)} %shard_map.69.refs_0_), channel_id=1, source_target_pairs={{0,16},{8,24},{16,0},{24,8},{1,17},{9,25},{17,1},{25,9},{2,18},{10... | collective-permute-start | bytes 245768 | tf_op jit(solution)/shard_map/ppermute | solution.py:26
  25.5 1.7 %collective-permute-done.10 = bf16[160,128]{1,0:T(8,128)(2,1)S(1)} collective-permute-done((bf16[160,128]{1,0:T(8,128)(2,1)S(1)}, bf16[160,128]{1,0:T(8,128)(2,1)S(1)}, u32[]{:S(2)}, u32[]{:S(2)}) %collective-permute-start.10) | collective-permute-done | bytes 40992 | tf_op jit(solution)/shard_map/ppermute | solution.py:52
  27.3 1.2 %collective-permute-done.9.refs_1_ = bf16[160,256]{1,0:T(8,128)(2,1)S(1)} collective-permute-done((bf16[160,256]{1,0:T(8,128)(2,1)S(1)}, bf16[160,256]{1,0:T(8,128)(2,1)S(1)}, u32[]{:S(2)}, u32[]{:S(2)}) %collective-permute-start.9) | collective-permute-done | bytes 81952 | tf_op jit(solution)/shard_map/ppermute | solution.py:26
  28.4 3.1 %collective-permute-done.11.refs_2_ = bf16[160,256]{1,0:T(8,128)(2,1)S(1)} collective-permute-done((bf16[160,256]{1,0:T(8,128)(2,1)S(1)}, bf16[160,256]{1,0:T(8,128)(2,1)S(1)}, u32[]{:S(2)}, u32[]{:S(2)}) %collective-permute-start.11) | collective-permute-done | bytes 81952 | tf_op jit(solution)/shard_map/ppermute | solution.py:26
  31.5 0.6 %shard_map.73 = (bf16[160,576]{1,0:T(8,128)(2,1)S(1)}, bf16[160,576]{1,0:T(8,128)(2,1)S(1)}) custom-call(bf16[160,256]{1,0:T(8,128)(2,1)S(1)} %shard_map.69.refs_0_, bf16[160,256]{1,0:T(8,128)(2,1)S(1)} %collective-permute-done.9.refs_1_, bf16[160,256]{1,0:T(8,128)(2,1)S(1)} %collective-permute-done.11.refs_2_, bf16[3,128,4608]{2,1,0:T(8,128)(2,1)S(1)} %bitcast.13, ...), custom_call_target="tpu_custom_call" | custom-call | tf_op jit(solution)/shard_map/pallas_call | solution.py:131
  32.2 1.6 %collective-permute-start.17 = (bf16[160,576]{1,0:T(8,128)(2,1)S(1)}, bf16[160,576]{1,0:T(8,128)(2,1)S(1)}, u32[]{:S(2)}, u32[]{:S(2)}) collective-permute-start(bf16[160,576]{1,0:T(8,128)(2,1)S(1)} %get-tuple-element.30), channel_id=1, source_target_pairs={{0,4},{1,5},{2,6},{3,7},{4,0},{5,1},{6,2},{7,3},{8,12},{9,13},{10,... | collective-permute-start | bytes 552968 | tf_op jit(solution)/shard_map/ppermute | solution.py:52
  33.8 0.5 %collective-permute-start.14 = (bf16[160,576]{1,0:T(8,128)(2,1)S(1)}, bf16[160,576]{1,0:T(8,128)(2,1)S(1)}, u32[]{:S(2)}, u32[]{:S(2)}) collective-permute-start(bf16[160,576]{1,0:T(8,128)(2,1)S(1)} %get-tuple-element.27), channel_id=1, source_target_pairs={{0,2},{1,3},{2,0},{3,1},{4,6},{5,7},{6,4},{7,5},{8,10},{9,11},{10,... | collective-permute-start | bytes 552968 | tf_op jit(solution)/shard_map/ppermute | solution.py:52
  34.3 0.6 %shard_map.72 = (bf16[160,576]{1,0:T(8,128)(2,1)S(1)}, bf16[160,576]{1,0:T(8,128)(2,1)S(1)}) custom-call(bf16[160,256]{1,0:T(8,128)(2,1)S(1)} %shard_map.69.refs_0_, bf16[160,256]{1,0:T(8,128)(2,1)S(1)} %collective-permute-done.9.refs_1_, bf16[160,256]{1,0:T(8,128)(2,1)S(1)} %collective-permute-done.11.refs_2_, bf16[3,128,4608]{2,1,0:T(8,128)(2,1)S(1)} %bitcast.14, ...), custom_call_target="tpu_custom_call" | custom-call | tf_op jit(solution)/shard_map/pallas_call | solution.py:131
  35.0 0.6 %shard_map.71 = (bf16[160,576]{1,0:T(8,128)(2,1)S(1)}, bf16[160,576]{1,0:T(8,128)(2,1)S(1)}) custom-call(bf16[160,256]{1,0:T(8,128)(2,1)S(1)} %shard_map.69.refs_0_, bf16[160,256]{1,0:T(8,128)(2,1)S(1)} %collective-permute-done.9.refs_1_, bf16[160,256]{1,0:T(8,128)(2,1)S(1)} %collective-permute-done.11.refs_2_, bf16[3,128,4608]{2,1,0:T(8,128)(2,1)S(1)} %bitcast.15, ...), custom_call_target="tpu_custom_call" | custom-call | tf_op jit(solution)/shard_map/pallas_call | solution.py:131
  35.6 1.6 %collective-permute-start.13 = (bf16[160,576]{1,0:T(8,128)(2,1)S(1)}, bf16[160,576]{1,0:T(8,128)(2,1)S(1)}, u32[]{:S(2)}, u32[]{:S(2)}) collective-permute-start(bf16[160,576]{1,0:T(8,128)(2,1)S(1)} %get-tuple-element.25), channel_id=1, source_target_pairs={{0,2},{1,3},{2,0},{3,1},{4,6},{5,7},{6,4},{7,5},{8,10},{9,11},{10,... | collective-permute-start | bytes 552968 | tf_op jit(solution)/shard_map/ppermute | solution.py:52
  37.2 0.6 %shard_map.70 = (bf16[160,576]{1,0:T(8,128)(2,1)S(1)}, bf16[160,576]{1,0:T(8,128)(2,1)S(1)}) custom-call(bf16[160,256]{1,0:T(8,128)(2,1)S(1)} %shard_map.69.refs_0_, bf16[160,256]{1,0:T(8,128)(2,1)S(1)} %collective-permute-done.9.refs_1_, bf16[160,256]{1,0:T(8,128)(2,1)S(1)} %collective-permute-done.11.refs_2_, bf16[3,128,4608]{2,1,0:T(8,128)(2,1)S(1)} %bitcast.16, ...), custom_call_target="tpu_custom_call" | custom-call | tf_op jit(solution)/shard_map/pallas_call | solution.py:131
  38.2 2.0 %collective-permute-done.17.b_ref = bf16[160,576]{1,0:T(8,128)(2,1)S(1)} collective-permute-done((bf16[160,576]{1,0:T(8,128)(2,1)S(1)}, bf16[160,576]{1,0:T(8,128)(2,1)S(1)}, u32[]{:S(2)}, u32[]{:S(2)}) %collective-permute-start.17) | collective-permute-done | bytes 184352 | tf_op jit(solution)/shard_map/ppermute | solution.py:52
  40.3 1.4 %collective-permute-done.14.b_ref = bf16[160,576]{1,0:T(8,128)(2,1)S(1)} collective-permute-done((bf16[160,576]{1,0:T(8,128)(2,1)S(1)}, bf16[160,576]{1,0:T(8,128)(2,1)S(1)}, u32[]{:S(2)}, u32[]{:S(2)}) %collective-permute-start.14) | collective-permute-done | bytes 184352 | tf_op jit(solution)/shard_map/ppermute | solution.py:52
  42.0 0.6 %maximum_select_fusion = bf16[2,160,128]{2,1,0:T(8,128)(2,1)} fusion(bf16[1,160,128]{2,1,0:T(8,128)(2,1)S(1)} %bitcast.22, bf16[1,160,128]{2,1,0:T(8,128)(2,1)S(1)} %get-tuple-element.34, pred[]{:T(512)S(6)} %eq.5), kind=kLoop, calls=%fused_computation.2 | loop fusion | flops 122880 | bytes 163841 | tf_op jit(solution)/shard_map/jit(_where)/select_n | solution.py:238
  42.7 3.4 %collective-permute-done.13.refs_1_ = bf16[160,576]{1,0:T(8,128)(2,1)S(1)} collective-permute-done((bf16[160,576]{1,0:T(8,128)(2,1)S(1)}, bf16[160,576]{1,0:T(8,128)(2,1)S(1)}, u32[]{:S(2)}, u32[]{:S(2)}) %collective-permute-start.13) | collective-permute-done | bytes 184352 | tf_op jit(solution)/shard_map/ppermute | solution.py:52
  46.1 1.9 %collective-permute-done.18.refs_4_ = bf16[160,576]{1,0:T(8,128)(2,1)S(1)} collective-permute-done((bf16[160,576]{1,0:T(8,128)(2,1)S(1)}, bf16[160,576]{1,0:T(8,128)(2,1)S(1)}, u32[]{:S(2)}, u32[]{:S(2)}) %collective-permute-start.18) | collective-permute-done | bytes 184352 | tf_op jit(solution)/shard_map/ppermute | solution.py:52
  48.1 0.8 %shard_map.76 = bf16[320,576]{1,0:T(8,128)(2,1)} custom-call(bf16[160,576]{1,0:T(8,128)(2,1)S(1)} %get-tuple-element.24.refs_0_, bf16[160,576]{1,0:T(8,128)(2,1)S(1)} %collective-permute-done.13.refs_1_, bf16[160,576]{1,0:T(8,128)(2,1)S(1)} %collective-permute-done.15.refs_2_, bf16[160,576]{1,0:T(8,128)(2,1)S(1)} %collective-permute-done.16.refs_3_, ...), custom_call_target="tpu_custom_call" | custom-call | tf_op jit(solution)/shard_map/pallas_call | solution.py:173
  (26 shorter events, 1.9 us)
Async XLA Ops:
  0.6 13.6 %collective-permute-start.4 = (bf16[4608,128]{1,0:T(8,128)(2,1)}, bf16[4608,128]{1,0:T(8,128)(2,1)S(1)}, u32[]{:S(2)}, u32[]{:S(2)}) collective-permute-start(bf16[4608,128]{1,0:T(8,128)(2,1)} %bitcast.17), channel_id=1, source_target_pairs={{0,1},{1,0},{2,3},{3,2},{4,5},{5,4},{6,7},{7,6},{8,9},{9,8},{10,11... | collective-permute-start | bytes 3538952 | tf_op jit(solution)/shard_map/ppermute | solution.py:52
  2.2 8.5 %collective-permute-start = (bf16[160,576]{1,0:T(8,128)(2,1)S(1)}, bf16[160,576]{1,0:T(8,128)(2,1)S(1)}, u32[]{:S(2)}, u32[]{:S(2)}) collective-permute-start(bf16[160,576]{1,0:T(8,128)(2,1)S(1)} %get-tuple-element.33.refs_0_), channel_id=1, source_target_pairs={{0,2},{1,3},{2,0},{3,1},{4,6},{5,7},{6,4},{7,5},{8,10},{9,11},{10,... | collective-permute-start | bytes 552968 | tf_op jit(solution)/shard_map/ppermute | solution.py:52
  4.8 7.9 %collective-permute-start.3 = (bf16[160,576]{1,0:T(8,128)(2,1)S(1)}, bf16[160,576]{1,0:T(8,128)(2,1)S(1)}, u32[]{:S(2)}, u32[]{:S(2)}) collective-permute-start(bf16[160,576]{1,0:T(8,128)(2,1)S(1)} %get-tuple-element.17), channel_id=1, source_target_pairs={{0,5},{1,4},{2,7},{3,6},{4,1},{5,0},{6,3},{7,2},{8,13},{9,12},{10,... | collective-permute-start | bytes 552968 | tf_op jit(solution)/shard_map/ppermute | solution.py:52
  6.1 9.4 %collective-permute-start.1 = (bf16[160,576]{1,0:T(8,128)(2,1)S(1)}, bf16[160,576]{1,0:T(8,128)(2,1)S(1)}, u32[]{:S(2)}, u32[]{:S(2)}) collective-permute-start(bf16[160,576]{1,0:T(8,128)(2,1)S(1)} %get-tuple-element.17), channel_id=1, source_target_pairs={{0,3},{1,2},{2,1},{3,0},{4,7},{5,6},{6,5},{7,4},{8,11},{9,10},{10,... | collective-permute-start | bytes 552968 | tf_op jit(solution)/shard_map/ppermute | solution.py:52
  6.6 10.3 %collective-permute-start.2 = (bf16[160,576]{1,0:T(8,128)(2,1)S(1)}, bf16[160,576]{1,0:T(8,128)(2,1)S(1)}, u32[]{:S(2)}, u32[]{:S(2)}) collective-permute-start(bf16[160,576]{1,0:T(8,128)(2,1)S(1)} %get-tuple-element.33.refs_0_), channel_id=1, source_target_pairs={{0,4},{1,5},{2,6},{3,7},{4,0},{5,1},{6,2},{7,3},{8,12},{9,13},{10,... | collective-permute-start | bytes 552968 | tf_op jit(solution)/shard_map/ppermute | solution.py:52
  10.7 10.2 %collective-permute-start.7 = (bf16[160,576]{1,0:T(8,128)(2,1)S(1)}, bf16[160,576]{1,0:T(8,128)(2,1)S(1)}, u32[]{:S(2)}, u32[]{:S(2)}) collective-permute-start(bf16[160,576]{1,0:T(8,128)(2,1)S(1)} %collective-permute-done.refs_1_), channel_id=1, source_target_pairs={{0,4},{1,5},{2,6},{3,7},{4,0},{5,1},{6,2},{7,3},{8,12},{9,13},{10,... | collective-permute-start | bytes 552968 | tf_op jit(solution)/shard_map/ppermute | solution.py:52
  12.7 8.2 %collective-permute-start.8 = (bf16[160,576]{1,0:T(8,128)(2,1)S(1)}, bf16[160,576]{1,0:T(8,128)(2,1)S(1)}, u32[]{:S(2)}, u32[]{:S(2)}) collective-permute-start(bf16[160,576]{1,0:T(8,128)(2,1)S(1)} %collective-permute-done.3.refs_4_), channel_id=1, source_target_pairs={{0,2},{1,3},{2,0},{3,1},{4,6},{5,7},{6,4},{7,5},{8,10},{9,11},{10,... | collective-permute-start | bytes 552968 | tf_op jit(solution)/shard_map/ppermute | solution.py:52
  14.2 2.7 %collective-permute-start.5 = (bf16[160,576]{1,0:T(8,128)(2,1)S(1)}, bf16[160,576]{1,0:T(8,128)(2,1)S(1)}, u32[]{:S(2)}, u32[]{:S(2)}) collective-permute-start(bf16[160,576]{1,0:T(8,128)(2,1)S(1)} %get-tuple-element.17), channel_id=1, source_target_pairs={{0,1},{1,0},{2,3},{3,2},{4,5},{5,4},{6,7},{7,6},{8,9},{9,8},{10,11... | collective-permute-start | bytes 552968 | tf_op jit(solution)/shard_map/ppermute | solution.py:52
  15.5 5.4 %copy-start = (bf16[1,3,128,4608]{3,2,1,0:T(8,128)(2,1)S(1)}, bf16[1,3,128,4608]{3,2,1,0:T(8,128)(2,1)}, u32[]{:S(2)}) copy-start(bf16[1,3,128,4608]{3,2,1,0:T(8,128)(2,1)} %param.9) | copy-start | bytes 10616836
  15.5 1.4 %collective-permute-start.6 = (f32[2,128]{1,0:T(2,128)S(1)}, f32[2,128]{1,0:T(2,128)S(1)}, u32[]{:S(2)}, u32[]{:S(2)}) collective-permute-start(f32[2,128]{1,0:T(2,128)S(1)} %pad_maximum_fusion.refs_8_), channel_id=1, source_target_pairs={{0,1},{1,0},{2,3},{3,2},{4,5},{5,4},{6,7},{7,6},{8,9},{9,8},{10,11... | collective-permute-start | bytes 3080 | tf_op jit(solution)/shard_map/ppermute | solution.py:52
  16.9 1.3 %copy-start.1 = (bf16[1,4608,128]{2,1,0:T(8,128)(2,1)S(1)}, bf16[1,4608,128]{2,1,0:T(8,128)(2,1)}, u32[]{:S(2)}) copy-start(bf16[1,4608,128]{2,1,0:T(8,128)(2,1)} %param.6) | copy-start | bytes 3538948
  21.0 10.6 %collective-permute-start.12 = (bf16[3,128,4608]{2,1,0:T(8,128)(2,1)S(1)}, bf16[3,128,4608]{2,1,0:T(8,128)(2,1)S(1)}, u32[]{:S(2)}, u32[]{:S(2)}) collective-permute-start(bf16[3,128,4608]{2,1,0:T(8,128)(2,1)S(1)} %bitcast.12), channel_id=1, source_target_pairs={{0,1},{1,0},{2,3},{3,2},{4,5},{5,4},{6,7},{7,6},{8,9},{9,8},{10,11... | collective-permute-start | bytes 10616840 | tf_op jit(solution)/shard_map/ppermute | solution.py:52
  21.3 7.2 %collective-permute-start.9 = (bf16[160,256]{1,0:T(8,128)(2,1)S(1)}, bf16[160,256]{1,0:T(8,128)(2,1)S(1)}, u32[]{:S(2)}, u32[]{:S(2)}) collective-permute-start(bf16[160,256]{1,0:T(8,128)(2,1)S(1)} %shard_map.69.refs_0_), channel_id=1, source_target_pairs={{0,8},{8,16},{16,24},{24,0},{1,9},{9,17},{17,25},{25,1},{2,10},{10... | collective-permute-start | bytes 245768 | tf_op jit(solution)/shard_map/ppermute | solution.py:26
  22.9 8.6 %collective-permute-start.11 = (bf16[160,256]{1,0:T(8,128)(2,1)S(1)}, bf16[160,256]{1,0:T(8,128)(2,1)S(1)}, u32[]{:S(2)}, u32[]{:S(2)}) collective-permute-start(bf16[160,256]{1,0:T(8,128)(2,1)S(1)} %shard_map.69.refs_0_), channel_id=1, source_target_pairs={{0,16},{8,24},{16,0},{24,8},{1,17},{9,25},{17,1},{25,9},{2,18},{10... | collective-permute-start | bytes 245768 | tf_op jit(solution)/shard_map/ppermute | solution.py:26
  25.5 1.8 %collective-permute-start.10 = (bf16[160,128]{1,0:T(8,128)(2,1)S(1)}, bf16[160,128]{1,0:T(8,128)(2,1)S(1)}, u32[]{:S(2)}, u32[]{:S(2)}) collective-permute-start(bf16[160,128]{1,0:T(8,128)(2,1)S(1)} %get-tuple-element.35), channel_id=1, source_target_pairs={{0,1},{1,0},{2,3},{3,2},{4,5},{5,4},{6,7},{7,6},{8,9},{9,8},{10,11... | collective-permute-start | bytes 122888 | tf_op jit(solution)/shard_map/ppermute | solution.py:52
  32.2 8.0 %collective-permute-start.17 = (bf16[160,576]{1,0:T(8,128)(2,1)S(1)}, bf16[160,576]{1,0:T(8,128)(2,1)S(1)}, u32[]{:S(2)}, u32[]{:S(2)}) collective-permute-start(bf16[160,576]{1,0:T(8,128)(2,1)S(1)} %get-tuple-element.30), channel_id=1, source_target_pairs={{0,4},{1,5},{2,6},{3,7},{4,0},{5,1},{6,2},{7,3},{8,12},{9,13},{10,... | collective-permute-start | bytes 552968 | tf_op jit(solution)/shard_map/ppermute | solution.py:52
  33.8 8.0 %collective-permute-start.14 = (bf16[160,576]{1,0:T(8,128)(2,1)S(1)}, bf16[160,576]{1,0:T(8,128)(2,1)S(1)}, u32[]{:S(2)}, u32[]{:S(2)}) collective-permute-start(bf16[160,576]{1,0:T(8,128)(2,1)S(1)} %get-tuple-element.27), channel_id=1, source_target_pairs={{0,2},{1,3},{2,0},{3,1},{4,6},{5,7},{6,4},{7,5},{8,10},{9,11},{10,... | collective-permute-start | bytes 552968 | tf_op jit(solution)/shard_map/ppermute | solution.py:52
  34.9 7.8 %collective-permute-start.19 = (bf16[160,576]{1,0:T(8,128)(2,1)S(1)}, bf16[160,576]{1,0:T(8,128)(2,1)S(1)}, u32[]{:S(2)}, u32[]{:S(2)}) collective-permute-start(bf16[160,576]{1,0:T(8,128)(2,1)S(1)} %get-tuple-element.31), channel_id=1, source_target_pairs={{0,5},{1,4},{2,7},{3,6},{4,1},{5,0},{6,3},{7,2},{8,13},{9,12},{10,... | collective-permute-start | bytes 552968 | tf_op jit(solution)/shard_map/ppermute | solution.py:52
  35.6 10.5 %collective-permute-start.13 = (bf16[160,576]{1,0:T(8,128)(2,1)S(1)}, bf16[160,576]{1,0:T(8,128)(2,1)S(1)}, u32[]{:S(2)}, u32[]{:S(2)}) collective-permute-start(bf16[160,576]{1,0:T(8,128)(2,1)S(1)} %get-tuple-element.25), channel_id=1, source_target_pairs={{0,2},{1,3},{2,0},{3,1},{4,6},{5,7},{6,4},{7,5},{8,10},{9,11},{10,... | collective-permute-start | bytes 552968 | tf_op jit(solution)/shard_map/ppermute | solution.py:52
  37.8 8.3 %collective-permute-start.16 = (bf16[160,576]{1,0:T(8,128)(2,1)S(1)}, bf16[160,576]{1,0:T(8,128)(2,1)S(1)}, u32[]{:S(2)}, u32[]{:S(2)}) collective-permute-start(bf16[160,576]{1,0:T(8,128)(2,1)S(1)} %get-tuple-element.28), channel_id=1, source_target_pairs={{0,1},{1,0},{2,3},{3,2},{4,5},{5,4},{6,7},{7,6},{8,9},{9,8},{10,11... | collective-permute-start | bytes 552968 | tf_op jit(solution)/shard_map/ppermute | solution.py:52
  40.2 7.8 %collective-permute-start.18 = (bf16[160,576]{1,0:T(8,128)(2,1)S(1)}, bf16[160,576]{1,0:T(8,128)(2,1)S(1)}, u32[]{:S(2)}, u32[]{:S(2)}) collective-permute-start(bf16[160,576]{1,0:T(8,128)(2,1)S(1)} %shard_map.75), channel_id=1, source_target_pairs={{0,3},{1,2},{2,1},{3,0},{4,7},{5,6},{6,5},{7,4},{8,11},{9,10},{10,... | collective-permute-start | bytes 552968 | tf_op jit(solution)/shard_map/ppermute | solution.py:52
  41.8 6.3 %collective-permute-start.15 = (bf16[160,576]{1,0:T(8,128)(2,1)S(1)}, bf16[160,576]{1,0:T(8,128)(2,1)S(1)}, u32[]{:S(2)}, u32[]{:S(2)}) collective-permute-start(bf16[160,576]{1,0:T(8,128)(2,1)S(1)} %shard_map.74), channel_id=1, source_target_pairs={{0,4},{1,5},{2,6},{3,7},{4,0},{5,1},{6,2},{7,3},{8,12},{9,13},{10,... | collective-permute-start | bytes 552968 | tf_op jit(solution)/shard_map/ppermute | solution.py:52

commit v6 on v3

--- a/solution.py
+++ b/solution.py
@@ -9,6 +9,7 @@
 from jax.sharding import PartitionSpec as P
 
 LAYERS = 4
+TAIL_PARTS = 2
 VMEM_LIMIT = 16 * 1024 * 1024
 
 
@@ -142,25 +143,33 @@
             out_ref[step * per_block + piece] = total[:, piece * width:(piece + 1) * width].astype(jnp.bfloat16)
 
 
-def sum_two_kernel(a_ref, b_ref, out_ref):
-    out_ref[...] = (a_ref[...].astype(jnp.float32) + b_ref[...].astype(jnp.float32)).astype(jnp.bfloat16)
-
-
-def sum_two(a, b):
-    return call(sum_two_kernel, jax.ShapeDtypeStruct(a.shape, jnp.bfloat16))(a, b)
-
-
-def finish_kernel(*refs):
+def sum_two_kernel(a_ref, b_ref, *out_refs):
+    first = 0
+    for out_ref in out_refs:
+        rows = slice(first, first + out_ref.shape[0])
+        out_ref[...] = (a_ref[rows, :].astype(jnp.float32) + b_ref[rows, :].astype(jnp.float32)).astype(jnp.bfloat16)
+        first = rows.stop
+
+
+def sum_two(a, b, parts):
+    rows, width = a.shape
+    edges = [rows * part // parts // 16 * 16 for part in range(parts)] + [rows]
+    shapes = [jax.ShapeDtypeStruct((end - start, width), jnp.bfloat16) for start, end in zip(edges, edges[1:])]
+    return call(sum_two_kernel, shapes)(a, b)
+
+
+def finish_kernel(half, *refs):
     *parts, out_ref, sums, sems = refs
-    half = len(parts) // 2
-    rows = parts[0].shape[0]
+    rows = sums.shape[1]
     core = lax.axis_index("latent") % 2
     copies = []
     for index, (place, group) in enumerate(((core, parts[:half]), (1 - core, parts[half:]))):
-        total = group[0][...].astype(jnp.float32)
-        for part in group[1:]:
-            total += part[...].astype(jnp.float32)
-        sums[index] = total.astype(out_ref.dtype)
+        first = 0
+        for last in group[2:]:
+            some = slice(first, first + last.shape[0])
+            total = sum(part[some, :].astype(jnp.float32) for part in group[:2]) + last[...].astype(jnp.float32)
+            sums[index, some, :] = total.astype(out_ref.dtype)
+            first = some.stop
         target = out_ref.at[pl.ds(pl.multiple_of(place * rows, 16), rows), :]
         copies.append(pltpu.make_async_copy(sums.at[index], target, sems.at[index]))
         copies[-1].start()
@@ -171,7 +180,7 @@
 def finish(mine, other, dtype):
     rows, width = mine[0].shape
     return pl.pallas_call(
-        finish_kernel,
+        functools.partial(finish_kernel, len(mine)),
         out_shape=jax.ShapeDtypeStruct((2 * rows, width), dtype),
         out_specs=pl.BlockSpec(memory_space=pl.ANY),
         scratch_shapes=[pltpu.VMEM((2, rows, width), dtype), pltpu.SemaphoreType.DMA((2,))],
@@ -215,10 +224,11 @@
     y_same, y_cross = decode_chip(2, acts, own, sib, width)
     from_x_same, from_y_cross = to_peer(x_same, 2), to_peer(y_cross, 5)
     own_same, own_cross = decode_chip(0, acts, own, sib, width)
-    y_sum, x_sum = sum_two(y_same, for_y), sum_two(x_cross, for_x)
-    from_y_same, from_x_cross = to_peer(y_sum, 4), to_peer(x_sum, 3)
     from_sib = to_peer(own_cross, 1)
-    return finish((own_same, from_x_same, from_y_same), (from_sib, from_x_cross, from_y_cross), dtype)
+    y_sums = [after(part, from_sib) for part in sum_two(y_same, for_y, TAIL_PARTS)]
+    from_y_same = [to_peer(part, 4) for part in y_sums]
+    from_x_cross = [to_peer(part, 3) for part in sum_two(x_cross, for_x, 1)]
+    return finish((own_same, from_x_same, *from_y_same), (from_sib, from_y_cross, *from_x_cross), dtype)
 
 
 def shards(residual, encoder, enc_bias, gate_code, decoder):

time: 47.9 us -> 47.9 us (level)
  waiting for transfers between devices: 19.5 us -> 18.2 us
  starting transfers between devices: 18.7 us -> 19.8 us
    ppermute x18 -> x19, waiting for transfers between devices: 16.2 us -> 14.8 us  [to_peer(): lax.ppermute(value, 'latent', [(i, i ^ offset) for i in range(lax.axis_si...]
    ppermute x18 -> x19, starting transfers between devices: 14.4 us -> 15.6 us  [to_peer(): lax.ppermute(value, 'latent', [(i, i ^ offset) for i in range(lax.axis_si...]
  transfers between devices with their start and end apart: 20 -> 21, of which waited for: 11 -> 11; matrix products, arithmetic and copies ran while one was open for 6% -> 6% of each run, Pallas kernels for 6% -> 6%
where the time goes in v6:
time: 47.9 us; the launch traced here: 47.4 us
  starting transfers between devices  19.8 us (41%)
  waiting for transfers between devices  18.2 us (38%)
  Pallas kernels  4.36 us (9%)
  local copies, waits for them, and re-layouts  2.35 us (5%)
  other arithmetic  1.97 us (4%)
  between operations  0.73 us (2%)
    ppermute x19, starting transfers between devices, to_peer(): lax.ppermute(value, 'latent', [(i, i ^ offset) for i in range(lax.axis_si...  15.6 us
    ppermute x19, waiting for transfers between devices, to_peer(): lax.ppermute(value, 'latent', [(i, i ^ offset) for i in range(lax.axis_si...  14.8 us
    ppermute x2, starting transfers between devices, earlier_layers(): lax.ppermute(value, 'section', [(i, (i + shift) % count) for i in range(c...  4.23 us
    ppermute x2, waiting for transfers between devices, earlier_layers(): lax.ppermute(value, 'section', [(i, (i + shift) % count) for i in range(c...  3.34 us
    pallas_call x4, Pallas kernels, decode_chip(): call(functools.partial(decode_chip_kernel, chip_offset), (shape, shape))  2.51 us
    unnamed x4, local copies, waits for them, and re-layouts  1.27 us
    squeeze x1, local copies, waits for them, and re-layouts, shards(): lax.dynamic_index_in_dim(halves, place + half, 0, keepdims=False)  1.06 us
  transfers between devices with their start and end apart: 21, of which 11 were waited for; matrix products, arithmetic and copies ran while one was open for 6% of the time, Pallas kernels for 6%

profile of v6, /device:TPU:0, one launch (start us, length us, event | category | flops | bytes accessed | tf_op | source)
XLA Modules:
  0.0 47.4 jit_solution(1788162304816474022)
XLA Ops:
  1.1 1.1 %dynamic-slice_bitcast_fusion = (bf16[160,576]{1,0:T(8,128)(2,1)S(1)}, bf16[160,576]{1,0:T(8,128)(2,1)S(1)}) fusion(bf16[8,160,576]{2,1,0:T(8,128)(2,1)} %bitcast.20, s32[]{:T(128)S(6)} %select_n.36, s32[]{:T(128)S(6)} %select_n.35), kind=kLoop, calls=%fused_computation | loop fusion | bytes 737288 | tf_op jit(solution)/shard_map/jit(dynamic_index_in_dim)/squeeze | solution.py:243
  2.2 2.6 %collective-permute-start = (bf16[160,576]{1,0:T(8,128)(2,1)S(1)}, bf16[160,576]{1,0:T(8,128)(2,1)S(1)}, u32[]{:S(2)}, u32[]{:S(2)}) collective-permute-start(bf16[160,576]{1,0:T(8,128)(2,1)S(1)} %get-tuple-element.41.refs_0_), channel_id=1, source_target_pairs={{0,2},{1,3},{2,0},{3,1},{4,6},{5,7},{6,4},{7,5},{8,10},{9,11},{10,... | collective-permute-start | bytes 552968 | tf_op jit(solution)/shard_map/ppermute | solution.py:53
  4.8 1.3 %collective-permute-start.3 = (bf16[160,576]{1,0:T(8,128)(2,1)S(1)}, bf16[160,576]{1,0:T(8,128)(2,1)S(1)}, u32[]{:S(2)}, u32[]{:S(2)}) collective-permute-start(bf16[160,576]{1,0:T(8,128)(2,1)S(1)} %get-tuple-element.21), channel_id=1, source_target_pairs={{0,5},{1,4},{2,7},{3,6},{4,1},{5,0},{6,3},{7,2},{8,13},{9,12},{10,... | collective-permute-start | bytes 552968 | tf_op jit(solution)/shard_map/ppermute | solution.py:53
  6.7 4.1 %collective-permute-done.refs_1_ = bf16[160,576]{1,0:T(8,128)(2,1)S(1)} collective-permute-done((bf16[160,576]{1,0:T(8,128)(2,1)S(1)}, bf16[160,576]{1,0:T(8,128)(2,1)S(1)}, u32[]{:S(2)}, u32[]{:S(2)}) %collective-permute-start) | collective-permute-done | bytes 184352 | tf_op jit(solution)/shard_map/ppermute | solution.py:53
  10.7 2.0 %collective-permute-start.7 = (bf16[160,576]{1,0:T(8,128)(2,1)S(1)}, bf16[160,576]{1,0:T(8,128)(2,1)S(1)}, u32[]{:S(2)}, u32[]{:S(2)}) collective-permute-start(bf16[160,576]{1,0:T(8,128)(2,1)S(1)} %collective-permute-done.refs_1_), channel_id=1, source_target_pairs={{0,4},{1,5},{2,6},{3,7},{4,0},{5,1},{6,2},{7,3},{8,12},{9,13},{10,... | collective-permute-start | bytes 552968 | tf_op jit(solution)/shard_map/ppermute | solution.py:53
  12.7 1.5 %collective-permute-start.8 = (bf16[160,576]{1,0:T(8,128)(2,1)S(1)}, bf16[160,576]{1,0:T(8,128)(2,1)S(1)}, u32[]{:S(2)}, u32[]{:S(2)}) collective-permute-start(bf16[160,576]{1,0:T(8,128)(2,1)S(1)} %collective-permute-done.3.refs_4_), channel_id=1, source_target_pairs={{0,2},{1,3},{2,0},{3,1},{4,6},{5,7},{6,4},{7,5},{8,10},{9,11},{10,... | collective-permute-start | bytes 552968 | tf_op jit(solution)/shard_map/ppermute | solution.py:53
  14.2 0.7 %add_multiply_fusion = f32[1,128]{1,0:T(1,128)S(1)} fusion(s32[1,128]{1,0:T(1,128)} %param.8), kind=kLoop, calls=%fused_computation.5 | loop fusion | flops 384 | bytes 1024 | tf_op jit(solution)/shard_map/mul | solution.py:244
  14.9 0.7 %pad_maximum_fusion.refs_8_ = f32[2,128]{1,0:T(2,128)S(1)} fusion(f32[1,128]{1,0:T(1,128)S(1)} %add_multiply_fusion, f32[1,128]{1,0:T(1,128)} %param.7), kind=kLoop, calls=%fused_computation.4 | loop fusion | flops 256 | bytes 2048 | tf_op jit(solution)/shard_map/stack | solution.py:245
  15.5 0.6 %collective-permute-start.6 = (f32[2,128]{1,0:T(2,128)S(1)}, f32[2,128]{1,0:T(2,128)S(1)}, u32[]{:S(2)}, u32[]{:S(2)}) collective-permute-start(f32[2,128]{1,0:T(2,128)S(1)} %pad_maximum_fusion.refs_8_), channel_id=1, source_target_pairs={{0,1},{1,0},{2,3},{3,2},{4,5},{5,4},{6,7},{7,6},{8,9},{9,8},{10,11... | collective-permute-start | bytes 3080 | tf_op jit(solution)/shard_map/ppermute | solution.py:53
  16.1 0.7 %collective-permute-done.2.refs_3_ = bf16[160,576]{1,0:T(8,128)(2,1)S(1)} collective-permute-done((bf16[160,576]{1,0:T(8,128)(2,1)S(1)}, bf16[160,576]{1,0:T(8,128)(2,1)S(1)}, u32[]{:S(2)}, u32[]{:S(2)}) %collective-permute-start.2) | collective-permute-done | bytes 184352 | tf_op jit(solution)/shard_map/ppermute | solution.py:53
  16.9 1.3 %copy-done.1 = bf16[1,4608,128]{2,1,0:T(8,128)(2,1)S(1)} copy-done((bf16[1,4608,128]{2,1,0:T(8,128)(2,1)S(1)}, bf16[1,4608,128]{2,1,0:T(8,128)(2,1)}, u32[]{:S(2)}) %copy-start.1) | copy-done | bytes 1179672
  18.2 0.6 %shard_map.68 = (f32[160,256]{1,0:T(8,128)S(1)}, f32[1,256]{1,0:T(1,128)S(1)}, bf16[2,576,256]{2,1,0:T(8,128)(2,1)S(1)}) custom-call(bf16[160,576]{1,0:T(8,128)(2,1)S(1)} %get-tuple-element.41.refs_0_, bf16[160,576]{1,0:T(8,128)(2,1)S(1)} %collective-permute-done.refs_1_, bf16[160,576]{1,0:T(8,128)(2,1)S(1)} %collective-permute-done.1.refs_2_, ...), custom_call_target="tpu_custom_call" | custom-call | flops 283115520 | tf_op jit(solution)/shard_map/pallas_call | solution.py:94
  18.8 2.1 %collective-permute-done.7.refs_0_ = bf16[160,576]{1,0:T(8,128)(2,1)S(1)} collective-permute-done((bf16[160,576]{1,0:T(8,128)(2,1)S(1)}, bf16[160,576]{1,0:T(8,128)(2,1)S(1)}, u32[]{:S(2)}, u32[]{:S(2)}) %collective-permute-start.7) | collective-permute-done | bytes 184352 | tf_op jit(solution)/shard_map/ppermute | solution.py:53
  21.3 2.7 %collective-permute-start.10 = (bf16[160,256]{1,0:T(8,128)(2,1)S(1)}, bf16[160,256]{1,0:T(8,128)(2,1)S(1)}, u32[]{:S(2)}, u32[]{:S(2)}) collective-permute-start(bf16[160,256]{1,0:T(8,128)(2,1)S(1)} %shard_map.69.refs_0_), channel_id=1, source_target_pairs={{0,16},{8,24},{16,0},{24,8},{1,17},{9,25},{17,1},{25,9},{2,18},{10... | collective-permute-start | bytes 245768 | tf_op jit(solution)/shard_map/ppermute | solution.py:27
  23.9 1.6 %collective-permute-start.9 = (bf16[160,256]{1,0:T(8,128)(2,1)S(1)}, bf16[160,256]{1,0:T(8,128)(2,1)S(1)}, u32[]{:S(2)}, u32[]{:S(2)}) collective-permute-start(bf16[160,256]{1,0:T(8,128)(2,1)S(1)} %shard_map.69.refs_0_), channel_id=1, source_target_pairs={{0,8},{8,16},{16,24},{24,0},{1,9},{9,17},{17,25},{25,1},{2,10},{10... | collective-permute-start | bytes 245768 | tf_op jit(solution)/shard_map/ppermute | solution.py:27
  25.5 1.7 %collective-permute-done.11 = bf16[160,128]{1,0:T(8,128)(2,1)S(1)} collective-permute-done((bf16[160,128]{1,0:T(8,128)(2,1)S(1)}, bf16[160,128]{1,0:T(8,128)(2,1)S(1)}, u32[]{:S(2)}, u32[]{:S(2)}) %collective-permute-start.11) | collective-permute-done | bytes 40992 | tf_op jit(solution)/shard_map/ppermute | solution.py:53
  27.3 3.3 %collective-permute-done.10.refs_2_ = bf16[160,256]{1,0:T(8,128)(2,1)S(1)} collective-permute-done((bf16[160,256]{1,0:T(8,128)(2,1)S(1)}, bf16[160,256]{1,0:T(8,128)(2,1)S(1)}, u32[]{:S(2)}, u32[]{:S(2)}) %collective-permute-start.10) | collective-permute-done | bytes 81952 | tf_op jit(solution)/shard_map/ppermute | solution.py:27
  30.6 0.6 %shard_map.73 = (bf16[160,576]{1,0:T(8,128)(2,1)S(1)}, bf16[160,576]{1,0:T(8,128)(2,1)S(1)}) custom-call(bf16[160,256]{1,0:T(8,128)(2,1)S(1)} %shard_map.69.refs_0_, bf16[160,256]{1,0:T(8,128)(2,1)S(1)} %collective-permute-done.9.refs_1_, bf16[160,256]{1,0:T(8,128)(2,1)S(1)} %collective-permute-done.10.refs_2_, bf16[3,128,4608]{2,1,0:T(8,128)(2,1)S(1)} %bitcast.13, ...), custom_call_target="tpu_custom_call" | custom-call | tf_op jit(solution)/shard_map/pallas_call | solution.py:132
  31.2 1.6 %collective-permute-start.19 = (bf16[160,576]{1,0:T(8,128)(2,1)S(1)}, bf16[160,576]{1,0:T(8,128)(2,1)S(1)}, u32[]{:S(2)}, u32[]{:S(2)}) collective-permute-start(bf16[160,576]{1,0:T(8,128)(2,1)S(1)} %get-tuple-element.39), channel_id=1, source_target_pairs={{0,4},{1,5},{2,6},{3,7},{4,0},{5,1},{6,2},{7,3},{8,12},{9,13},{10,... | collective-permute-start | bytes 552968 | tf_op jit(solution)/shard_map/ppermute | solution.py:53
  33.3 0.6 %shard_map.70 = (bf16[160,576]{1,0:T(8,128)(2,1)S(1)}, bf16[160,576]{1,0:T(8,128)(2,1)S(1)}) custom-call(bf16[160,256]{1,0:T(8,128)(2,1)S(1)} %shard_map.69.refs_0_, bf16[160,256]{1,0:T(8,128)(2,1)S(1)} %collective-permute-done.9.refs_1_, bf16[160,256]{1,0:T(8,128)(2,1)S(1)} %collective-permute-done.10.refs_2_, bf16[3,128,4608]{2,1,0:T(8,128)(2,1)S(1)} %bitcast.14, ...), custom_call_target="tpu_custom_call" | custom-call | tf_op jit(solution)/shard_map/pallas_call | solution.py:132
  34.1 0.6 %shard_map.72 = (bf16[160,576]{1,0:T(8,128)(2,1)S(1)}, bf16[160,576]{1,0:T(8,128)(2,1)S(1)}) custom-call(bf16[160,256]{1,0:T(8,128)(2,1)S(1)} %shard_map.69.refs_0_, bf16[160,256]{1,0:T(8,128)(2,1)S(1)} %collective-permute-done.9.refs_1_, bf16[160,256]{1,0:T(8,128)(2,1)S(1)} %collective-permute-done.10.refs_2_, bf16[3,128,4608]{2,1,0:T(8,128)(2,1)S(1)} %bitcast.15, ...), custom_call_target="tpu_custom_call" | custom-call | tf_op jit(solution)/shard_map/pallas_call | solution.py:132
  34.7 0.6 %collective-permute-start.18 = (bf16[160,576]{1,0:T(8,128)(2,1)S(1)}, bf16[160,576]{1,0:T(8,128)(2,1)S(1)}, u32[]{:S(2)}, u32[]{:S(2)}) collective-permute-start(bf16[160,576]{1,0:T(8,128)(2,1)S(1)} %get-tuple-element.37), channel_id=1, source_target_pairs={{0,5},{1,4},{2,7},{3,6},{4,1},{5,0},{6,3},{7,2},{8,13},{9,12},{10,... | collective-permute-start | bytes 552968 | tf_op jit(solution)/shard_map/ppermute | solution.py:53
  35.3 0.6 %shard_map.71 = (bf16[160,576]{1,0:T(8,128)(2,1)S(1)}, bf16[160,576]{1,0:T(8,128)(2,1)S(1)}) custom-call(bf16[160,256]{1,0:T(8,128)(2,1)S(1)} %shard_map.69.refs_0_, bf16[160,256]{1,0:T(8,128)(2,1)S(1)} %collective-permute-done.9.refs_1_, bf16[160,256]{1,0:T(8,128)(2,1)S(1)} %collective-permute-done.10.refs_2_, bf16[3,128,4608]{2,1,0:T(8,128)(2,1)S(1)} %bitcast.16, ...), custom_call_target="tpu_custom_call" | custom-call | tf_op jit(solution)/shard_map/pallas_call | solution.py:132
  35.9 1.6 %collective-permute-start.13 = (bf16[160,576]{1,0:T(8,128)(2,1)S(1)}, bf16[160,576]{1,0:T(8,128)(2,1)S(1)}, u32[]{:S(2)}, u32[]{:S(2)}) collective-permute-start(bf16[160,576]{1,0:T(8,128)(2,1)S(1)} %get-tuple-element.29), channel_id=1, source_target_pairs={{0,2},{1,3},{2,0},{3,1},{4,6},{5,7},{6,4},{7,5},{8,10},{9,11},{10,... | collective-permute-start | bytes 552968 | tf_op jit(solution)/shard_map/ppermute | solution.py:53
  37.7 0.9 %collective-permute-done.14.b_ref = bf16[160,576]{1,0:T(8,128)(2,1)S(1)} collective-permute-done((bf16[160,576]{1,0:T(8,128)(2,1)S(1)}, bf16[160,576]{1,0:T(8,128)(2,1)S(1)}, u32[]{:S(2)}, u32[]{:S(2)}) %collective-permute-start.14) | collective-permute-done | bytes 184352 | tf_op jit(solution)/shard_map/ppermute | solution.py:53
  38.7 1.1 %collective-permute-start.17 = (bf16[80,576]{1,0:T(8,128)(2,1)S(1)}, bf16[80,576]{1,0:T(8,128)(2,1)S(1)}, u32[]{:S(2)}, u32[]{:S(2)}) collective-permute-start(bf16[80,576]{1,0:T(8,128)(2,1)S(1)} %get-tuple-element.36), channel_id=1, source_target_pairs={{0,4},{1,5},{2,6},{3,7},{4,0},{5,1},{6,2},{7,3},{8,12},{9,13},{10,... | collective-permute-start | bytes 276488 | tf_op jit(solution)/shard_map/ppermute | solution.py:53
  39.8 1.0 %collective-permute-start.16 = (bf16[80,576]{1,0:T(8,128)(2,1)S(1)}, bf16[80,576]{1,0:T(8,128)(2,1)S(1)}, u32[]{:S(2)}, u32[]{:S(2)}) collective-permute-start(bf16[80,576]{1,0:T(8,128)(2,1)S(1)} %get-tuple-element.34), channel_id=1, source_target_pairs={{0,4},{1,5},{2,6},{3,7},{4,0},{5,1},{6,2},{7,3},{8,12},{9,13},{10,... | collective-permute-start | bytes 276488 | tf_op jit(solution)/shard_map/ppermute | solution.py:53
  40.8 0.6 %maximum_select_fusion = bf16[2,160,128]{2,1,0:T(8,128)(2,1)} fusion(bf16[1,160,128]{2,1,0:T(8,128)(2,1)S(1)} %bitcast.22, bf16[1,160,128]{2,1,0:T(8,128)(2,1)S(1)} %get-tuple-element.42, pred[]{:T(512)S(6)} %eq.5), kind=kLoop, calls=%fused_computation.2 | loop fusion | flops 122880 | bytes 163841 | tf_op jit(solution)/shard_map/jit(_where)/select_n | solution.py:248
  41.5 2.4 %collective-permute-done.13.refs_1_ = bf16[160,576]{1,0:T(8,128)(2,1)S(1)} collective-permute-done((bf16[160,576]{1,0:T(8,128)(2,1)S(1)}, bf16[160,576]{1,0:T(8,128)(2,1)S(1)}, u32[]{:S(2)}, u32[]{:S(2)}) %collective-permute-start.13) | collective-permute-done | bytes 184352 | tf_op jit(solution)/shard_map/ppermute | solution.py:53
  43.9 0.8 %collective-permute-done.17.refs_3_ = bf16[80,576]{1,0:T(8,128)(2,1)S(1)} collective-permute-done((bf16[80,576]{1,0:T(8,128)(2,1)S(1)}, bf16[80,576]{1,0:T(8,128)(2,1)S(1)}, u32[]{:S(2)}, u32[]{:S(2)}) %collective-permute-start.17) | collective-permute-done | bytes 92192 | tf_op jit(solution)/shard_map/ppermute | solution.py:53
  44.8 1.8 %collective-permute-done.16.refs_2_ = bf16[80,576]{1,0:T(8,128)(2,1)S(1)} collective-permute-done((bf16[80,576]{1,0:T(8,128)(2,1)S(1)}, bf16[80,576]{1,0:T(8,128)(2,1)S(1)}, u32[]{:S(2)}, u32[]{:S(2)}) %collective-permute-start.16) | collective-permute-done | bytes 92192 | tf_op jit(solution)/shard_map/ppermute | solution.py:53
  46.5 0.8 %shard_map.76 = bf16[320,576]{1,0:T(8,128)(2,1)} custom-call(bf16[160,576]{1,0:T(8,128)(2,1)S(1)} %get-tuple-element.28.refs_0_, bf16[160,576]{1,0:T(8,128)(2,1)S(1)} %collective-permute-done.13.refs_1_, bf16[80,576]{1,0:T(8,128)(2,1)S(1)} %collective-permute-done.16.refs_2_, bf16[80,576]{1,0:T(8,128)(2,1)S(1)} %collective-permute-done.17.refs_3_, ...), custom_call_target="tpu_custom_call" | custom-call | tf_op jit(solution)/shard_map/pallas_call | solution.py:182
  (28 shorter events, 2.4 us)
Async XLA Ops:
  0.6 13.6 %collective-permute-start.4 = (bf16[4608,128]{1,0:T(8,128)(2,1)}, bf16[4608,128]{1,0:T(8,128)(2,1)S(1)}, u32[]{:S(2)}, u32[]{:S(2)}) collective-permute-start(bf16[4608,128]{1,0:T(8,128)(2,1)} %bitcast.17), channel_id=1, source_target_pairs={{0,1},{1,0},{2,3},{3,2},{4,5},{5,4},{6,7},{7,6},{8,9},{9,8},{10,11... | collective-permute-start | bytes 3538952 | tf_op jit(solution)/shard_map/ppermute | solution.py:53
  2.2 8.5 %collective-permute-start = (bf16[160,576]{1,0:T(8,128)(2,1)S(1)}, bf16[160,576]{1,0:T(8,128)(2,1)S(1)}, u32[]{:S(2)}, u32[]{:S(2)}) collective-permute-start(bf16[160,576]{1,0:T(8,128)(2,1)S(1)} %get-tuple-element.41.refs_0_), channel_id=1, source_target_pairs={{0,2},{1,3},{2,0},{3,1},{4,6},{5,7},{6,4},{7,5},{8,10},{9,11},{10,... | collective-permute-start | bytes 552968 | tf_op jit(solution)/shard_map/ppermute | solution.py:53
  4.8 7.9 %collective-permute-start.3 = (bf16[160,576]{1,0:T(8,128)(2,1)S(1)}, bf16[160,576]{1,0:T(8,128)(2,1)S(1)}, u32[]{:S(2)}, u32[]{:S(2)}) collective-permute-start(bf16[160,576]{1,0:T(8,128)(2,1)S(1)} %get-tuple-element.21), channel_id=1, source_target_pairs={{0,5},{1,4},{2,7},{3,6},{4,1},{5,0},{6,3},{7,2},{8,13},{9,12},{10,... | collective-permute-start | bytes 552968 | tf_op jit(solution)/shard_map/ppermute | solution.py:53
  6.1 9.4 %collective-permute-start.1 = (bf16[160,576]{1,0:T(8,128)(2,1)S(1)}, bf16[160,576]{1,0:T(8,128)(2,1)S(1)}, u32[]{:S(2)}, u32[]{:S(2)}) collective-permute-start(bf16[160,576]{1,0:T(8,128)(2,1)S(1)} %get-tuple-element.21), channel_id=1, source_target_pairs={{0,3},{1,2},{2,1},{3,0},{4,7},{5,6},{6,5},{7,4},{8,11},{9,10},{10,... | collective-permute-start | bytes 552968 | tf_op jit(solution)/shard_map/ppermute | solution.py:53
  6.6 10.3 %collective-permute-start.2 = (bf16[160,576]{1,0:T(8,128)(2,1)S(1)}, bf16[160,576]{1,0:T(8,128)(2,1)S(1)}, u32[]{:S(2)}, u32[]{:S(2)}) collective-permute-start(bf16[160,576]{1,0:T(8,128)(2,1)S(1)} %get-tuple-element.41.refs_0_), channel_id=1, source_target_pairs={{0,4},{1,5},{2,6},{3,7},{4,0},{5,1},{6,2},{7,3},{8,12},{9,13},{10,... | collective-permute-start | bytes 552968 | tf_op jit(solution)/shard_map/ppermute | solution.py:53
  10.7 10.2 %collective-permute-start.7 = (bf16[160,576]{1,0:T(8,128)(2,1)S(1)}, bf16[160,576]{1,0:T(8,128)(2,1)S(1)}, u32[]{:S(2)}, u32[]{:S(2)}) collective-permute-start(bf16[160,576]{1,0:T(8,128)(2,1)S(1)} %collective-permute-done.refs_1_), channel_id=1, source_target_pairs={{0,4},{1,5},{2,6},{3,7},{4,0},{5,1},{6,2},{7,3},{8,12},{9,13},{10,... | collective-permute-start | bytes 552968 | tf_op jit(solution)/shard_map/ppermute | solution.py:53
  12.7 8.2 %collective-permute-start.8 = (bf16[160,576]{1,0:T(8,128)(2,1)S(1)}, bf16[160,576]{1,0:T(8,128)(2,1)S(1)}, u32[]{:S(2)}, u32[]{:S(2)}) collective-permute-start(bf16[160,576]{1,0:T(8,128)(2,1)S(1)} %collective-permute-done.3.refs_4_), channel_id=1, source_target_pairs={{0,2},{1,3},{2,0},{3,1},{4,6},{5,7},{6,4},{7,5},{8,10},{9,11},{10,... | collective-permute-start | bytes 552968 | tf_op jit(solution)/shard_map/ppermute | solution.py:53
  14.2 2.7 %collective-permute-start.5 = (bf16[160,576]{1,0:T(8,128)(2,1)S(1)}, bf16[160,576]{1,0:T(8,128)(2,1)S(1)}, u32[]{:S(2)}, u32[]{:S(2)}) collective-permute-start(bf16[160,576]{1,0:T(8,128)(2,1)S(1)} %get-tuple-element.21), channel_id=1, source_target_pairs={{0,1},{1,0},{2,3},{3,2},{4,5},{5,4},{6,7},{7,6},{8,9},{9,8},{10,11... | collective-permute-start | bytes 552968 | tf_op jit(solution)/shard_map/ppermute | solution.py:53
  15.5 5.4 %copy-start = (bf16[1,3,128,4608]{3,2,1,0:T(8,128)(2,1)S(1)}, bf16[1,3,128,4608]{3,2,1,0:T(8,128)(2,1)}, u32[]{:S(2)}) copy-start(bf16[1,3,128,4608]{3,2,1,0:T(8,128)(2,1)} %param.9) | copy-start | bytes 10616836
  15.5 1.4 %collective-permute-start.6 = (f32[2,128]{1,0:T(2,128)S(1)}, f32[2,128]{1,0:T(2,128)S(1)}, u32[]{:S(2)}, u32[]{:S(2)}) collective-permute-start(f32[2,128]{1,0:T(2,128)S(1)} %pad_maximum_fusion.refs_8_), channel_id=1, source_target_pairs={{0,1},{1,0},{2,3},{3,2},{4,5},{5,4},{6,7},{7,6},{8,9},{9,8},{10,11... | collective-permute-start | bytes 3080 | tf_op jit(solution)/shard_map/ppermute | solution.py:53
  16.9 1.3 %copy-start.1 = (bf16[1,4608,128]{2,1,0:T(8,128)(2,1)S(1)}, bf16[1,4608,128]{2,1,0:T(8,128)(2,1)}, u32[]{:S(2)}) copy-start(bf16[1,4608,128]{2,1,0:T(8,128)(2,1)} %param.6) | copy-start | bytes 3538948
  21.0 9.6 %collective-permute-start.12 = (bf16[3,128,4608]{2,1,0:T(8,128)(2,1)S(1)}, bf16[3,128,4608]{2,1,0:T(8,128)(2,1)S(1)}, u32[]{:S(2)}, u32[]{:S(2)}) collective-permute-start(bf16[3,128,4608]{2,1,0:T(8,128)(2,1)S(1)} %bitcast.12), channel_id=1, source_target_pairs={{0,1},{1,0},{2,3},{3,2},{4,5},{5,4},{6,7},{7,6},{8,9},{9,8},{10,11... | collective-permute-start | bytes 10616840 | tf_op jit(solution)/shard_map/ppermute | solution.py:53
  21.3 9.3 %collective-permute-start.10 = (bf16[160,256]{1,0:T(8,128)(2,1)S(1)}, bf16[160,256]{1,0:T(8,128)(2,1)S(1)}, u32[]{:S(2)}, u32[]{:S(2)}) collective-permute-start(bf16[160,256]{1,0:T(8,128)(2,1)S(1)} %shard_map.69.refs_0_), channel_id=1, source_target_pairs={{0,16},{8,24},{16,0},{24,8},{1,17},{9,25},{17,1},{25,9},{2,18},{10... | collective-permute-start | bytes 245768 | tf_op jit(solution)/shard_map/ppermute | solution.py:27
  23.9 6.7 %collective-permute-start.9 = (bf16[160,256]{1,0:T(8,128)(2,1)S(1)}, bf16[160,256]{1,0:T(8,128)(2,1)S(1)}, u32[]{:S(2)}, u32[]{:S(2)}) collective-permute-start(bf16[160,256]{1,0:T(8,128)(2,1)S(1)} %shard_map.69.refs_0_), channel_id=1, source_target_pairs={{0,8},{8,16},{16,24},{24,0},{1,9},{9,17},{17,25},{25,1},{2,10},{10... | collective-permute-start | bytes 245768 | tf_op jit(solution)/shard_map/ppermute | solution.py:27
  25.5 1.7 %collective-permute-start.11 = (bf16[160,128]{1,0:T(8,128)(2,1)S(1)}, bf16[160,128]{1,0:T(8,128)(2,1)S(1)}, u32[]{:S(2)}, u32[]{:S(2)}) collective-permute-start(bf16[160,128]{1,0:T(8,128)(2,1)S(1)} %get-tuple-element.43), channel_id=1, source_target_pairs={{0,1},{1,0},{2,3},{3,2},{4,5},{5,4},{6,7},{7,6},{8,9},{9,8},{10,11... | collective-permute-start | bytes 122888 | tf_op jit(solution)/shard_map/ppermute | solution.py:53
  31.2 6.3 %collective-permute-start.19 = (bf16[160,576]{1,0:T(8,128)(2,1)S(1)}, bf16[160,576]{1,0:T(8,128)(2,1)S(1)}, u32[]{:S(2)}, u32[]{:S(2)}) collective-permute-start(bf16[160,576]{1,0:T(8,128)(2,1)S(1)} %get-tuple-element.39), channel_id=1, source_target_pairs={{0,4},{1,5},{2,6},{3,7},{4,0},{5,1},{6,2},{7,3},{8,12},{9,13},{10,... | collective-permute-start | bytes 552968 | tf_op jit(solution)/shard_map/ppermute | solution.py:53
  32.8 5.8 %collective-permute-start.14 = (bf16[160,576]{1,0:T(8,128)(2,1)S(1)}, bf16[160,576]{1,0:T(8,128)(2,1)S(1)}, u32[]{:S(2)}, u32[]{:S(2)}) collective-permute-start(bf16[160,576]{1,0:T(8,128)(2,1)S(1)} %get-tuple-element.31), channel_id=1, source_target_pairs={{0,2},{1,3},{2,0},{3,1},{4,6},{5,7},{6,4},{7,5},{8,10},{9,11},{10,... | collective-permute-start | bytes 552968 | tf_op jit(solution)/shard_map/ppermute | solution.py:53
  34.0 4.7 %collective-permute-start.15 = (bf16[160,576]{1,0:T(8,128)(2,1)S(1)}, bf16[160,576]{1,0:T(8,128)(2,1)S(1)}, u32[]{:S(2)}, u32[]{:S(2)}) collective-permute-start(bf16[160,576]{1,0:T(8,128)(2,1)S(1)} %get-tuple-element.33), channel_id=1, source_target_pairs={{0,1},{1,0},{2,3},{3,2},{4,5},{5,4},{6,7},{7,6},{8,9},{9,8},{10,11... | collective-permute-start | bytes 552968 | tf_op jit(solution)/shard_map/ppermute | solution.py:53
  34.7 6.8 %collective-permute-start.18 = (bf16[160,576]{1,0:T(8,128)(2,1)S(1)}, bf16[160,576]{1,0:T(8,128)(2,1)S(1)}, u32[]{:S(2)}, u32[]{:S(2)}) collective-permute-start(bf16[160,576]{1,0:T(8,128)(2,1)S(1)} %get-tuple-element.37), channel_id=1, source_target_pairs={{0,5},{1,4},{2,7},{3,6},{4,1},{5,0},{6,3},{7,2},{8,13},{9,12},{10,... | collective-permute-start | bytes 552968 | tf_op jit(solution)/shard_map/ppermute | solution.py:53
  35.9 8.0 %collective-permute-start.13 = (bf16[160,576]{1,0:T(8,128)(2,1)S(1)}, bf16[160,576]{1,0:T(8,128)(2,1)S(1)}, u32[]{:S(2)}, u32[]{:S(2)}) collective-permute-start(bf16[160,576]{1,0:T(8,128)(2,1)S(1)} %get-tuple-element.29), channel_id=1, source_target_pairs={{0,2},{1,3},{2,0},{3,1},{4,6},{5,7},{6,4},{7,5},{8,10},{9,11},{10,... | collective-permute-start | bytes 552968 | tf_op jit(solution)/shard_map/ppermute | solution.py:53
  37.6 8.9 %collective-permute-start.20 = (bf16[160,576]{1,0:T(8,128)(2,1)S(1)}, bf16[160,576]{1,0:T(8,128)(2,1)S(1)}, u32[]{:S(2)}, u32[]{:S(2)}) collective-permute-start(bf16[160,576]{1,0:T(8,128)(2,1)S(1)} %shard_map.75), channel_id=1, source_target_pairs={{0,3},{1,2},{2,1},{3,0},{4,7},{5,6},{6,5},{7,4},{8,11},{9,10},{10,... | collective-permute-start | bytes 552968 | tf_op jit(solution)/shard_map/ppermute | solution.py:53
  38.7 6.1 %collective-permute-start.17 = (bf16[80,576]{1,0:T(8,128)(2,1)S(1)}, bf16[80,576]{1,0:T(8,128)(2,1)S(1)}, u32[]{:S(2)}, u32[]{:S(2)}) collective-permute-start(bf16[80,576]{1,0:T(8,128)(2,1)S(1)} %get-tuple-element.36), channel_id=1, source_target_pairs={{0,4},{1,5},{2,6},{3,7},{4,0},{5,1},{6,2},{7,3},{8,12},{9,13},{10,... | collective-permute-start | bytes 276488 | tf_op jit(solution)/shard_map/ppermute | solution.py:53
  39.8 6.7 %collective-permute-start.16 = (bf16[80,576]{1,0:T(8,128)(2,1)S(1)}, bf16[80,576]{1,0:T(8,128)(2,1)S(1)}, u32[]{:S(2)}, u32[]{:S(2)}) collective-permute-start(bf16[80,576]{1,0:T(8,128)(2,1)S(1)} %get-tuple-element.34), channel_id=1, source_target_pairs={{0,4},{1,5},{2,6},{3,7},{4,0},{5,1},{6,2},{7,3},{8,12},{9,13},{10,... | collective-permute-start | bytes 276488 | tf_op jit(solution)/shard_map/ppermute | solution.py:53

commit v7 on v3

--- a/solution.py
+++ b/solution.py
@@ -192,9 +192,9 @@
         enc_sib, gates_sib, dec_sib = (to_peer(value, 1) for value in (encoder, gates, decoder))
         near_sum, *rest = encode_near(near, tuple(far), encoder, enc_sib, gates, gates_sib)
     else:
-        near = {0: mine, 2: to_peer(mine, 2), 3: to_peer(other, 3), 4: to_peer(mine, 4), 5: to_peer(other, 5)}
+        near = {0: mine, 5: to_peer(other, 5), 4: to_peer(mine, 4), 3: to_peer(other, 3), 2: to_peer(mine, 2)}
         enc_sib = to_peer(encoder, 1)
-        far = {6: to_peer(near[2], 4), 7: to_peer(near[5], 2)}
+        far = {7: to_peer(near[5], 2), 6: to_peer(near[2], 4)}
         near[1] = to_peer(after(other, enc_sib), 1)
         gates_sib = to_peer(after(gates, enc_sib), 1)
         near_sum, *rest = encode_near(near, tuple(far), encoder, enc_sib, gates, gates_sib)

time: 47.9 us -> 47.8 us (level)
  waiting for transfers between devices: 19.5 us -> 20.6 us
  starting transfers between devices: 18.7 us -> 17.6 us
    ppermute x18, waiting for transfers between devices: 16.2 us -> 17.3 us  [to_peer(): lax.ppermute(value, 'latent', [(i, i ^ offset) for i in range(lax.axis_si...]
    ppermute x18, starting transfers between devices: 14.4 us -> 13.4 us  [to_peer(): lax.ppermute(value, 'latent', [(i, i ^ offset) for i in range(lax.axis_si...]
where the time goes in v7:
time: 47.8 us; the launch traced here: 47.6 us
  waiting for transfers between devices  20.6 us (43%)
  starting transfers between devices  17.6 us (37%)
  Pallas kernels  4.35 us (9%)
  local copies, waits for them, and re-layouts  2.35 us (5%)
  other arithmetic  1.97 us (4%)
  between operations  0.72 us (2%)
    ppermute x18, waiting for transfers between devices, to_peer(): lax.ppermute(value, 'latent', [(i, i ^ offset) for i in range(lax.axis_si...  17.3 us
    ppermute x18, starting transfers between devices, to_peer(): lax.ppermute(value, 'latent', [(i, i ^ offset) for i in range(lax.axis_si...  13.4 us
    ppermute x2, starting transfers between devices, earlier_layers(): lax.ppermute(value, 'section', [(i, (i + shift) % count) for i in range(c...  4.23 us
    ppermute x2, waiting for transfers between devices, earlier_layers(): lax.ppermute(value, 'section', [(i, (i + shift) % count) for i in range(c...  3.34 us
    pallas_call x4, Pallas kernels, decode_chip(): call(functools.partial(decode_chip_kernel, chip_offset), (shape, shape))  2.51 us
    unnamed x4, local copies, waits for them, and re-layouts  1.28 us
    squeeze x1, local copies, waits for them, and re-layouts, shards(): lax.dynamic_index_in_dim(halves, place + half, 0, keepdims=False)  1.06 us
  transfers between devices with their start and end apart: 20, of which 11 were waited for; matrix products, arithmetic and copies ran while one was open for 6% of the time, Pallas kernels for 6%

profile of v7, /device:TPU:0, one launch (start us, length us, event | category | flops | bytes accessed | tf_op | source)
XLA Modules:
  0.0 47.6 jit_solution(8681093380387912113)
XLA Ops:
  1.1 1.1 %dynamic-slice_bitcast_fusion = (bf16[160,576]{1,0:T(8,128)(2,1)S(1)}, bf16[160,576]{1,0:T(8,128)(2,1)S(1)}) fusion(bf16[8,160,576]{2,1,0:T(8,128)(2,1)} %bitcast.20, s32[]{:T(128)S(6)} %select_n.36, s32[]{:T(128)S(6)} %select_n.35), kind=kLoop, calls=%fused_computation | loop fusion | bytes 737288 | tf_op jit(solution)/shard_map/jit(dynamic_index_in_dim)/squeeze | solution.py:233
  2.2 2.7 %collective-permute-start = (bf16[160,576]{1,0:T(8,128)(2,1)S(1)}, bf16[160,576]{1,0:T(8,128)(2,1)S(1)}, u32[]{:S(2)}, u32[]{:S(2)}) collective-permute-start(bf16[160,576]{1,0:T(8,128)(2,1)S(1)} %get-tuple-element.17), channel_id=1, source_target_pairs={{0,5},{1,4},{2,7},{3,6},{4,1},{5,0},{6,3},{7,2},{8,13},{9,12},{10,... | collective-permute-start | bytes 552968 | tf_op jit(solution)/shard_map/ppermute | solution.py:52
  4.9 1.5 %collective-permute-start.3 = (bf16[160,576]{1,0:T(8,128)(2,1)S(1)}, bf16[160,576]{1,0:T(8,128)(2,1)S(1)}, u32[]{:S(2)}, u32[]{:S(2)}) collective-permute-start(bf16[160,576]{1,0:T(8,128)(2,1)S(1)} %get-tuple-element.33.refs_0_), channel_id=1, source_target_pairs={{0,2},{1,3},{2,0},{3,1},{4,6},{5,7},{6,4},{7,5},{8,10},{9,11},{10,... | collective-permute-start | bytes 552968 | tf_op jit(solution)/shard_map/ppermute | solution.py:52
  6.9 3.4 %collective-permute-done.refs_1_ = bf16[160,576]{1,0:T(8,128)(2,1)S(1)} collective-permute-done((bf16[160,576]{1,0:T(8,128)(2,1)S(1)}, bf16[160,576]{1,0:T(8,128)(2,1)S(1)}, u32[]{:S(2)}, u32[]{:S(2)}) %collective-permute-start) | collective-permute-done | bytes 184352 | tf_op jit(solution)/shard_map/ppermute | solution.py:52
  10.3 1.5 %collective-permute-start.7 = (bf16[160,576]{1,0:T(8,128)(2,1)S(1)}, bf16[160,576]{1,0:T(8,128)(2,1)S(1)}, u32[]{:S(2)}, u32[]{:S(2)}) collective-permute-start(bf16[160,576]{1,0:T(8,128)(2,1)S(1)} %collective-permute-done.refs_1_), channel_id=1, source_target_pairs={{0,2},{1,3},{2,0},{3,1},{4,6},{5,7},{6,4},{7,5},{8,10},{9,11},{10,... | collective-permute-start | bytes 552968 | tf_op jit(solution)/shard_map/ppermute | solution.py:52
  11.8 1.0 %collective-permute-done.3.refs_4_ = bf16[160,576]{1,0:T(8,128)(2,1)S(1)} collective-permute-done((bf16[160,576]{1,0:T(8,128)(2,1)S(1)}, bf16[160,576]{1,0:T(8,128)(2,1)S(1)}, u32[]{:S(2)}, u32[]{:S(2)}) %collective-permute-start.3) | collective-permute-done | bytes 184352 | tf_op jit(solution)/shard_map/ppermute | solution.py:52
  13.1 0.7 %collective-permute-start.5 = (bf16[160,576]{1,0:T(8,128)(2,1)S(1)}, bf16[160,576]{1,0:T(8,128)(2,1)S(1)}, u32[]{:S(2)}, u32[]{:S(2)}) collective-permute-start(bf16[160,576]{1,0:T(8,128)(2,1)S(1)} %get-tuple-element.17), channel_id=1, source_target_pairs={{0,1},{1,0},{2,3},{3,2},{4,5},{5,4},{6,7},{7,6},{8,9},{9,8},{10,11... | collective-permute-start | bytes 552968 | tf_op jit(solution)/shard_map/ppermute | solution.py:52
  13.9 0.7 %add_multiply_fusion = f32[1,128]{1,0:T(1,128)S(1)} fusion(s32[1,128]{1,0:T(1,128)} %param.8), kind=kLoop, calls=%fused_computation.5 | loop fusion | flops 384 | bytes 1024 | tf_op jit(solution)/shard_map/mul | solution.py:234
  14.5 0.7 %pad_maximum_fusion.refs_8_ = f32[2,128]{1,0:T(2,128)S(1)} fusion(f32[1,128]{1,0:T(1,128)S(1)} %add_multiply_fusion, f32[1,128]{1,0:T(1,128)} %param.7), kind=kLoop, calls=%fused_computation.4 | loop fusion | flops 256 | bytes 2048 | tf_op jit(solution)/shard_map/stack | solution.py:235
  15.3 1.0 %collective-permute-done.2.refs_3_ = bf16[160,576]{1,0:T(8,128)(2,1)S(1)} collective-permute-done((bf16[160,576]{1,0:T(8,128)(2,1)S(1)}, bf16[160,576]{1,0:T(8,128)(2,1)S(1)}, u32[]{:S(2)}, u32[]{:S(2)}) %collective-permute-start.2) | collective-permute-done | bytes 184352 | tf_op jit(solution)/shard_map/ppermute | solution.py:52
  16.4 1.3 %copy-done.1 = bf16[1,4608,128]{2,1,0:T(8,128)(2,1)S(1)} copy-done((bf16[1,4608,128]{2,1,0:T(8,128)(2,1)S(1)}, bf16[1,4608,128]{2,1,0:T(8,128)(2,1)}, u32[]{:S(2)}) %copy-start.1) | copy-done | bytes 1179672
  17.7 0.6 %shard_map.68 = (f32[160,256]{1,0:T(8,128)S(1)}, f32[1,256]{1,0:T(1,128)S(1)}, bf16[2,576,256]{2,1,0:T(8,128)(2,1)S(1)}) custom-call(bf16[160,576]{1,0:T(8,128)(2,1)S(1)} %get-tuple-element.33.refs_0_, bf16[160,576]{1,0:T(8,128)(2,1)S(1)} %collective-permute-done.refs_1_, bf16[160,576]{1,0:T(8,128)(2,1)S(1)} %collective-permute-done.1.refs_2_, ...), custom_call_target="tpu_custom_call" | custom-call | flops 283115520 | tf_op jit(solution)/shard_map/pallas_call | solution.py:93
  18.3 2.4 %collective-permute-done.7.refs_0_ = bf16[160,576]{1,0:T(8,128)(2,1)S(1)} collective-permute-done((bf16[160,576]{1,0:T(8,128)(2,1)S(1)}, bf16[160,576]{1,0:T(8,128)(2,1)S(1)}, u32[]{:S(2)}, u32[]{:S(2)}) %collective-permute-start.7) | collective-permute-done | bytes 184352 | tf_op jit(solution)/shard_map/ppermute | solution.py:52
  21.0 2.7 %collective-permute-start.10 = (bf16[160,256]{1,0:T(8,128)(2,1)S(1)}, bf16[160,256]{1,0:T(8,128)(2,1)S(1)}, u32[]{:S(2)}, u32[]{:S(2)}) collective-permute-start(bf16[160,256]{1,0:T(8,128)(2,1)S(1)} %shard_map.69.refs_0_), channel_id=1, source_target_pairs={{0,16},{8,24},{16,0},{24,8},{1,17},{9,25},{17,1},{25,9},{2,18},{10... | collective-permute-start | bytes 245768 | tf_op jit(solution)/shard_map/ppermute | solution.py:26
  23.7 1.6 %collective-permute-start.9 = (bf16[160,256]{1,0:T(8,128)(2,1)S(1)}, bf16[160,256]{1,0:T(8,128)(2,1)S(1)}, u32[]{:S(2)}, u32[]{:S(2)}) collective-permute-start(bf16[160,256]{1,0:T(8,128)(2,1)S(1)} %shard_map.69.refs_0_), channel_id=1, source_target_pairs={{0,8},{8,16},{16,24},{24,0},{1,9},{9,17},{17,25},{25,1},{2,10},{10... | collective-permute-start | bytes 245768 | tf_op jit(solution)/shard_map/ppermute | solution.py:26
  25.3 1.7 %collective-permute-done.11 = bf16[160,128]{1,0:T(8,128)(2,1)S(1)} collective-permute-done((bf16[160,128]{1,0:T(8,128)(2,1)S(1)}, bf16[160,128]{1,0:T(8,128)(2,1)S(1)}, u32[]{:S(2)}, u32[]{:S(2)}) %collective-permute-start.11) | collective-permute-done | bytes 40992 | tf_op jit(solution)/shard_map/ppermute | solution.py:52
  27.0 3.3 %collective-permute-done.10.refs_2_ = bf16[160,256]{1,0:T(8,128)(2,1)S(1)} collective-permute-done((bf16[160,256]{1,0:T(8,128)(2,1)S(1)}, bf16[160,256]{1,0:T(8,128)(2,1)S(1)}, u32[]{:S(2)}, u32[]{:S(2)}) %collective-permute-start.10) | collective-permute-done | bytes 81952 | tf_op jit(solution)/shard_map/ppermute | solution.py:26
  30.3 0.6 %shard_map.73 = (bf16[160,576]{1,0:T(8,128)(2,1)S(1)}, bf16[160,576]{1,0:T(8,128)(2,1)S(1)}) custom-call(bf16[160,256]{1,0:T(8,128)(2,1)S(1)} %shard_map.69.refs_0_, bf16[160,256]{1,0:T(8,128)(2,1)S(1)} %collective-permute-done.9.refs_1_, bf16[160,256]{1,0:T(8,128)(2,1)S(1)} %collective-permute-done.10.refs_2_, bf16[3,128,4608]{2,1,0:T(8,128)(2,1)S(1)} %bitcast.13, ...), custom_call_target="tpu_custom_call" | custom-call | tf_op jit(solution)/shard_map/pallas_call | solution.py:131
  31.0 0.5 %collective-permute-start.17 = (bf16[160,576]{1,0:T(8,128)(2,1)S(1)}, bf16[160,576]{1,0:T(8,128)(2,1)S(1)}, u32[]{:S(2)}, u32[]{:S(2)}) collective-permute-start(bf16[160,576]{1,0:T(8,128)(2,1)S(1)} %get-tuple-element.30), channel_id=1, source_target_pairs={{0,4},{1,5},{2,6},{3,7},{4,0},{5,1},{6,2},{7,3},{8,12},{9,13},{10,... | collective-permute-start | bytes 552968 | tf_op jit(solution)/shard_map/ppermute | solution.py:52
  31.5 1.5 %collective-permute-start.14 = (bf16[160,576]{1,0:T(8,128)(2,1)S(1)}, bf16[160,576]{1,0:T(8,128)(2,1)S(1)}, u32[]{:S(2)}, u32[]{:S(2)}) collective-permute-start(bf16[160,576]{1,0:T(8,128)(2,1)S(1)} %get-tuple-element.27), channel_id=1, source_target_pairs={{0,2},{1,3},{2,0},{3,1},{4,6},{5,7},{6,4},{7,5},{8,10},{9,11},{10,... | collective-permute-start | bytes 552968 | tf_op jit(solution)/shard_map/ppermute | solution.py:52
  33.0 0.6 %shard_map.72 = (bf16[160,576]{1,0:T(8,128)(2,1)S(1)}, bf16[160,576]{1,0:T(8,128)(2,1)S(1)}) custom-call(bf16[160,256]{1,0:T(8,128)(2,1)S(1)} %shard_map.69.refs_0_, bf16[160,256]{1,0:T(8,128)(2,1)S(1)} %collective-permute-done.9.refs_1_, bf16[160,256]{1,0:T(8,128)(2,1)S(1)} %collective-permute-done.10.refs_2_, bf16[3,128,4608]{2,1,0:T(8,128)(2,1)S(1)} %bitcast.14, ...), custom_call_target="tpu_custom_call" | custom-call | tf_op jit(solution)/shard_map/pallas_call | solution.py:131
  33.7 0.6 %shard_map.71 = (bf16[160,576]{1,0:T(8,128)(2,1)S(1)}, bf16[160,576]{1,0:T(8,128)(2,1)S(1)}) custom-call(bf16[160,256]{1,0:T(8,128)(2,1)S(1)} %shard_map.69.refs_0_, bf16[160,256]{1,0:T(8,128)(2,1)S(1)} %collective-permute-done.9.refs_1_, bf16[160,256]{1,0:T(8,128)(2,1)S(1)} %collective-permute-done.10.refs_2_, bf16[3,128,4608]{2,1,0:T(8,128)(2,1)S(1)} %bitcast.15, ...), custom_call_target="tpu_custom_call" | custom-call | tf_op jit(solution)/shard_map/pallas_call | solution.py:131
  34.4 0.6 %collective-permute-start.13 = (bf16[160,576]{1,0:T(8,128)(2,1)S(1)}, bf16[160,576]{1,0:T(8,128)(2,1)S(1)}, u32[]{:S(2)}, u32[]{:S(2)}) collective-permute-start(bf16[160,576]{1,0:T(8,128)(2,1)S(1)} %get-tuple-element.25), channel_id=1, source_target_pairs={{0,2},{1,3},{2,0},{3,1},{4,6},{5,7},{6,4},{7,5},{8,10},{9,11},{10,... | collective-permute-start | bytes 552968 | tf_op jit(solution)/shard_map/ppermute | solution.py:52
  34.9 0.6 %shard_map.70 = (bf16[160,576]{1,0:T(8,128)(2,1)S(1)}, bf16[160,576]{1,0:T(8,128)(2,1)S(1)}) custom-call(bf16[160,256]{1,0:T(8,128)(2,1)S(1)} %shard_map.69.refs_0_, bf16[160,256]{1,0:T(8,128)(2,1)S(1)} %collective-permute-done.9.refs_1_, bf16[160,256]{1,0:T(8,128)(2,1)S(1)} %collective-permute-done.10.refs_2_, bf16[3,128,4608]{2,1,0:T(8,128)(2,1)S(1)} %bitcast.16, ...), custom_call_target="tpu_custom_call" | custom-call | tf_op jit(solution)/shard_map/pallas_call | solution.py:131
  35.6 1.4 %collective-permute-start.16 = (bf16[160,576]{1,0:T(8,128)(2,1)S(1)}, bf16[160,576]{1,0:T(8,128)(2,1)S(1)}, u32[]{:S(2)}, u32[]{:S(2)}) collective-permute-start(bf16[160,576]{1,0:T(8,128)(2,1)S(1)} %get-tuple-element.28), channel_id=1, source_target_pairs={{0,1},{1,0},{2,3},{3,2},{4,5},{5,4},{6,7},{7,6},{8,9},{9,8},{10,11... | collective-permute-start | bytes 552968 | tf_op jit(solution)/shard_map/ppermute | solution.py:52
  37.5 0.7 %collective-permute-start.18 = (bf16[160,576]{1,0:T(8,128)(2,1)S(1)}, bf16[160,576]{1,0:T(8,128)(2,1)S(1)}, u32[]{:S(2)}, u32[]{:S(2)}) collective-permute-start(bf16[160,576]{1,0:T(8,128)(2,1)S(1)} %shard_map.75), channel_id=1, source_target_pairs={{0,3},{1,2},{2,1},{3,0},{4,7},{5,6},{6,5},{7,4},{8,11},{9,10},{10,... | collective-permute-start | bytes 552968 | tf_op jit(solution)/shard_map/ppermute | solution.py:52
  38.3 0.7 %collective-permute-start.15 = (bf16[160,576]{1,0:T(8,128)(2,1)S(1)}, bf16[160,576]{1,0:T(8,128)(2,1)S(1)}, u32[]{:S(2)}, u32[]{:S(2)}) collective-permute-start(bf16[160,576]{1,0:T(8,128)(2,1)S(1)} %shard_map.74), channel_id=1, source_target_pairs={{0,4},{1,5},{2,6},{3,7},{4,0},{5,1},{6,2},{7,3},{8,12},{9,13},{10,... | collective-permute-start | bytes 552968 | tf_op jit(solution)/shard_map/ppermute | solution.py:52
  39.1 0.6 %maximum_select_fusion = bf16[2,160,128]{2,1,0:T(8,128)(2,1)} fusion(bf16[1,160,128]{2,1,0:T(8,128)(2,1)S(1)} %bitcast.22, bf16[1,160,128]{2,1,0:T(8,128)(2,1)S(1)} %get-tuple-element.34, pred[]{:T(512)S(6)} %eq.5), kind=kLoop, calls=%fused_computation.2 | loop fusion | flops 122880 | bytes 163841 | tf_op jit(solution)/shard_map/jit(_where)/select_n | solution.py:238
  39.7 1.5 %collective-permute-done.19.refs_5_ = bf16[160,576]{1,0:T(8,128)(2,1)S(1)} collective-permute-done((bf16[160,576]{1,0:T(8,128)(2,1)S(1)}, bf16[160,576]{1,0:T(8,128)(2,1)S(1)}, u32[]{:S(2)}, u32[]{:S(2)}) %collective-permute-start.19) | collective-permute-done | bytes 184352 | tf_op jit(solution)/shard_map/ppermute | solution.py:52
  41.2 0.6 %collective-permute-done.13.refs_1_ = bf16[160,576]{1,0:T(8,128)(2,1)S(1)} collective-permute-done((bf16[160,576]{1,0:T(8,128)(2,1)S(1)}, bf16[160,576]{1,0:T(8,128)(2,1)S(1)}, u32[]{:S(2)}, u32[]{:S(2)}) %collective-permute-start.13) | collective-permute-done | bytes 184352 | tf_op jit(solution)/shard_map/ppermute | solution.py:52
  41.8 5.0 %collective-permute-done.18.refs_4_ = bf16[160,576]{1,0:T(8,128)(2,1)S(1)} collective-permute-done((bf16[160,576]{1,0:T(8,128)(2,1)S(1)}, bf16[160,576]{1,0:T(8,128)(2,1)S(1)}, u32[]{:S(2)}, u32[]{:S(2)}) %collective-permute-start.18) | collective-permute-done | bytes 184352 | tf_op jit(solution)/shard_map/ppermute | solution.py:52
  46.8 0.8 %shard_map.76 = bf16[320,576]{1,0:T(8,128)(2,1)} custom-call(bf16[160,576]{1,0:T(8,128)(2,1)S(1)} %get-tuple-element.24.refs_0_, bf16[160,576]{1,0:T(8,128)(2,1)S(1)} %collective-permute-done.13.refs_1_, bf16[160,576]{1,0:T(8,128)(2,1)S(1)} %collective-permute-done.15.refs_2_, bf16[160,576]{1,0:T(8,128)(2,1)S(1)} %collective-permute-done.16.refs_3_, ...), custom_call_target="tpu_custom_call" | custom-call | tf_op jit(solution)/shard_map/pallas_call | solution.py:173
  (26 shorter events, 2.5 us)
Async XLA Ops:
  0.6 12.5 %collective-permute-start.4 = (bf16[4608,128]{1,0:T(8,128)(2,1)}, bf16[4608,128]{1,0:T(8,128)(2,1)S(1)}, u32[]{:S(2)}, u32[]{:S(2)}) collective-permute-start(bf16[4608,128]{1,0:T(8,128)(2,1)} %bitcast.17), channel_id=1, source_target_pairs={{0,1},{1,0},{2,3},{3,2},{4,5},{5,4},{6,7},{7,6},{8,9},{9,8},{10,11... | collective-permute-start | bytes 3538952 | tf_op jit(solution)/shard_map/ppermute | solution.py:52
  2.2 8.1 %collective-permute-start = (bf16[160,576]{1,0:T(8,128)(2,1)S(1)}, bf16[160,576]{1,0:T(8,128)(2,1)S(1)}, u32[]{:S(2)}, u32[]{:S(2)}) collective-permute-start(bf16[160,576]{1,0:T(8,128)(2,1)S(1)} %get-tuple-element.17), channel_id=1, source_target_pairs={{0,5},{1,4},{2,7},{3,6},{4,1},{5,0},{6,3},{7,2},{8,13},{9,12},{10,... | collective-permute-start | bytes 552968 | tf_op jit(solution)/shard_map/ppermute | solution.py:52
  4.9 7.9 %collective-permute-start.3 = (bf16[160,576]{1,0:T(8,128)(2,1)S(1)}, bf16[160,576]{1,0:T(8,128)(2,1)S(1)}, u32[]{:S(2)}, u32[]{:S(2)}) collective-permute-start(bf16[160,576]{1,0:T(8,128)(2,1)S(1)} %get-tuple-element.33.refs_0_), channel_id=1, source_target_pairs={{0,2},{1,3},{2,0},{3,1},{4,6},{5,7},{6,4},{7,5},{8,10},{9,11},{10,... | collective-permute-start | bytes 552968 | tf_op jit(solution)/shard_map/ppermute | solution.py:52
  6.4 8.8 %collective-permute-start.1 = (bf16[160,576]{1,0:T(8,128)(2,1)S(1)}, bf16[160,576]{1,0:T(8,128)(2,1)S(1)}, u32[]{:S(2)}, u32[]{:S(2)}) collective-permute-start(bf16[160,576]{1,0:T(8,128)(2,1)S(1)} %get-tuple-element.33.refs_0_), channel_id=1, source_target_pairs={{0,4},{1,5},{2,6},{3,7},{4,0},{5,1},{6,2},{7,3},{8,12},{9,13},{10,... | collective-permute-start | bytes 552968 | tf_op jit(solution)/shard_map/ppermute | solution.py:52
  6.9 9.3 %collective-permute-start.2 = (bf16[160,576]{1,0:T(8,128)(2,1)S(1)}, bf16[160,576]{1,0:T(8,128)(2,1)S(1)}, u32[]{:S(2)}, u32[]{:S(2)}) collective-permute-start(bf16[160,576]{1,0:T(8,128)(2,1)S(1)} %get-tuple-element.17), channel_id=1, source_target_pairs={{0,3},{1,2},{2,1},{3,0},{4,7},{5,6},{6,5},{7,4},{8,11},{9,10},{10,... | collective-permute-start | bytes 552968 | tf_op jit(solution)/shard_map/ppermute | solution.py:52
  10.3 10.4 %collective-permute-start.7 = (bf16[160,576]{1,0:T(8,128)(2,1)S(1)}, bf16[160,576]{1,0:T(8,128)(2,1)S(1)}, u32[]{:S(2)}, u32[]{:S(2)}) collective-permute-start(bf16[160,576]{1,0:T(8,128)(2,1)S(1)} %collective-permute-done.refs_1_), channel_id=1, source_target_pairs={{0,2},{1,3},{2,0},{3,1},{4,6},{5,7},{6,4},{7,5},{8,10},{9,11},{10,... | collective-permute-start | bytes 552968 | tf_op jit(solution)/shard_map/ppermute | solution.py:52
  12.8 7.9 %collective-permute-start.8 = (bf16[160,576]{1,0:T(8,128)(2,1)S(1)}, bf16[160,576]{1,0:T(8,128)(2,1)S(1)}, u32[]{:S(2)}, u32[]{:S(2)}) collective-permute-start(bf16[160,576]{1,0:T(8,128)(2,1)S(1)} %collective-permute-done.3.refs_4_), channel_id=1, source_target_pairs={{0,4},{1,5},{2,6},{3,7},{4,0},{5,1},{6,2},{7,3},{8,12},{9,13},{10,... | collective-permute-start | bytes 552968 | tf_op jit(solution)/shard_map/ppermute | solution.py:52
  13.1 3.3 %collective-permute-start.5 = (bf16[160,576]{1,0:T(8,128)(2,1)S(1)}, bf16[160,576]{1,0:T(8,128)(2,1)S(1)}, u32[]{:S(2)}, u32[]{:S(2)}) collective-permute-start(bf16[160,576]{1,0:T(8,128)(2,1)S(1)} %get-tuple-element.17), channel_id=1, source_target_pairs={{0,1},{1,0},{2,3},{3,2},{4,5},{5,4},{6,7},{7,6},{8,9},{9,8},{10,11... | collective-permute-start | bytes 552968 | tf_op jit(solution)/shard_map/ppermute | solution.py:52
  15.2 5.5 %copy-start = (bf16[1,3,128,4608]{3,2,1,0:T(8,128)(2,1)S(1)}, bf16[1,3,128,4608]{3,2,1,0:T(8,128)(2,1)}, u32[]{:S(2)}) copy-start(bf16[1,3,128,4608]{3,2,1,0:T(8,128)(2,1)} %param.9) | copy-start | bytes 10616836
  15.2 1.2 %collective-permute-start.6 = (f32[2,128]{1,0:T(2,128)S(1)}, f32[2,128]{1,0:T(2,128)S(1)}, u32[]{:S(2)}, u32[]{:S(2)}) collective-permute-start(f32[2,128]{1,0:T(2,128)S(1)} %pad_maximum_fusion.refs_8_), channel_id=1, source_target_pairs={{0,1},{1,0},{2,3},{3,2},{4,5},{5,4},{6,7},{7,6},{8,9},{9,8},{10,11... | collective-permute-start | bytes 3080 | tf_op jit(solution)/shard_map/ppermute | solution.py:52
  16.4 1.3 %copy-start.1 = (bf16[1,4608,128]{2,1,0:T(8,128)(2,1)S(1)}, bf16[1,4608,128]{2,1,0:T(8,128)(2,1)}, u32[]{:S(2)}) copy-start(bf16[1,4608,128]{2,1,0:T(8,128)(2,1)} %param.6) | copy-start | bytes 3538948
  20.7 9.6 %collective-permute-start.12 = (bf16[3,128,4608]{2,1,0:T(8,128)(2,1)S(1)}, bf16[3,128,4608]{2,1,0:T(8,128)(2,1)S(1)}, u32[]{:S(2)}, u32[]{:S(2)}) collective-permute-start(bf16[3,128,4608]{2,1,0:T(8,128)(2,1)S(1)} %bitcast.12), channel_id=1, source_target_pairs={{0,1},{1,0},{2,3},{3,2},{4,5},{5,4},{6,7},{7,6},{8,9},{9,8},{10,11... | collective-permute-start | bytes 10616840 | tf_op jit(solution)/shard_map/ppermute | solution.py:52
  21.0 9.3 %collective-permute-start.10 = (bf16[160,256]{1,0:T(8,128)(2,1)S(1)}, bf16[160,256]{1,0:T(8,128)(2,1)S(1)}, u32[]{:S(2)}, u32[]{:S(2)}) collective-permute-start(bf16[160,256]{1,0:T(8,128)(2,1)S(1)} %shard_map.69.refs_0_), channel_id=1, source_target_pairs={{0,16},{8,24},{16,0},{24,8},{1,17},{9,25},{17,1},{25,9},{2,18},{10... | collective-permute-start | bytes 245768 | tf_op jit(solution)/shard_map/ppermute | solution.py:26
  23.7 6.7 %collective-permute-start.9 = (bf16[160,256]{1,0:T(8,128)(2,1)S(1)}, bf16[160,256]{1,0:T(8,128)(2,1)S(1)}, u32[]{:S(2)}, u32[]{:S(2)}) collective-permute-start(bf16[160,256]{1,0:T(8,128)(2,1)S(1)} %shard_map.69.refs_0_), channel_id=1, source_target_pairs={{0,8},{8,16},{16,24},{24,0},{1,9},{9,17},{17,25},{25,1},{2,10},{10... | collective-permute-start | bytes 245768 | tf_op jit(solution)/shard_map/ppermute | solution.py:26
  25.3 1.7 %collective-permute-start.11 = (bf16[160,128]{1,0:T(8,128)(2,1)S(1)}, bf16[160,128]{1,0:T(8,128)(2,1)S(1)}, u32[]{:S(2)}, u32[]{:S(2)}) collective-permute-start(bf16[160,128]{1,0:T(8,128)(2,1)S(1)} %get-tuple-element.35), channel_id=1, source_target_pairs={{0,1},{1,0},{2,3},{3,2},{4,5},{5,4},{6,7},{7,6},{8,9},{9,8},{10,11... | collective-permute-start | bytes 122888 | tf_op jit(solution)/shard_map/ppermute | solution.py:52
  31.0 6.5 %collective-permute-start.17 = (bf16[160,576]{1,0:T(8,128)(2,1)S(1)}, bf16[160,576]{1,0:T(8,128)(2,1)S(1)}, u32[]{:S(2)}, u32[]{:S(2)}) collective-permute-start(bf16[160,576]{1,0:T(8,128)(2,1)S(1)} %get-tuple-element.30), channel_id=1, source_target_pairs={{0,4},{1,5},{2,6},{3,7},{4,0},{5,1},{6,2},{7,3},{8,12},{9,13},{10,... | collective-permute-start | bytes 552968 | tf_op jit(solution)/shard_map/ppermute | solution.py:52
  31.5 6.8 %collective-permute-start.14 = (bf16[160,576]{1,0:T(8,128)(2,1)S(1)}, bf16[160,576]{1,0:T(8,128)(2,1)S(1)}, u32[]{:S(2)}, u32[]{:S(2)}) collective-permute-start(bf16[160,576]{1,0:T(8,128)(2,1)S(1)} %get-tuple-element.27), channel_id=1, source_target_pairs={{0,2},{1,3},{2,0},{3,1},{4,6},{5,7},{6,4},{7,5},{8,10},{9,11},{10,... | collective-permute-start | bytes 552968 | tf_op jit(solution)/shard_map/ppermute | solution.py:52
  33.7 7.5 %collective-permute-start.19 = (bf16[160,576]{1,0:T(8,128)(2,1)S(1)}, bf16[160,576]{1,0:T(8,128)(2,1)S(1)}, u32[]{:S(2)}, u32[]{:S(2)}) collective-permute-start(bf16[160,576]{1,0:T(8,128)(2,1)S(1)} %get-tuple-element.31), channel_id=1, source_target_pairs={{0,5},{1,4},{2,7},{3,6},{4,1},{5,0},{6,3},{7,2},{8,13},{9,12},{10,... | collective-permute-start | bytes 552968 | tf_op jit(solution)/shard_map/ppermute | solution.py:52
  34.4 7.4 %collective-permute-start.13 = (bf16[160,576]{1,0:T(8,128)(2,1)S(1)}, bf16[160,576]{1,0:T(8,128)(2,1)S(1)}, u32[]{:S(2)}, u32[]{:S(2)}) collective-permute-start(bf16[160,576]{1,0:T(8,128)(2,1)S(1)} %get-tuple-element.25), channel_id=1, source_target_pairs={{0,2},{1,3},{2,0},{3,1},{4,6},{5,7},{6,4},{7,5},{8,10},{9,11},{10,... | collective-permute-start | bytes 552968 | tf_op jit(solution)/shard_map/ppermute | solution.py:52
  35.6 6.3 %collective-permute-start.16 = (bf16[160,576]{1,0:T(8,128)(2,1)S(1)}, bf16[160,576]{1,0:T(8,128)(2,1)S(1)}, u32[]{:S(2)}, u32[]{:S(2)}) collective-permute-start(bf16[160,576]{1,0:T(8,128)(2,1)S(1)} %get-tuple-element.28), channel_id=1, source_target_pairs={{0,1},{1,0},{2,3},{3,2},{4,5},{5,4},{6,7},{7,6},{8,9},{9,8},{10,11... | collective-permute-start | bytes 552968 | tf_op jit(solution)/shard_map/ppermute | solution.py:52
  37.5 9.3 %collective-permute-start.18 = (bf16[160,576]{1,0:T(8,128)(2,1)S(1)}, bf16[160,576]{1,0:T(8,128)(2,1)S(1)}, u32[]{:S(2)}, u32[]{:S(2)}) collective-permute-start(bf16[160,576]{1,0:T(8,128)(2,1)S(1)} %shard_map.75), channel_id=1, source_target_pairs={{0,3},{1,2},{2,1},{3,0},{4,7},{5,6},{6,5},{7,4},{8,11},{9,10},{10,... | collective-permute-start | bytes 552968 | tf_op jit(solution)/shard_map/ppermute | solution.py:52
  38.3 8.5 %collective-permute-start.15 = (bf16[160,576]{1,0:T(8,128)(2,1)S(1)}, bf16[160,576]{1,0:T(8,128)(2,1)S(1)}, u32[]{:S(2)}, u32[]{:S(2)}) collective-permute-start(bf16[160,576]{1,0:T(8,128)(2,1)S(1)} %shard_map.74), channel_id=1, source_target_pairs={{0,4},{1,5},{2,6},{3,7},{4,0},{5,1},{6,2},{7,3},{8,12},{9,13},{10,... | collective-permute-start | bytes 552968 | tf_op jit(solution)/shard_map/ppermute | solution.py:52

commit v8 on v7

--- a/solution.py
+++ b/solution.py
@@ -217,7 +217,7 @@
     own_same, own_cross = decode_chip(0, acts, own, sib, width)
     y_sum, x_sum = sum_two(y_same, for_y), sum_two(x_cross, for_x)
     from_y_same, from_x_cross = to_peer(y_sum, 4), to_peer(x_sum, 3)
-    from_sib = to_peer(own_cross, 1)
+    from_sib = to_peer(after(own_cross, for_x), 1)
     return finish((own_same, from_x_same, from_y_same), (from_sib, from_x_cross, from_y_cross), dtype)
 
 

time: 47.8 us -> 48.2 us (level)
  waiting for transfers between devices: 20.6 us -> 21.5 us
  starting transfers between devices: 17.6 us -> 17.1 us
    ppermute x18, waiting for transfers between devices: 17.3 us -> 18.2 us  [to_peer(): lax.ppermute(value, 'latent', [(i, i ^ offset) for i in range(lax.axis_si...]
    ppermute x18, starting transfers between devices: 13.4 us -> 12.8 us  [to_peer(): lax.ppermute(value, 'latent', [(i, i ^ offset) for i in range(lax.axis_si...]
where the time goes in v8:
time: 48.2 us; the launch traced here: 48 us
  waiting for transfers between devices  21.5 us (45%)
  starting transfers between devices  17.1 us (35%)
  Pallas kernels  4.35 us (9%)
  local copies, waits for them, and re-layouts  2.35 us (5%)
  other arithmetic  1.97 us (4%)
  between operations  0.71 us (1%)
    ppermute x18, waiting for transfers between devices, to_peer(): lax.ppermute(value, 'latent', [(i, i ^ offset) for i in range(lax.axis_si...  18.2 us
    ppermute x18, starting transfers between devices, to_peer(): lax.ppermute(value, 'latent', [(i, i ^ offset) for i in range(lax.axis_si...  12.8 us
    ppermute x2, starting transfers between devices, earlier_layers(): lax.ppermute(value, 'section', [(i, (i + shift) % count) for i in range(c...  4.23 us
    ppermute x2, waiting for transfers between devices, earlier_layers(): lax.ppermute(value, 'section', [(i, (i + shift) % count) for i in range(c...  3.34 us
    pallas_call x4, Pallas kernels, decode_chip(): call(functools.partial(decode_chip_kernel, chip_offset), (shape, shape))  2.51 us
    unnamed x4, local copies, waits for them, and re-layouts  1.27 us
    squeeze x1, local copies, waits for them, and re-layouts, shards(): lax.dynamic_index_in_dim(halves, place + half, 0, keepdims=False)  1.06 us
  transfers between devices with their start and end apart: 20, of which 11 were waited for; matrix products, arithmetic and copies ran while one was open for 6% of the time, Pallas kernels for 6%

profile of v8, /device:TPU:0, one launch (start us, length us, event | category | flops | bytes accessed | tf_op | source)
XLA Modules:
  0.0 48.0 jit_solution(9525138275574453625)
XLA Ops:
  1.1 1.1 %dynamic-slice_bitcast_fusion = (bf16[160,576]{1,0:T(8,128)(2,1)S(1)}, bf16[160,576]{1,0:T(8,128)(2,1)S(1)}) fusion(bf16[8,160,576]{2,1,0:T(8,128)(2,1)} %bitcast.20, s32[]{:T(128)S(6)} %select_n.36, s32[]{:T(128)S(6)} %select_n.35), kind=kLoop, calls=%fused_computation | loop fusion | bytes 737288 | tf_op jit(solution)/shard_map/jit(dynamic_index_in_dim)/squeeze | solution.py:233
  2.2 2.7 %collective-permute-start = (bf16[160,576]{1,0:T(8,128)(2,1)S(1)}, bf16[160,576]{1,0:T(8,128)(2,1)S(1)}, u32[]{:S(2)}, u32[]{:S(2)}) collective-permute-start(bf16[160,576]{1,0:T(8,128)(2,1)S(1)} %get-tuple-element.18), channel_id=1, source_target_pairs={{0,5},{1,4},{2,7},{3,6},{4,1},{5,0},{6,3},{7,2},{8,13},{9,12},{10,... | collective-permute-start | bytes 552968 | tf_op jit(solution)/shard_map/ppermute | solution.py:52
  4.9 1.5 %collective-permute-start.3 = (bf16[160,576]{1,0:T(8,128)(2,1)S(1)}, bf16[160,576]{1,0:T(8,128)(2,1)S(1)}, u32[]{:S(2)}, u32[]{:S(2)}) collective-permute-start(bf16[160,576]{1,0:T(8,128)(2,1)S(1)} %get-tuple-element.35.refs_0_), channel_id=1, source_target_pairs={{0,2},{1,3},{2,0},{3,1},{4,6},{5,7},{6,4},{7,5},{8,10},{9,11},{10,... | collective-permute-start | bytes 552968 | tf_op jit(solution)/shard_map/ppermute | solution.py:52
  6.9 3.4 %collective-permute-done.refs_1_ = bf16[160,576]{1,0:T(8,128)(2,1)S(1)} collective-permute-done((bf16[160,576]{1,0:T(8,128)(2,1)S(1)}, bf16[160,576]{1,0:T(8,128)(2,1)S(1)}, u32[]{:S(2)}, u32[]{:S(2)}) %collective-permute-start) | collective-permute-done | bytes 184352 | tf_op jit(solution)/shard_map/ppermute | solution.py:52
  10.3 1.5 %collective-permute-start.7 = (bf16[160,576]{1,0:T(8,128)(2,1)S(1)}, bf16[160,576]{1,0:T(8,128)(2,1)S(1)}, u32[]{:S(2)}, u32[]{:S(2)}) collective-permute-start(bf16[160,576]{1,0:T(8,128)(2,1)S(1)} %collective-permute-done.refs_1_), channel_id=1, source_target_pairs={{0,2},{1,3},{2,0},{3,1},{4,6},{5,7},{6,4},{7,5},{8,10},{9,11},{10,... | collective-permute-start | bytes 552968 | tf_op jit(solution)/shard_map/ppermute | solution.py:52
  11.8 1.0 %collective-permute-done.3.refs_4_ = bf16[160,576]{1,0:T(8,128)(2,1)S(1)} collective-permute-done((bf16[160,576]{1,0:T(8,128)(2,1)S(1)}, bf16[160,576]{1,0:T(8,128)(2,1)S(1)}, u32[]{:S(2)}, u32[]{:S(2)}) %collective-permute-start.3) | collective-permute-done | bytes 184352 | tf_op jit(solution)/shard_map/ppermute | solution.py:52
  13.1 0.7 %collective-permute-start.5 = (bf16[160,576]{1,0:T(8,128)(2,1)S(1)}, bf16[160,576]{1,0:T(8,128)(2,1)S(1)}, u32[]{:S(2)}, u32[]{:S(2)}) collective-permute-start(bf16[160,576]{1,0:T(8,128)(2,1)S(1)} %get-tuple-element.18), channel_id=1, source_target_pairs={{0,1},{1,0},{2,3},{3,2},{4,5},{5,4},{6,7},{7,6},{8,9},{9,8},{10,11... | collective-permute-start | bytes 552968 | tf_op jit(solution)/shard_map/ppermute | solution.py:52
  13.9 0.7 %add_multiply_fusion = f32[1,128]{1,0:T(1,128)S(1)} fusion(s32[1,128]{1,0:T(1,128)} %param.8), kind=kLoop, calls=%fused_computation.5 | loop fusion | flops 384 | bytes 1024 | tf_op jit(solution)/shard_map/mul | solution.py:234
  14.5 0.7 %pad_maximum_fusion.refs_8_ = f32[2,128]{1,0:T(2,128)S(1)} fusion(f32[1,128]{1,0:T(1,128)S(1)} %add_multiply_fusion, f32[1,128]{1,0:T(1,128)} %param.7), kind=kLoop, calls=%fused_computation.4 | loop fusion | flops 256 | bytes 2048 | tf_op jit(solution)/shard_map/stack | solution.py:235
  15.2 1.1 %collective-permute-done.2.refs_3_ = bf16[160,576]{1,0:T(8,128)(2,1)S(1)} collective-permute-done((bf16[160,576]{1,0:T(8,128)(2,1)S(1)}, bf16[160,576]{1,0:T(8,128)(2,1)S(1)}, u32[]{:S(2)}, u32[]{:S(2)}) %collective-permute-start.2) | collective-permute-done | bytes 184352 | tf_op jit(solution)/shard_map/ppermute | solution.py:52
  16.2 1.1 %collective-permute-start.6 = (f32[2,128]{1,0:T(2,128)S(1)}, f32[2,128]{1,0:T(2,128)S(1)}, u32[]{:S(2)}, u32[]{:S(2)}) collective-permute-start(f32[2,128]{1,0:T(2,128)S(1)} %pad_maximum_fusion.refs_8_), channel_id=1, source_target_pairs={{0,1},{1,0},{2,3},{3,2},{4,5},{5,4},{6,7},{7,6},{8,9},{9,8},{10,11... | collective-permute-start | bytes 3080 | tf_op jit(solution)/shard_map/ppermute | solution.py:52
  17.4 0.8 %collective-permute-done.6.refs_9_ = f32[2,128]{1,0:T(2,128)S(1)} collective-permute-done((f32[2,128]{1,0:T(2,128)S(1)}, f32[2,128]{1,0:T(2,128)S(1)}, u32[]{:S(2)}, u32[]{:S(2)}) %collective-permute-start.6) | collective-permute-done | bytes 1056 | tf_op jit(solution)/shard_map/ppermute | solution.py:52
  18.2 1.3 %copy-done.1 = bf16[1,4608,128]{2,1,0:T(8,128)(2,1)S(1)} copy-done((bf16[1,4608,128]{2,1,0:T(8,128)(2,1)S(1)}, bf16[1,4608,128]{2,1,0:T(8,128)(2,1)}, u32[]{:S(2)}) %copy-start.1) | copy-done | bytes 1179672
  19.4 0.6 %shard_map.68 = (f32[160,256]{1,0:T(8,128)S(1)}, f32[1,256]{1,0:T(1,128)S(1)}, bf16[2,576,256]{2,1,0:T(8,128)(2,1)S(1)}) custom-call(bf16[160,576]{1,0:T(8,128)(2,1)S(1)} %get-tuple-element.35.refs_0_, bf16[160,576]{1,0:T(8,128)(2,1)S(1)} %collective-permute-done.refs_1_, bf16[160,576]{1,0:T(8,128)(2,1)S(1)} %collective-permute-done.1.refs_2_, ...), custom_call_target="tpu_custom_call" | custom-call | flops 283115520 | tf_op jit(solution)/shard_map/pallas_call | solution.py:93
  20.1 0.7 %collective-permute-done.7.refs_0_ = bf16[160,576]{1,0:T(8,128)(2,1)S(1)} collective-permute-done((bf16[160,576]{1,0:T(8,128)(2,1)S(1)}, bf16[160,576]{1,0:T(8,128)(2,1)S(1)}, u32[]{:S(2)}, u32[]{:S(2)}) %collective-permute-start.7) | collective-permute-done | bytes 184352 | tf_op jit(solution)/shard_map/ppermute | solution.py:52
  21.0 2.7 %collective-permute-start.10 = (bf16[160,256]{1,0:T(8,128)(2,1)S(1)}, bf16[160,256]{1,0:T(8,128)(2,1)S(1)}, u32[]{:S(2)}, u32[]{:S(2)}) collective-permute-start(bf16[160,256]{1,0:T(8,128)(2,1)S(1)} %shard_map.69.refs_0_), channel_id=1, source_target_pairs={{0,16},{8,24},{16,0},{24,8},{1,17},{9,25},{17,1},{25,9},{2,18},{10... | collective-permute-start | bytes 245768 | tf_op jit(solution)/shard_map/ppermute | solution.py:26
  23.7 1.6 %collective-permute-start.9 = (bf16[160,256]{1,0:T(8,128)(2,1)S(1)}, bf16[160,256]{1,0:T(8,128)(2,1)S(1)}, u32[]{:S(2)}, u32[]{:S(2)}) collective-permute-start(bf16[160,256]{1,0:T(8,128)(2,1)S(1)} %shard_map.69.refs_0_), channel_id=1, source_target_pairs={{0,8},{8,16},{16,24},{24,0},{1,9},{9,17},{17,25},{25,1},{2,10},{10... | collective-permute-start | bytes 245768 | tf_op jit(solution)/shard_map/ppermute | solution.py:26
  25.3 1.7 %collective-permute-done.11 = bf16[160,128]{1,0:T(8,128)(2,1)S(1)} collective-permute-done((bf16[160,128]{1,0:T(8,128)(2,1)S(1)}, bf16[160,128]{1,0:T(8,128)(2,1)S(1)}, u32[]{:S(2)}, u32[]{:S(2)}) %collective-permute-start.11) | collective-permute-done | bytes 40992 | tf_op jit(solution)/shard_map/ppermute | solution.py:52
  27.0 3.3 %collective-permute-done.10.refs_2_ = bf16[160,256]{1,0:T(8,128)(2,1)S(1)} collective-permute-done((bf16[160,256]{1,0:T(8,128)(2,1)S(1)}, bf16[160,256]{1,0:T(8,128)(2,1)S(1)}, u32[]{:S(2)}, u32[]{:S(2)}) %collective-permute-start.10) | collective-permute-done | bytes 81952 | tf_op jit(solution)/shard_map/ppermute | solution.py:26
  30.3 0.6 %shard_map.73 = (bf16[160,576]{1,0:T(8,128)(2,1)S(1)}, bf16[160,576]{1,0:T(8,128)(2,1)S(1)}) custom-call(bf16[160,256]{1,0:T(8,128)(2,1)S(1)} %shard_map.69.refs_0_, bf16[160,256]{1,0:T(8,128)(2,1)S(1)} %collective-permute-done.9.refs_1_, bf16[160,256]{1,0:T(8,128)(2,1)S(1)} %collective-permute-done.10.refs_2_, bf16[3,128,4608]{2,1,0:T(8,128)(2,1)S(1)} %bitcast.13, ...), custom_call_target="tpu_custom_call" | custom-call | tf_op jit(solution)/shard_map/pallas_call | solution.py:131
  31.0 1.6 %collective-permute-start.14 = (bf16[160,576]{1,0:T(8,128)(2,1)S(1)}, bf16[160,576]{1,0:T(8,128)(2,1)S(1)}, u32[]{:S(2)}, u32[]{:S(2)}) collective-permute-start(bf16[160,576]{1,0:T(8,128)(2,1)S(1)} %get-tuple-element.28), channel_id=1, source_target_pairs={{0,2},{1,3},{2,0},{3,1},{4,6},{5,7},{6,4},{7,5},{8,10},{9,11},{10,... | collective-permute-start | bytes 552968 | tf_op jit(solution)/shard_map/ppermute | solution.py:52
  33.0 0.6 %shard_map.72 = (bf16[160,576]{1,0:T(8,128)(2,1)S(1)}, bf16[160,576]{1,0:T(8,128)(2,1)S(1)}) custom-call(bf16[160,256]{1,0:T(8,128)(2,1)S(1)} %shard_map.69.refs_0_, bf16[160,256]{1,0:T(8,128)(2,1)S(1)} %collective-permute-done.9.refs_1_, bf16[160,256]{1,0:T(8,128)(2,1)S(1)} %collective-permute-done.10.refs_2_, bf16[3,128,4608]{2,1,0:T(8,128)(2,1)S(1)} %bitcast.14, ...), custom_call_target="tpu_custom_call" | custom-call | tf_op jit(solution)/shard_map/pallas_call | solution.py:131
  33.7 0.6 %shard_map.71 = (bf16[160,576]{1,0:T(8,128)(2,1)S(1)}, bf16[160,576]{1,0:T(8,128)(2,1)S(1)}) custom-call(bf16[160,256]{1,0:T(8,128)(2,1)S(1)} %shard_map.69.refs_0_, bf16[160,256]{1,0:T(8,128)(2,1)S(1)} %collective-permute-done.9.refs_1_, bf16[160,256]{1,0:T(8,128)(2,1)S(1)} %collective-permute-done.10.refs_2_, bf16[3,128,4608]{2,1,0:T(8,128)(2,1)S(1)} %bitcast.15, ...), custom_call_target="tpu_custom_call" | custom-call | tf_op jit(solution)/shard_map/pallas_call | solution.py:131
  34.4 0.6 %collective-permute-start.13 = (bf16[160,576]{1,0:T(8,128)(2,1)S(1)}, bf16[160,576]{1,0:T(8,128)(2,1)S(1)}, u32[]{:S(2)}, u32[]{:S(2)}) collective-permute-start(bf16[160,576]{1,0:T(8,128)(2,1)S(1)} %get-tuple-element.26), channel_id=1, source_target_pairs={{0,2},{1,3},{2,0},{3,1},{4,6},{5,7},{6,4},{7,5},{8,10},{9,11},{10,... | collective-permute-start | bytes 552968 | tf_op jit(solution)/shard_map/ppermute | solution.py:52
  34.9 0.6 %shard_map.70 = (bf16[160,576]{1,0:T(8,128)(2,1)S(1)}, bf16[160,576]{1,0:T(8,128)(2,1)S(1)}) custom-call(bf16[160,256]{1,0:T(8,128)(2,1)S(1)} %shard_map.69.refs_0_, bf16[160,256]{1,0:T(8,128)(2,1)S(1)} %collective-permute-done.9.refs_1_, bf16[160,256]{1,0:T(8,128)(2,1)S(1)} %collective-permute-done.10.refs_2_, bf16[3,128,4608]{2,1,0:T(8,128)(2,1)S(1)} %bitcast.16, ...), custom_call_target="tpu_custom_call" | custom-call | tf_op jit(solution)/shard_map/pallas_call | solution.py:131
  35.6 1.6 %collective-permute-done.14.b_ref = bf16[160,576]{1,0:T(8,128)(2,1)S(1)} collective-permute-done((bf16[160,576]{1,0:T(8,128)(2,1)S(1)}, bf16[160,576]{1,0:T(8,128)(2,1)S(1)}, u32[]{:S(2)}, u32[]{:S(2)}) %collective-permute-start.14) | collective-permute-done | bytes 184352 | tf_op jit(solution)/shard_map/ppermute | solution.py:52
  37.2 0.6 %collective-permute-start.15 = (bf16[160,576]{1,0:T(8,128)(2,1)S(1)}, bf16[160,576]{1,0:T(8,128)(2,1)S(1)}, u32[]{:S(2)}, u32[]{:S(2)}) collective-permute-start(bf16[160,576]{1,0:T(8,128)(2,1)S(1)} %shard_map.74), channel_id=1, source_target_pairs={{0,4},{1,5},{2,6},{3,7},{4,0},{5,1},{6,2},{7,3},{8,12},{9,13},{10,... | collective-permute-start | bytes 552968 | tf_op jit(solution)/shard_map/ppermute | solution.py:52
  37.8 2.2 %collective-permute-done.16.b_ref = bf16[160,576]{1,0:T(8,128)(2,1)S(1)} collective-permute-done((bf16[160,576]{1,0:T(8,128)(2,1)S(1)}, bf16[160,576]{1,0:T(8,128)(2,1)S(1)}, u32[]{:S(2)}, u32[]{:S(2)}) %collective-permute-start.16) | collective-permute-done | bytes 184352 | tf_op jit(solution)/shard_map/ppermute | solution.py:52
  40.1 0.7 %collective-permute-start.17 = (bf16[160,576]{1,0:T(8,128)(2,1)S(1)}, bf16[160,576]{1,0:T(8,128)(2,1)S(1)}, u32[]{:S(2)}, u32[]{:S(2)}) collective-permute-start(bf16[160,576]{1,0:T(8,128)(2,1)S(1)} %get-tuple-element.31), channel_id=1, source_target_pairs={{0,1},{1,0},{2,3},{3,2},{4,5},{5,4},{6,7},{7,6},{8,9},{9,8},{10,11... | collective-permute-start | bytes 552968 | tf_op jit(solution)/shard_map/ppermute | solution.py:52
  40.8 0.6 %maximum_select_fusion = bf16[2,160,128]{2,1,0:T(8,128)(2,1)} fusion(bf16[1,160,128]{2,1,0:T(8,128)(2,1)S(1)} %bitcast.22, bf16[1,160,128]{2,1,0:T(8,128)(2,1)S(1)} %get-tuple-element.36, pred[]{:T(512)S(6)} %eq.5), kind=kLoop, calls=%fused_computation.2 | loop fusion | flops 122880 | bytes 163841 | tf_op jit(solution)/shard_map/jit(_where)/select_n | solution.py:238
  41.8 5.3 %collective-permute-done.15.refs_2_ = bf16[160,576]{1,0:T(8,128)(2,1)S(1)} collective-permute-done((bf16[160,576]{1,0:T(8,128)(2,1)S(1)}, bf16[160,576]{1,0:T(8,128)(2,1)S(1)}, u32[]{:S(2)}, u32[]{:S(2)}) %collective-permute-start.15) | collective-permute-done | bytes 184352 | tf_op jit(solution)/shard_map/ppermute | solution.py:52
  47.1 0.9 %shard_map.76 = bf16[320,576]{1,0:T(8,128)(2,1)} custom-call(bf16[160,576]{1,0:T(8,128)(2,1)S(1)} %get-tuple-element.25.refs_0_, bf16[160,576]{1,0:T(8,128)(2,1)S(1)} %collective-permute-done.13.refs_1_, bf16[160,576]{1,0:T(8,128)(2,1)S(1)} %collective-permute-done.15.refs_2_, bf16[160,576]{1,0:T(8,128)(2,1)S(1)} %collective-permute-done.17.refs_3_, ...), custom_call_target="tpu_custom_call" | custom-call | tf_op jit(solution)/shard_map/pallas_call | solution.py:173
  (26 shorter events, 2.7 us)
Async XLA Ops:
  0.6 12.5 %collective-permute-start.4 = (bf16[4608,128]{1,0:T(8,128)(2,1)}, bf16[4608,128]{1,0:T(8,128)(2,1)S(1)}, u32[]{:S(2)}, u32[]{:S(2)}) collective-permute-start(bf16[4608,128]{1,0:T(8,128)(2,1)} %bitcast.17), channel_id=1, source_target_pairs={{0,1},{1,0},{2,3},{3,2},{4,5},{5,4},{6,7},{7,6},{8,9},{9,8},{10,11... | collective-permute-start | bytes 3538952 | tf_op jit(solution)/shard_map/ppermute | solution.py:52
  2.2 8.1 %collective-permute-start = (bf16[160,576]{1,0:T(8,128)(2,1)S(1)}, bf16[160,576]{1,0:T(8,128)(2,1)S(1)}, u32[]{:S(2)}, u32[]{:S(2)}) collective-permute-start(bf16[160,576]{1,0:T(8,128)(2,1)S(1)} %get-tuple-element.18), channel_id=1, source_target_pairs={{0,5},{1,4},{2,7},{3,6},{4,1},{5,0},{6,3},{7,2},{8,13},{9,12},{10,... | collective-permute-start | bytes 552968 | tf_op jit(solution)/shard_map/ppermute | solution.py:52
  4.9 7.9 %collective-permute-start.3 = (bf16[160,576]{1,0:T(8,128)(2,1)S(1)}, bf16[160,576]{1,0:T(8,128)(2,1)S(1)}, u32[]{:S(2)}, u32[]{:S(2)}) collective-permute-start(bf16[160,576]{1,0:T(8,128)(2,1)S(1)} %get-tuple-element.35.refs_0_), channel_id=1, source_target_pairs={{0,2},{1,3},{2,0},{3,1},{4,6},{5,7},{6,4},{7,5},{8,10},{9,11},{10,... | collective-permute-start | bytes 552968 | tf_op jit(solution)/shard_map/ppermute | solution.py:52
  6.4 9.8 %collective-permute-start.2 = (bf16[160,576]{1,0:T(8,128)(2,1)S(1)}, bf16[160,576]{1,0:T(8,128)(2,1)S(1)}, u32[]{:S(2)}, u32[]{:S(2)}) collective-permute-start(bf16[160,576]{1,0:T(8,128)(2,1)S(1)} %get-tuple-element.18), channel_id=1, source_target_pairs={{0,3},{1,2},{2,1},{3,0},{4,7},{5,6},{6,5},{7,4},{8,11},{9,10},{10,... | collective-permute-start | bytes 552968 | tf_op jit(solution)/shard_map/ppermute | solution.py:52
  6.4 10.9 %collective-permute-start.1 = (bf16[160,576]{1,0:T(8,128)(2,1)S(1)}, bf16[160,576]{1,0:T(8,128)(2,1)S(1)}, u32[]{:S(2)}, u32[]{:S(2)}) collective-permute-start(bf16[160,576]{1,0:T(8,128)(2,1)S(1)} %get-tuple-element.35.refs_0_), channel_id=1, source_target_pairs={{0,4},{1,5},{2,6},{3,7},{4,0},{5,1},{6,2},{7,3},{8,12},{9,13},{10,... | collective-permute-start | bytes 552968 | tf_op jit(solution)/shard_map/ppermute | solution.py:52
  10.3 10.4 %collective-permute-start.7 = (bf16[160,576]{1,0:T(8,128)(2,1)S(1)}, bf16[160,576]{1,0:T(8,128)(2,1)S(1)}, u32[]{:S(2)}, u32[]{:S(2)}) collective-permute-start(bf16[160,576]{1,0:T(8,128)(2,1)S(1)} %collective-permute-done.refs_1_), channel_id=1, source_target_pairs={{0,2},{1,3},{2,0},{3,1},{4,6},{5,7},{6,4},{7,5},{8,10},{9,11},{10,... | collective-permute-start | bytes 552968 | tf_op jit(solution)/shard_map/ppermute | solution.py:52
  12.8 7.9 %collective-permute-start.8 = (bf16[160,576]{1,0:T(8,128)(2,1)S(1)}, bf16[160,576]{1,0:T(8,128)(2,1)S(1)}, u32[]{:S(2)}, u32[]{:S(2)}) collective-permute-start(bf16[160,576]{1,0:T(8,128)(2,1)S(1)} %collective-permute-done.3.refs_4_), channel_id=1, source_target_pairs={{0,4},{1,5},{2,6},{3,7},{4,0},{5,1},{6,2},{7,3},{8,12},{9,13},{10,... | collective-permute-start | bytes 552968 | tf_op jit(solution)/shard_map/ppermute | solution.py:52
  13.1 5.1 %collective-permute-start.5 = (bf16[160,576]{1,0:T(8,128)(2,1)S(1)}, bf16[160,576]{1,0:T(8,128)(2,1)S(1)}, u32[]{:S(2)}, u32[]{:S(2)}) collective-permute-start(bf16[160,576]{1,0:T(8,128)(2,1)S(1)} %get-tuple-element.18), channel_id=1, source_target_pairs={{0,1},{1,0},{2,3},{3,2},{4,5},{5,4},{6,7},{7,6},{8,9},{9,8},{10,11... | collective-permute-start | bytes 552968 | tf_op jit(solution)/shard_map/ppermute | solution.py:52
  15.2 5.5 %copy-start = (bf16[1,3,128,4608]{3,2,1,0:T(8,128)(2,1)S(1)}, bf16[1,3,128,4608]{3,2,1,0:T(8,128)(2,1)}, u32[]{:S(2)}) copy-start(bf16[1,3,128,4608]{3,2,1,0:T(8,128)(2,1)} %param.9) | copy-start | bytes 10616836
  16.2 1.9 %collective-permute-start.6 = (f32[2,128]{1,0:T(2,128)S(1)}, f32[2,128]{1,0:T(2,128)S(1)}, u32[]{:S(2)}, u32[]{:S(2)}) collective-permute-start(f32[2,128]{1,0:T(2,128)S(1)} %pad_maximum_fusion.refs_8_), channel_id=1, source_target_pairs={{0,1},{1,0},{2,3},{3,2},{4,5},{5,4},{6,7},{7,6},{8,9},{9,8},{10,11... | collective-permute-start | bytes 3080 | tf_op jit(solution)/shard_map/ppermute | solution.py:52
  18.2 1.3 %copy-start.1 = (bf16[1,4608,128]{2,1,0:T(8,128)(2,1)S(1)}, bf16[1,4608,128]{2,1,0:T(8,128)(2,1)}, u32[]{:S(2)}) copy-start(bf16[1,4608,128]{2,1,0:T(8,128)(2,1)} %param.6) | copy-start | bytes 3538948
  20.7 9.6 %collective-permute-start.12 = (bf16[3,128,4608]{2,1,0:T(8,128)(2,1)S(1)}, bf16[3,128,4608]{2,1,0:T(8,128)(2,1)S(1)}, u32[]{:S(2)}, u32[]{:S(2)}) collective-permute-start(bf16[3,128,4608]{2,1,0:T(8,128)(2,1)S(1)} %bitcast.12), channel_id=1, source_target_pairs={{0,1},{1,0},{2,3},{3,2},{4,5},{5,4},{6,7},{7,6},{8,9},{9,8},{10,11... | collective-permute-start | bytes 10616840 | tf_op jit(solution)/shard_map/ppermute | solution.py:52
  21.0 9.3 %collective-permute-start.10 = (bf16[160,256]{1,0:T(8,128)(2,1)S(1)}, bf16[160,256]{1,0:T(8,128)(2,1)S(1)}, u32[]{:S(2)}, u32[]{:S(2)}) collective-permute-start(bf16[160,256]{1,0:T(8,128)(2,1)S(1)} %shard_map.69.refs_0_), channel_id=1, source_target_pairs={{0,16},{8,24},{16,0},{24,8},{1,17},{9,25},{17,1},{25,9},{2,18},{10... | collective-permute-start | bytes 245768 | tf_op jit(solution)/shard_map/ppermute | solution.py:26
  23.7 6.7 %collective-permute-start.9 = (bf16[160,256]{1,0:T(8,128)(2,1)S(1)}, bf16[160,256]{1,0:T(8,128)(2,1)S(1)}, u32[]{:S(2)}, u32[]{:S(2)}) collective-permute-start(bf16[160,256]{1,0:T(8,128)(2,1)S(1)} %shard_map.69.refs_0_), channel_id=1, source_target_pairs={{0,8},{8,16},{16,24},{24,0},{1,9},{9,17},{17,25},{25,1},{2,10},{10... | collective-permute-start | bytes 245768 | tf_op jit(solution)/shard_map/ppermute | solution.py:26
  25.3 1.7 %collective-permute-start.11 = (bf16[160,128]{1,0:T(8,128)(2,1)S(1)}, bf16[160,128]{1,0:T(8,128)(2,1)S(1)}, u32[]{:S(2)}, u32[]{:S(2)}) collective-permute-start(bf16[160,128]{1,0:T(8,128)(2,1)S(1)} %get-tuple-element.37), channel_id=1, source_target_pairs={{0,1},{1,0},{2,3},{3,2},{4,5},{5,4},{6,7},{7,6},{8,9},{9,8},{10,11... | collective-permute-start | bytes 122888 | tf_op jit(solution)/shard_map/ppermute | solution.py:52
  31.0 6.1 %collective-permute-start.14 = (bf16[160,576]{1,0:T(8,128)(2,1)S(1)}, bf16[160,576]{1,0:T(8,128)(2,1)S(1)}, u32[]{:S(2)}, u32[]{:S(2)}) collective-permute-start(bf16[160,576]{1,0:T(8,128)(2,1)S(1)} %get-tuple-element.28), channel_id=1, source_target_pairs={{0,2},{1,3},{2,0},{3,1},{4,6},{5,7},{6,4},{7,5},{8,10},{9,11},{10,... | collective-permute-start | bytes 552968 | tf_op jit(solution)/shard_map/ppermute | solution.py:52
  32.5 7.5 %collective-permute-start.16 = (bf16[160,576]{1,0:T(8,128)(2,1)S(1)}, bf16[160,576]{1,0:T(8,128)(2,1)S(1)}, u32[]{:S(2)}, u32[]{:S(2)}) collective-permute-start(bf16[160,576]{1,0:T(8,128)(2,1)S(1)} %get-tuple-element.30), channel_id=1, source_target_pairs={{0,4},{1,5},{2,6},{3,7},{4,0},{5,1},{6,2},{7,3},{8,12},{9,13},{10,... | collective-permute-start | bytes 552968 | tf_op jit(solution)/shard_map/ppermute | solution.py:52
  33.7 7.8 %collective-permute-start.19 = (bf16[160,576]{1,0:T(8,128)(2,1)S(1)}, bf16[160,576]{1,0:T(8,128)(2,1)S(1)}, u32[]{:S(2)}, u32[]{:S(2)}) collective-permute-start(bf16[160,576]{1,0:T(8,128)(2,1)S(1)} %get-tuple-element.33), channel_id=1, source_target_pairs={{0,5},{1,4},{2,7},{3,6},{4,1},{5,0},{6,3},{7,2},{8,13},{9,12},{10,... | collective-permute-start | bytes 552968 | tf_op jit(solution)/shard_map/ppermute | solution.py:52
  34.4 7.4 %collective-permute-start.13 = (bf16[160,576]{1,0:T(8,128)(2,1)S(1)}, bf16[160,576]{1,0:T(8,128)(2,1)S(1)}, u32[]{:S(2)}, u32[]{:S(2)}) collective-permute-start(bf16[160,576]{1,0:T(8,128)(2,1)S(1)} %get-tuple-element.26), channel_id=1, source_target_pairs={{0,2},{1,3},{2,0},{3,1},{4,6},{5,7},{6,4},{7,5},{8,10},{9,11},{10,... | collective-permute-start | bytes 552968 | tf_op jit(solution)/shard_map/ppermute | solution.py:52
  37.2 9.9 %collective-permute-start.15 = (bf16[160,576]{1,0:T(8,128)(2,1)S(1)}, bf16[160,576]{1,0:T(8,128)(2,1)S(1)}, u32[]{:S(2)}, u32[]{:S(2)}) collective-permute-start(bf16[160,576]{1,0:T(8,128)(2,1)S(1)} %shard_map.74), channel_id=1, source_target_pairs={{0,4},{1,5},{2,6},{3,7},{4,0},{5,1},{6,2},{7,3},{8,12},{9,13},{10,... | collective-permute-start | bytes 552968 | tf_op jit(solution)/shard_map/ppermute | solution.py:52
  40.1 7.1 %collective-permute-start.18 = (bf16[160,576]{1,0:T(8,128)(2,1)S(1)}, bf16[160,576]{1,0:T(8,128)(2,1)S(1)}, u32[]{:S(2)}, u32[]{:S(2)}) collective-permute-start(bf16[160,576]{1,0:T(8,128)(2,1)S(1)} %shard_map.75), channel_id=1, source_target_pairs={{0,3},{1,2},{2,1},{3,0},{4,7},{5,6},{6,5},{7,4},{8,11},{9,10},{10,... | collective-permute-start | bytes 552968 | tf_op jit(solution)/shard_map/ppermute | solution.py:52
  40.1 7.0 %collective-permute-start.17 = (bf16[160,576]{1,0:T(8,128)(2,1)S(1)}, bf16[160,576]{1,0:T(8,128)(2,1)S(1)}, u32[]{:S(2)}, u32[]{:S(2)}) collective-permute-start(bf16[160,576]{1,0:T(8,128)(2,1)S(1)} %get-tuple-element.31), channel_id=1, source_target_pairs={{0,1},{1,0},{2,3},{3,2},{4,5},{5,4},{6,7},{7,6},{8,9},{9,8},{10,11... | collective-permute-start | bytes 552968 | tf_op jit(solution)/shard_map/ppermute | solution.py:52

commit v9 on v7

--- a/solution.py
+++ b/solution.py
@@ -121,9 +121,16 @@
     columns = pl.ds(pl.multiple_of(((place // 2) ^ chip_offset) * (2 * width), 128), 2 * width)
     total = decoded(acts, own_ref, sib_ref, columns).astype(jnp.bfloat16)
     low, high = total[:, :width], total[:, width:]
-    first_core = place % 2 == 0
-    same_ref[...] = jnp.where(first_core, low, high)
-    cross_ref[...] = jnp.where(first_core, high, low)
+
+    @pl.when(place % 2 == 0)
+    def _():
+        same_ref[...] = low
+        cross_ref[...] = high
+
+    @pl.when(place % 2 == 1)
+    def _():
+        same_ref[...] = high
+        cross_ref[...] = low
 
 
 def decode_chip(chip_offset, acts, own, sib, width):

time: 47.8 us -> 47.8 us (level)
  no operation moved by 1% of the time
where the time goes in v9:
time: 47.8 us; the launch traced here: 47.7 us
  waiting for transfers between devices  20.6 us (43%)
  starting transfers between devices  17.7 us (37%)
  Pallas kernels  4.36 us (9%)
  local copies, waits for them, and re-layouts  2.35 us (5%)
  other arithmetic  1.97 us (4%)
  between operations  0.74 us (2%)
    ppermute x18, waiting for transfers between devices, to_peer(): lax.ppermute(value, 'latent', [(i, i ^ offset) for i in range(lax.axis_si...  17.2 us
    ppermute x18, starting transfers between devices, to_peer(): lax.ppermute(value, 'latent', [(i, i ^ offset) for i in range(lax.axis_si...  13.4 us
    ppermute x2, starting transfers between devices, earlier_layers(): lax.ppermute(value, 'section', [(i, (i + shift) % count) for i in range(c...  4.23 us
    ppermute x2, waiting for transfers between devices, earlier_layers(): lax.ppermute(value, 'section', [(i, (i + shift) % count) for i in range(c...  3.34 us
    pallas_call x4, Pallas kernels, decode_chip(): call(functools.partial(decode_chip_kernel, chip_offset), (shape, shape))  2.52 us
    unnamed x4, local copies, waits for them, and re-layouts  1.28 us
    squeeze x1, local copies, waits for them, and re-layouts, shards(): lax.dynamic_index_in_dim(halves, place + half, 0, keepdims=False)  1.06 us
  transfers between devices with their start and end apart: 20, of which 11 were waited for; matrix products, arithmetic and copies ran while one was open for 6% of the time, Pallas kernels for 6%

profile of v9, /device:TPU:0, one launch (start us, length us, event | category | flops | bytes accessed | tf_op | source)
XLA Modules:
  0.0 47.7 jit_solution(15841218707022010267)
XLA Ops:
  1.1 1.1 %dynamic-slice_bitcast_fusion = (bf16[160,576]{1,0:T(8,128)(2,1)S(1)}, bf16[160,576]{1,0:T(8,128)(2,1)S(1)}) fusion(bf16[8,160,576]{2,1,0:T(8,128)(2,1)} %bitcast.20, s32[]{:T(128)S(6)} %select_n.36, s32[]{:T(128)S(6)} %select_n.35), kind=kLoop, calls=%fused_computation | loop fusion | bytes 737288 | tf_op jit(solution)/shard_map/jit(dynamic_index_in_dim)/squeeze | solution.py:240
  2.2 2.7 %collective-permute-start = (bf16[160,576]{1,0:T(8,128)(2,1)S(1)}, bf16[160,576]{1,0:T(8,128)(2,1)S(1)}, u32[]{:S(2)}, u32[]{:S(2)}) collective-permute-start(bf16[160,576]{1,0:T(8,128)(2,1)S(1)} %get-tuple-element.17), channel_id=1, source_target_pairs={{0,5},{1,4},{2,7},{3,6},{4,1},{5,0},{6,3},{7,2},{8,13},{9,12},{10,... | collective-permute-start | bytes 552968 | tf_op jit(solution)/shard_map/ppermute | solution.py:52
  4.9 1.5 %collective-permute-start.3 = (bf16[160,576]{1,0:T(8,128)(2,1)S(1)}, bf16[160,576]{1,0:T(8,128)(2,1)S(1)}, u32[]{:S(2)}, u32[]{:S(2)}) collective-permute-start(bf16[160,576]{1,0:T(8,128)(2,1)S(1)} %get-tuple-element.33.refs_0_), channel_id=1, source_target_pairs={{0,2},{1,3},{2,0},{3,1},{4,6},{5,7},{6,4},{7,5},{8,10},{9,11},{10,... | collective-permute-start | bytes 552968 | tf_op jit(solution)/shard_map/ppermute | solution.py:52
  6.9 3.4 %collective-permute-done.refs_1_ = bf16[160,576]{1,0:T(8,128)(2,1)S(1)} collective-permute-done((bf16[160,576]{1,0:T(8,128)(2,1)S(1)}, bf16[160,576]{1,0:T(8,128)(2,1)S(1)}, u32[]{:S(2)}, u32[]{:S(2)}) %collective-permute-start) | collective-permute-done | bytes 184352 | tf_op jit(solution)/shard_map/ppermute | solution.py:52
  10.3 1.5 %collective-permute-start.7 = (bf16[160,576]{1,0:T(8,128)(2,1)S(1)}, bf16[160,576]{1,0:T(8,128)(2,1)S(1)}, u32[]{:S(2)}, u32[]{:S(2)}) collective-permute-start(bf16[160,576]{1,0:T(8,128)(2,1)S(1)} %collective-permute-done.refs_1_), channel_id=1, source_target_pairs={{0,2},{1,3},{2,0},{3,1},{4,6},{5,7},{6,4},{7,5},{8,10},{9,11},{10,... | collective-permute-start | bytes 552968 | tf_op jit(solution)/shard_map/ppermute | solution.py:52
  11.8 1.0 %collective-permute-done.3.refs_4_ = bf16[160,576]{1,0:T(8,128)(2,1)S(1)} collective-permute-done((bf16[160,576]{1,0:T(8,128)(2,1)S(1)}, bf16[160,576]{1,0:T(8,128)(2,1)S(1)}, u32[]{:S(2)}, u32[]{:S(2)}) %collective-permute-start.3) | collective-permute-done | bytes 184352 | tf_op jit(solution)/shard_map/ppermute | solution.py:52
  13.1 0.7 %collective-permute-start.5 = (bf16[160,576]{1,0:T(8,128)(2,1)S(1)}, bf16[160,576]{1,0:T(8,128)(2,1)S(1)}, u32[]{:S(2)}, u32[]{:S(2)}) collective-permute-start(bf16[160,576]{1,0:T(8,128)(2,1)S(1)} %get-tuple-element.17), channel_id=1, source_target_pairs={{0,1},{1,0},{2,3},{3,2},{4,5},{5,4},{6,7},{7,6},{8,9},{9,8},{10,11... | collective-permute-start | bytes 552968 | tf_op jit(solution)/shard_map/ppermute | solution.py:52
  13.9 0.7 %add_multiply_fusion = f32[1,128]{1,0:T(1,128)S(1)} fusion(s32[1,128]{1,0:T(1,128)} %param.8), kind=kLoop, calls=%fused_computation.5 | loop fusion | flops 384 | bytes 1024 | tf_op jit(solution)/shard_map/mul | solution.py:241
  14.5 0.7 %pad_maximum_fusion.refs_8_ = f32[2,128]{1,0:T(2,128)S(1)} fusion(f32[1,128]{1,0:T(1,128)S(1)} %add_multiply_fusion, f32[1,128]{1,0:T(1,128)} %param.7), kind=kLoop, calls=%fused_computation.4 | loop fusion | flops 256 | bytes 2048 | tf_op jit(solution)/shard_map/stack | solution.py:242
  15.3 1.0 %collective-permute-done.2.refs_3_ = bf16[160,576]{1,0:T(8,128)(2,1)S(1)} collective-permute-done((bf16[160,576]{1,0:T(8,128)(2,1)S(1)}, bf16[160,576]{1,0:T(8,128)(2,1)S(1)}, u32[]{:S(2)}, u32[]{:S(2)}) %collective-permute-start.2) | collective-permute-done | bytes 184352 | tf_op jit(solution)/shard_map/ppermute | solution.py:52
  16.4 1.3 %copy-done.1 = bf16[1,4608,128]{2,1,0:T(8,128)(2,1)S(1)} copy-done((bf16[1,4608,128]{2,1,0:T(8,128)(2,1)S(1)}, bf16[1,4608,128]{2,1,0:T(8,128)(2,1)}, u32[]{:S(2)}) %copy-start.1) | copy-done | bytes 1179672
  17.7 0.6 %shard_map.68 = (f32[160,256]{1,0:T(8,128)S(1)}, f32[1,256]{1,0:T(1,128)S(1)}, bf16[2,576,256]{2,1,0:T(8,128)(2,1)S(1)}) custom-call(bf16[160,576]{1,0:T(8,128)(2,1)S(1)} %get-tuple-element.33.refs_0_, bf16[160,576]{1,0:T(8,128)(2,1)S(1)} %collective-permute-done.refs_1_, bf16[160,576]{1,0:T(8,128)(2,1)S(1)} %collective-permute-done.1.refs_2_, ...), custom_call_target="tpu_custom_call" | custom-call | flops 283115520 | tf_op jit(solution)/shard_map/pallas_call | solution.py:93
  18.3 2.4 %collective-permute-done.7.refs_0_ = bf16[160,576]{1,0:T(8,128)(2,1)S(1)} collective-permute-done((bf16[160,576]{1,0:T(8,128)(2,1)S(1)}, bf16[160,576]{1,0:T(8,128)(2,1)S(1)}, u32[]{:S(2)}, u32[]{:S(2)}) %collective-permute-start.7) | collective-permute-done | bytes 184352 | tf_op jit(solution)/shard_map/ppermute | solution.py:52
  21.0 2.7 %collective-permute-start.10 = (bf16[160,256]{1,0:T(8,128)(2,1)S(1)}, bf16[160,256]{1,0:T(8,128)(2,1)S(1)}, u32[]{:S(2)}, u32[]{:S(2)}) collective-permute-start(bf16[160,256]{1,0:T(8,128)(2,1)S(1)} %shard_map.69.refs_0_), channel_id=1, source_target_pairs={{0,16},{8,24},{16,0},{24,8},{1,17},{9,25},{17,1},{25,9},{2,18},{10... | collective-permute-start | bytes 245768 | tf_op jit(solution)/shard_map/ppermute | solution.py:26
  23.7 1.6 %collective-permute-start.9 = (bf16[160,256]{1,0:T(8,128)(2,1)S(1)}, bf16[160,256]{1,0:T(8,128)(2,1)S(1)}, u32[]{:S(2)}, u32[]{:S(2)}) collective-permute-start(bf16[160,256]{1,0:T(8,128)(2,1)S(1)} %shard_map.69.refs_0_), channel_id=1, source_target_pairs={{0,8},{8,16},{16,24},{24,0},{1,9},{9,17},{17,25},{25,1},{2,10},{10... | collective-permute-start | bytes 245768 | tf_op jit(solution)/shard_map/ppermute | solution.py:26
  25.3 1.7 %collective-permute-done.11 = bf16[160,128]{1,0:T(8,128)(2,1)S(1)} collective-permute-done((bf16[160,128]{1,0:T(8,128)(2,1)S(1)}, bf16[160,128]{1,0:T(8,128)(2,1)S(1)}, u32[]{:S(2)}, u32[]{:S(2)}) %collective-permute-start.11) | collective-permute-done | bytes 40992 | tf_op jit(solution)/shard_map/ppermute | solution.py:52
  27.0 3.3 %collective-permute-done.10.refs_2_ = bf16[160,256]{1,0:T(8,128)(2,1)S(1)} collective-permute-done((bf16[160,256]{1,0:T(8,128)(2,1)S(1)}, bf16[160,256]{1,0:T(8,128)(2,1)S(1)}, u32[]{:S(2)}, u32[]{:S(2)}) %collective-permute-start.10) | collective-permute-done | bytes 81952 | tf_op jit(solution)/shard_map/ppermute | solution.py:26
  30.3 0.6 %shard_map.73 = (bf16[160,576]{1,0:T(8,128)(2,1)S(1)}, bf16[160,576]{1,0:T(8,128)(2,1)S(1)}) custom-call(bf16[160,256]{1,0:T(8,128)(2,1)S(1)} %shard_map.69.refs_0_, bf16[160,256]{1,0:T(8,128)(2,1)S(1)} %collective-permute-done.9.refs_1_, bf16[160,256]{1,0:T(8,128)(2,1)S(1)} %collective-permute-done.10.refs_2_, bf16[3,128,4608]{2,1,0:T(8,128)(2,1)S(1)} %bitcast.13, ...), custom_call_target="tpu_custom_call" | custom-call | tf_op jit(solution)/shard_map/pallas_call | solution.py:138
  31.0 0.5 %collective-permute-start.17 = (bf16[160,576]{1,0:T(8,128)(2,1)S(1)}, bf16[160,576]{1,0:T(8,128)(2,1)S(1)}, u32[]{:S(2)}, u32[]{:S(2)}) collective-permute-start(bf16[160,576]{1,0:T(8,128)(2,1)S(1)} %get-tuple-element.30), channel_id=1, source_target_pairs={{0,4},{1,5},{2,6},{3,7},{4,0},{5,1},{6,2},{7,3},{8,12},{9,13},{10,... | collective-permute-start | bytes 552968 | tf_op jit(solution)/shard_map/ppermute | solution.py:52
  31.5 1.5 %collective-permute-start.14 = (bf16[160,576]{1,0:T(8,128)(2,1)S(1)}, bf16[160,576]{1,0:T(8,128)(2,1)S(1)}, u32[]{:S(2)}, u32[]{:S(2)}) collective-permute-start(bf16[160,576]{1,0:T(8,128)(2,1)S(1)} %get-tuple-element.27), channel_id=1, source_target_pairs={{0,2},{1,3},{2,0},{3,1},{4,6},{5,7},{6,4},{7,5},{8,10},{9,11},{10,... | collective-permute-start | bytes 552968 | tf_op jit(solution)/shard_map/ppermute | solution.py:52
  33.0 0.6 %shard_map.72 = (bf16[160,576]{1,0:T(8,128)(2,1)S(1)}, bf16[160,576]{1,0:T(8,128)(2,1)S(1)}) custom-call(bf16[160,256]{1,0:T(8,128)(2,1)S(1)} %shard_map.69.refs_0_, bf16[160,256]{1,0:T(8,128)(2,1)S(1)} %collective-permute-done.9.refs_1_, bf16[160,256]{1,0:T(8,128)(2,1)S(1)} %collective-permute-done.10.refs_2_, bf16[3,128,4608]{2,1,0:T(8,128)(2,1)S(1)} %bitcast.14, ...), custom_call_target="tpu_custom_call" | custom-call | tf_op jit(solution)/shard_map/pallas_call | solution.py:138
  33.8 0.6 %shard_map.71 = (bf16[160,576]{1,0:T(8,128)(2,1)S(1)}, bf16[160,576]{1,0:T(8,128)(2,1)S(1)}) custom-call(bf16[160,256]{1,0:T(8,128)(2,1)S(1)} %shard_map.69.refs_0_, bf16[160,256]{1,0:T(8,128)(2,1)S(1)} %collective-permute-done.9.refs_1_, bf16[160,256]{1,0:T(8,128)(2,1)S(1)} %collective-permute-done.10.refs_2_, bf16[3,128,4608]{2,1,0:T(8,128)(2,1)S(1)} %bitcast.15, ...), custom_call_target="tpu_custom_call" | custom-call | tf_op jit(solution)/shard_map/pallas_call | solution.py:138
  34.4 0.6 %collective-permute-start.13 = (bf16[160,576]{1,0:T(8,128)(2,1)S(1)}, bf16[160,576]{1,0:T(8,128)(2,1)S(1)}, u32[]{:S(2)}, u32[]{:S(2)}) collective-permute-start(bf16[160,576]{1,0:T(8,128)(2,1)S(1)} %get-tuple-element.25), channel_id=1, source_target_pairs={{0,2},{1,3},{2,0},{3,1},{4,6},{5,7},{6,4},{7,5},{8,10},{9,11},{10,... | collective-permute-start | bytes 552968 | tf_op jit(solution)/shard_map/ppermute | solution.py:52
  35.0 0.6 %shard_map.70 = (bf16[160,576]{1,0:T(8,128)(2,1)S(1)}, bf16[160,576]{1,0:T(8,128)(2,1)S(1)}) custom-call(bf16[160,256]{1,0:T(8,128)(2,1)S(1)} %shard_map.69.refs_0_, bf16[160,256]{1,0:T(8,128)(2,1)S(1)} %collective-permute-done.9.refs_1_, bf16[160,256]{1,0:T(8,128)(2,1)S(1)} %collective-permute-done.10.refs_2_, bf16[3,128,4608]{2,1,0:T(8,128)(2,1)S(1)} %bitcast.16, ...), custom_call_target="tpu_custom_call" | custom-call | tf_op jit(solution)/shard_map/pallas_call | solution.py:138
  35.6 1.4 %collective-permute-start.16 = (bf16[160,576]{1,0:T(8,128)(2,1)S(1)}, bf16[160,576]{1,0:T(8,128)(2,1)S(1)}, u32[]{:S(2)}, u32[]{:S(2)}) collective-permute-start(bf16[160,576]{1,0:T(8,128)(2,1)S(1)} %get-tuple-element.28), channel_id=1, source_target_pairs={{0,1},{1,0},{2,3},{3,2},{4,5},{5,4},{6,7},{7,6},{8,9},{9,8},{10,11... | collective-permute-start | bytes 552968 | tf_op jit(solution)/shard_map/ppermute | solution.py:52
  37.5 0.8 %collective-permute-start.18 = (bf16[160,576]{1,0:T(8,128)(2,1)S(1)}, bf16[160,576]{1,0:T(8,128)(2,1)S(1)}, u32[]{:S(2)}, u32[]{:S(2)}) collective-permute-start(bf16[160,576]{1,0:T(8,128)(2,1)S(1)} %shard_map.75), channel_id=1, source_target_pairs={{0,3},{1,2},{2,1},{3,0},{4,7},{5,6},{6,5},{7,4},{8,11},{9,10},{10,... | collective-permute-start | bytes 552968 | tf_op jit(solution)/shard_map/ppermute | solution.py:52
  38.3 0.8 %collective-permute-start.15 = (bf16[160,576]{1,0:T(8,128)(2,1)S(1)}, bf16[160,576]{1,0:T(8,128)(2,1)S(1)}, u32[]{:S(2)}, u32[]{:S(2)}) collective-permute-start(bf16[160,576]{1,0:T(8,128)(2,1)S(1)} %shard_map.74), channel_id=1, source_target_pairs={{0,4},{1,5},{2,6},{3,7},{4,0},{5,1},{6,2},{7,3},{8,12},{9,13},{10,... | collective-permute-start | bytes 552968 | tf_op jit(solution)/shard_map/ppermute | solution.py:52
  39.1 0.6 %maximum_select_fusion = bf16[2,160,128]{2,1,0:T(8,128)(2,1)} fusion(bf16[1,160,128]{2,1,0:T(8,128)(2,1)S(1)} %bitcast.22, bf16[1,160,128]{2,1,0:T(8,128)(2,1)S(1)} %get-tuple-element.34, pred[]{:T(512)S(6)} %eq.5), kind=kLoop, calls=%fused_computation.2 | loop fusion | flops 122880 | bytes 163841 | tf_op jit(solution)/shard_map/jit(_where)/select_n | solution.py:245
  39.7 1.4 %collective-permute-done.19.refs_5_ = bf16[160,576]{1,0:T(8,128)(2,1)S(1)} collective-permute-done((bf16[160,576]{1,0:T(8,128)(2,1)S(1)}, bf16[160,576]{1,0:T(8,128)(2,1)S(1)}, u32[]{:S(2)}, u32[]{:S(2)}) %collective-permute-start.19) | collective-permute-done | bytes 184352 | tf_op jit(solution)/shard_map/ppermute | solution.py:52
  41.2 0.7 %collective-permute-done.13.refs_1_ = bf16[160,576]{1,0:T(8,128)(2,1)S(1)} collective-permute-done((bf16[160,576]{1,0:T(8,128)(2,1)S(1)}, bf16[160,576]{1,0:T(8,128)(2,1)S(1)}, u32[]{:S(2)}, u32[]{:S(2)}) %collective-permute-start.13) | collective-permute-done | bytes 184352 | tf_op jit(solution)/shard_map/ppermute | solution.py:52
  41.8 5.0 %collective-permute-done.18.refs_4_ = bf16[160,576]{1,0:T(8,128)(2,1)S(1)} collective-permute-done((bf16[160,576]{1,0:T(8,128)(2,1)S(1)}, bf16[160,576]{1,0:T(8,128)(2,1)S(1)}, u32[]{:S(2)}, u32[]{:S(2)}) %collective-permute-start.18) | collective-permute-done | bytes 184352 | tf_op jit(solution)/shard_map/ppermute | solution.py:52
  46.8 0.8 %shard_map.76 = bf16[320,576]{1,0:T(8,128)(2,1)} custom-call(bf16[160,576]{1,0:T(8,128)(2,1)S(1)} %get-tuple-element.24.refs_0_, bf16[160,576]{1,0:T(8,128)(2,1)S(1)} %collective-permute-done.13.refs_1_, bf16[160,576]{1,0:T(8,128)(2,1)S(1)} %collective-permute-done.15.refs_2_, bf16[160,576]{1,0:T(8,128)(2,1)S(1)} %collective-permute-done.16.refs_3_, ...), custom_call_target="tpu_custom_call" | custom-call | tf_op jit(solution)/shard_map/pallas_call | solution.py:180
  (26 shorter events, 2.4 us)
Async XLA Ops:
  0.6 12.5 %collective-permute-start.4 = (bf16[4608,128]{1,0:T(8,128)(2,1)}, bf16[4608,128]{1,0:T(8,128)(2,1)S(1)}, u32[]{:S(2)}, u32[]{:S(2)}) collective-permute-start(bf16[4608,128]{1,0:T(8,128)(2,1)} %bitcast.17), channel_id=1, source_target_pairs={{0,1},{1,0},{2,3},{3,2},{4,5},{5,4},{6,7},{7,6},{8,9},{9,8},{10,11... | collective-permute-start | bytes 3538952 | tf_op jit(solution)/shard_map/ppermute | solution.py:52
  2.2 8.1 %collective-permute-start = (bf16[160,576]{1,0:T(8,128)(2,1)S(1)}, bf16[160,576]{1,0:T(8,128)(2,1)S(1)}, u32[]{:S(2)}, u32[]{:S(2)}) collective-permute-start(bf16[160,576]{1,0:T(8,128)(2,1)S(1)} %get-tuple-element.17), channel_id=1, source_target_pairs={{0,5},{1,4},{2,7},{3,6},{4,1},{5,0},{6,3},{7,2},{8,13},{9,12},{10,... | collective-permute-start | bytes 552968 | tf_op jit(solution)/shard_map/ppermute | solution.py:52
  4.9 7.9 %collective-permute-start.3 = (bf16[160,576]{1,0:T(8,128)(2,1)S(1)}, bf16[160,576]{1,0:T(8,128)(2,1)S(1)}, u32[]{:S(2)}, u32[]{:S(2)}) collective-permute-start(bf16[160,576]{1,0:T(8,128)(2,1)S(1)} %get-tuple-element.33.refs_0_), channel_id=1, source_target_pairs={{0,2},{1,3},{2,0},{3,1},{4,6},{5,7},{6,4},{7,5},{8,10},{9,11},{10,... | collective-permute-start | bytes 552968 | tf_op jit(solution)/shard_map/ppermute | solution.py:52
  6.4 8.8 %collective-permute-start.1 = (bf16[160,576]{1,0:T(8,128)(2,1)S(1)}, bf16[160,576]{1,0:T(8,128)(2,1)S(1)}, u32[]{:S(2)}, u32[]{:S(2)}) collective-permute-start(bf16[160,576]{1,0:T(8,128)(2,1)S(1)} %get-tuple-element.33.refs_0_), channel_id=1, source_target_pairs={{0,4},{1,5},{2,6},{3,7},{4,0},{5,1},{6,2},{7,3},{8,12},{9,13},{10,... | collective-permute-start | bytes 552968 | tf_op jit(solution)/shard_map/ppermute | solution.py:52
  6.9 9.3 %collective-permute-start.2 = (bf16[160,576]{1,0:T(8,128)(2,1)S(1)}, bf16[160,576]{1,0:T(8,128)(2,1)S(1)}, u32[]{:S(2)}, u32[]{:S(2)}) collective-permute-start(bf16[160,576]{1,0:T(8,128)(2,1)S(1)} %get-tuple-element.17), channel_id=1, source_target_pairs={{0,3},{1,2},{2,1},{3,0},{4,7},{5,6},{6,5},{7,4},{8,11},{9,10},{10,... | collective-permute-start | bytes 552968 | tf_op jit(solution)/shard_map/ppermute | solution.py:52
  10.3 10.4 %collective-permute-start.7 = (bf16[160,576]{1,0:T(8,128)(2,1)S(1)}, bf16[160,576]{1,0:T(8,128)(2,1)S(1)}, u32[]{:S(2)}, u32[]{:S(2)}) collective-permute-start(bf16[160,576]{1,0:T(8,128)(2,1)S(1)} %collective-permute-done.refs_1_), channel_id=1, source_target_pairs={{0,2},{1,3},{2,0},{3,1},{4,6},{5,7},{6,4},{7,5},{8,10},{9,11},{10,... | collective-permute-start | bytes 552968 | tf_op jit(solution)/shard_map/ppermute | solution.py:52
  12.8 7.9 %collective-permute-start.8 = (bf16[160,576]{1,0:T(8,128)(2,1)S(1)}, bf16[160,576]{1,0:T(8,128)(2,1)S(1)}, u32[]{:S(2)}, u32[]{:S(2)}) collective-permute-start(bf16[160,576]{1,0:T(8,128)(2,1)S(1)} %collective-permute-done.3.refs_4_), channel_id=1, source_target_pairs={{0,4},{1,5},{2,6},{3,7},{4,0},{5,1},{6,2},{7,3},{8,12},{9,13},{10,... | collective-permute-start | bytes 552968 | tf_op jit(solution)/shard_map/ppermute | solution.py:52
  13.1 3.3 %collective-permute-start.5 = (bf16[160,576]{1,0:T(8,128)(2,1)S(1)}, bf16[160,576]{1,0:T(8,128)(2,1)S(1)}, u32[]{:S(2)}, u32[]{:S(2)}) collective-permute-start(bf16[160,576]{1,0:T(8,128)(2,1)S(1)} %get-tuple-element.17), channel_id=1, source_target_pairs={{0,1},{1,0},{2,3},{3,2},{4,5},{5,4},{6,7},{7,6},{8,9},{9,8},{10,11... | collective-permute-start | bytes 552968 | tf_op jit(solution)/shard_map/ppermute | solution.py:52
  15.2 5.5 %copy-start = (bf16[1,3,128,4608]{3,2,1,0:T(8,128)(2,1)S(1)}, bf16[1,3,128,4608]{3,2,1,0:T(8,128)(2,1)}, u32[]{:S(2)}) copy-start(bf16[1,3,128,4608]{3,2,1,0:T(8,128)(2,1)} %param.9) | copy-start | bytes 10616836
  15.2 1.2 %collective-permute-start.6 = (f32[2,128]{1,0:T(2,128)S(1)}, f32[2,128]{1,0:T(2,128)S(1)}, u32[]{:S(2)}, u32[]{:S(2)}) collective-permute-start(f32[2,128]{1,0:T(2,128)S(1)} %pad_maximum_fusion.refs_8_), channel_id=1, source_target_pairs={{0,1},{1,0},{2,3},{3,2},{4,5},{5,4},{6,7},{7,6},{8,9},{9,8},{10,11... | collective-permute-start | bytes 3080 | tf_op jit(solution)/shard_map/ppermute | solution.py:52
  16.4 1.3 %copy-start.1 = (bf16[1,4608,128]{2,1,0:T(8,128)(2,1)S(1)}, bf16[1,4608,128]{2,1,0:T(8,128)(2,1)}, u32[]{:S(2)}) copy-start(bf16[1,4608,128]{2,1,0:T(8,128)(2,1)} %param.6) | copy-start | bytes 3538948
  20.7 9.6 %collective-permute-start.12 = (bf16[3,128,4608]{2,1,0:T(8,128)(2,1)S(1)}, bf16[3,128,4608]{2,1,0:T(8,128)(2,1)S(1)}, u32[]{:S(2)}, u32[]{:S(2)}) collective-permute-start(bf16[3,128,4608]{2,1,0:T(8,128)(2,1)S(1)} %bitcast.12), channel_id=1, source_target_pairs={{0,1},{1,0},{2,3},{3,2},{4,5},{5,4},{6,7},{7,6},{8,9},{9,8},{10,11... | collective-permute-start | bytes 10616840 | tf_op jit(solution)/shard_map/ppermute | solution.py:52
  21.0 9.3 %collective-permute-start.10 = (bf16[160,256]{1,0:T(8,128)(2,1)S(1)}, bf16[160,256]{1,0:T(8,128)(2,1)S(1)}, u32[]{:S(2)}, u32[]{:S(2)}) collective-permute-start(bf16[160,256]{1,0:T(8,128)(2,1)S(1)} %shard_map.69.refs_0_), channel_id=1, source_target_pairs={{0,16},{8,24},{16,0},{24,8},{1,17},{9,25},{17,1},{25,9},{2,18},{10... | collective-permute-start | bytes 245768 | tf_op jit(solution)/shard_map/ppermute | solution.py:26
  23.7 6.7 %collective-permute-start.9 = (bf16[160,256]{1,0:T(8,128)(2,1)S(1)}, bf16[160,256]{1,0:T(8,128)(2,1)S(1)}, u32[]{:S(2)}, u32[]{:S(2)}) collective-permute-start(bf16[160,256]{1,0:T(8,128)(2,1)S(1)} %shard_map.69.refs_0_), channel_id=1, source_target_pairs={{0,8},{8,16},{16,24},{24,0},{1,9},{9,17},{17,25},{25,1},{2,10},{10... | collective-permute-start | bytes 245768 | tf_op jit(solution)/shard_map/ppermute | solution.py:26
  25.3 1.7 %collective-permute-start.11 = (bf16[160,128]{1,0:T(8,128)(2,1)S(1)}, bf16[160,128]{1,0:T(8,128)(2,1)S(1)}, u32[]{:S(2)}, u32[]{:S(2)}) collective-permute-start(bf16[160,128]{1,0:T(8,128)(2,1)S(1)} %get-tuple-element.35), channel_id=1, source_target_pairs={{0,1},{1,0},{2,3},{3,2},{4,5},{5,4},{6,7},{7,6},{8,9},{9,8},{10,11... | collective-permute-start | bytes 122888 | tf_op jit(solution)/shard_map/ppermute | solution.py:52
  31.0 6.5 %collective-permute-start.17 = (bf16[160,576]{1,0:T(8,128)(2,1)S(1)}, bf16[160,576]{1,0:T(8,128)(2,1)S(1)}, u32[]{:S(2)}, u32[]{:S(2)}) collective-permute-start(bf16[160,576]{1,0:T(8,128)(2,1)S(1)} %get-tuple-element.30), channel_id=1, source_target_pairs={{0,4},{1,5},{2,6},{3,7},{4,0},{5,1},{6,2},{7,3},{8,12},{9,13},{10,... | collective-permute-start | bytes 552968 | tf_op jit(solution)/shard_map/ppermute | solution.py:52
  31.5 6.8 %collective-permute-start.14 = (bf16[160,576]{1,0:T(8,128)(2,1)S(1)}, bf16[160,576]{1,0:T(8,128)(2,1)S(1)}, u32[]{:S(2)}, u32[]{:S(2)}) collective-permute-start(bf16[160,576]{1,0:T(8,128)(2,1)S(1)} %get-tuple-element.27), channel_id=1, source_target_pairs={{0,2},{1,3},{2,0},{3,1},{4,6},{5,7},{6,4},{7,5},{8,10},{9,11},{10,... | collective-permute-start | bytes 552968 | tf_op jit(solution)/shard_map/ppermute | solution.py:52
  33.7 7.5 %collective-permute-start.19 = (bf16[160,576]{1,0:T(8,128)(2,1)S(1)}, bf16[160,576]{1,0:T(8,128)(2,1)S(1)}, u32[]{:S(2)}, u32[]{:S(2)}) collective-permute-start(bf16[160,576]{1,0:T(8,128)(2,1)S(1)} %get-tuple-element.31), channel_id=1, source_target_pairs={{0,5},{1,4},{2,7},{3,6},{4,1},{5,0},{6,3},{7,2},{8,13},{9,12},{10,... | collective-permute-start | bytes 552968 | tf_op jit(solution)/shard_map/ppermute | solution.py:52
  34.4 7.4 %collective-permute-start.13 = (bf16[160,576]{1,0:T(8,128)(2,1)S(1)}, bf16[160,576]{1,0:T(8,128)(2,1)S(1)}, u32[]{:S(2)}, u32[]{:S(2)}) collective-permute-start(bf16[160,576]{1,0:T(8,128)(2,1)S(1)} %get-tuple-element.25), channel_id=1, source_target_pairs={{0,2},{1,3},{2,0},{3,1},{4,6},{5,7},{6,4},{7,5},{8,10},{9,11},{10,... | collective-permute-start | bytes 552968 | tf_op jit(solution)/shard_map/ppermute | solution.py:52
  35.6 6.2 %collective-permute-start.16 = (bf16[160,576]{1,0:T(8,128)(2,1)S(1)}, bf16[160,576]{1,0:T(8,128)(2,1)S(1)}, u32[]{:S(2)}, u32[]{:S(2)}) collective-permute-start(bf16[160,576]{1,0:T(8,128)(2,1)S(1)} %get-tuple-element.28), channel_id=1, source_target_pairs={{0,1},{1,0},{2,3},{3,2},{4,5},{5,4},{6,7},{7,6},{8,9},{9,8},{10,11... | collective-permute-start | bytes 552968 | tf_op jit(solution)/shard_map/ppermute | solution.py:52
  37.5 9.3 %collective-permute-start.18 = (bf16[160,576]{1,0:T(8,128)(2,1)S(1)}, bf16[160,576]{1,0:T(8,128)(2,1)S(1)}, u32[]{:S(2)}, u32[]{:S(2)}) collective-permute-start(bf16[160,576]{1,0:T(8,128)(2,1)S(1)} %shard_map.75), channel_id=1, source_target_pairs={{0,3},{1,2},{2,1},{3,0},{4,7},{5,6},{6,5},{7,4},{8,11},{9,10},{10,... | collective-permute-start | bytes 552968 | tf_op jit(solution)/shard_map/ppermute | solution.py:52
  38.3 8.5 %collective-permute-start.15 = (bf16[160,576]{1,0:T(8,128)(2,1)S(1)}, bf16[160,576]{1,0:T(8,128)(2,1)S(1)}, u32[]{:S(2)}, u32[]{:S(2)}) collective-permute-start(bf16[160,576]{1,0:T(8,128)(2,1)S(1)} %shard_map.74), channel_id=1, source_target_pairs={{0,4},{1,5},{2,6},{3,7},{4,0},{5,1},{6,2},{7,3},{8,12},{9,13},{10,... | collective-permute-start | bytes 552968 | tf_op jit(solution)/shard_map/ppermute | solution.py:52
